TPU v7x, 1024 devices: a whole 8x8x8 slice. The times are simulated.
1024 devices in a mesh: gx: 64 (over x, z_hi, core), gy: 16 (over y, z_lo).
Axes of the slice: x: 8, y: 8, z: 8 (z_hi: 4, z_lo: 2; z = z_hi * 2 + z_lo), core: 2. Of those that a mesh axis runs over, the one named last changes fastest.
Arguments:
- inputs: bfloat16 [384, 8192], P(None, 'gx'), may hold values from -6 to 6
- grad_out: bfloat16 [384, 8192], P(None, 'gx'), may hold values from -2 to 2
- w_in: bfloat16 [8192, 32768], P('gx', 'gy'), may hold values from -0.0625 to 0.0625
- w_out: bfloat16 [32768, 8192], P('gy', 'gx'), may hold values from -0.03125 to 0.03125
Outputs:
- grad_inputs: bfloat16 [384, 8192], P('gy', 'gx')
- grad_w_in: float32 [8192, 32768], P('gx', 'gy')
- grad_w_out: float32 [32768, 8192], P('gy', 'gx')
All inputs are finite; a program needn't handle non-finite values.
Results may differ from a plain program's by a relative error of at most 0.0049.
Values may be sent and summed in bfloat16 or wider, within the bound.
No kernel may reach another device: no remote copies, remote signals or barrier semaphores. Data moves between devices by JAX's collectives and lax.ppermute only.
A program may use at most 64 MiB of HBM per device.

v0:
```python
import jax
import jax.numpy as jnp
from jax import lax
from jax.sharding import PartitionSpec as P


def gelu_tanh(values):
    return jax.nn.gelu(values, approximate=True)


def activate(hidden_pre, grad_act):
    activation, pullback = jax.vjp(gelu_tanh, hidden_pre)
    grad_pre = pullback(grad_act)[0]
    return (activation.astype(jnp.bfloat16), grad_pre.astype(jnp.bfloat16))


def per_device(inputs, grad_out, w_in, w_out):
    hidden_pre = lax.psum_scatter(
        jnp.dot(inputs, w_in, preferred_element_type=jnp.float32),
        "gx",
        scatter_dimension=0,
        tiled=True,
    )
    grad_act = lax.psum_scatter(
        lax.dot_general(
            grad_out, w_out, (((1,), (1,)), ((), ())), preferred_element_type=jnp.float32
        ),
        "gx",
        scatter_dimension=0,
        tiled=True,
    )
    activation, grad_pre = activate(hidden_pre, grad_act)
    act_all, grad_all = (
        lax.all_gather(activation, "gx", axis=0, tiled=True),
        lax.all_gather(grad_pre, "gx", axis=0, tiled=True),
    )
    grad_w_out = lax.dot_general(
        act_all, grad_out, (((0,), (0,)), ((), ())), preferred_element_type=jnp.float32
    )
    grad_w_in = lax.dot_general(
        inputs, grad_all, (((0,), (0,)), ((), ())), preferred_element_type=jnp.float32
    )
    partial_in = lax.dot_general(
        grad_all, w_in, (((1,), (1,)), ((), ())), preferred_element_type=jnp.float32
    )
    grad_inputs = lax.psum_scatter(partial_in, "gy", scatter_dimension=0, tiled=True).astype(
        jnp.bfloat16
    )
    return (grad_inputs, grad_w_in, grad_w_out)


def solution(mesh):
    return jax.shard_map(
        per_device,
        mesh=mesh,
        in_specs=(P(None, "gx"), P(None, "gx"), P("gx", "gy"), P("gy", "gx")),
        out_specs=(P("gy", "gx"), P("gx", "gy"), P("gy", "gx")),
        check_vma=False,
    )
```

profile of v0, /device:TPU:4, one launch (start us, length us, event | category | flops | bytes accessed | tf_op | source)
XLA Modules:
  0.0 580.2 jit_solution(2242751092905763733)
XLA Ops:
  7.2 3.4 fusion.12
  10.6 2.2 fusion.13
  12.8 165.2 %fusion.11 = (f32[8,2048]{1,0:T(8,128)S(1)}, f32[8,2048]{1,0:T(8,128)S(1)}) fusion(f32[384,2048]{1,0:T(8,128)} %fusion.13, f32[384,2048]{1,0:T(8,128)} %fusion.12), kind=kCustom, calls=%all-reduce-scatter.2 | all-reduce-scatter fusion | flops 2097153 | bytes 6426624
  178.0 24.9 %collective-permute-start.15 = (f32[6,2048]{1,0:T(8,128)S(1)}, f32[6,2048]{1,0:T(8,128)S(1)}, u32[]{:S(2)}, u32[]{:S(2)}) collective-permute-start(f32[6,2048]{1,0:T(8,128)S(1)} %slice), channel_id=1, source_target_pairs={{0,256},{16,272},{32,288},{48,304},{64,320},{80,336},{96,352},{112... | collective-permute-start | bytes 147464
  210.7 2.2 collective-permute-start.11
  212.9 7.0 %collective-permute-start.12 = (f32[8,2048]{1,0:T(8,128)S(1)}, f32[8,2048]{1,0:T(8,128)S(1)}, u32[]{:S(2)}, u32[]{:S(2)}) collective-permute-start(f32[8,2048]{1,0:T(8,128)S(1)} %get-tuple-element.15), channel_id=1, source_target_pairs={{0,208},{16,224},{32,240},{48,256},{64,272},{80,288},{96,304},{112... | collective-permute-start | bytes 196616
  223.8 2.2 collective-permute-start.2
  226.0 3.7 collective-permute-start.3
  229.8 4.0 collective-permute-start.4
  233.7 3.6 collective-permute-start.5
  237.4 2.1 collective-permute-start.6
  239.5 3.7 collective-permute-start.7
  249.0 4.6 collective-permute-start.17
  253.7 4.2 collective-permute-start.18
  257.8 2.5 collective-permute-start.19
  260.4 4.0 collective-permute-start.20
  264.5 3.4 collective-permute-start.21
  289.7 4.8 collective-permute-done.27
  295.5 11.3 %concatenate.1 = f32[134,2048]{1,0:T(8,128)S(1)} concatenate(f32[6,2048]{1,0:T(8,128)S(1)} %collective-permute-done.31, f32[8,2048]{1,0:T(8,128)} %collective-permute-done.30, f32[8,2048]{1,0:T(8,128)} %collective-permute-done.29, f32[8,2048]{1,0:T(8,128)} %collective-permute-done.28, f32[8,2048]{1,0:T(8,128)} %collective-permute-done.27, f32[8,2048]{1,0:T(8,128)} %collective-permute-done.26, ...), dimensions={0} | concatenate | bytes 2195456
  308.3 95.5 %all-gather.5.cloned.1.call-done = bf16[64,6,2048]{2,1,0:T(8,128)(2,1)} async-done(((bf16[1,6,2048]{2,1,0:T(8,128)(2,1)}), bf16[64,6,2048]{2,1,0:T(8,128)(2,1)}) %all-gather.5.cloned.1.call-update) | async-done | bytes 1572880 | tf_op jit(solution)/shard_map/all_gather | solution.py:35
  403.8 2.6 reshape.7
  409.6 87.8 %all-gather.7.cloned.1.call-done = bf16[64,6,2048]{2,1,0:T(8,128)(2,1)} async-done(((bf16[1,6,2048]{2,1,0:T(8,128)(2,1)}), bf16[64,6,2048]{2,1,0:T(8,128)(2,1)}) %all-gather.7.cloned.1.call-update) | async-done | bytes 1572880 | tf_op jit(solution)/shard_map/all_gather | solution.py:34
  497.4 2.6 reshape.9
  501.6 70.8 %reduce-scatter.9.cloned.1.call-done = f32[24,128]{1,0:T(8,128)} async-done(((f32[384,128]{1,0:T(8,128)}), f32[24,128]{1,0:T(8,128)}) %reduce-scatter.9.cloned.1.call-update) | async-done | bytes 12304
  (83 shorter events, 47.1 us)
Async XLA Ops:
  7.2 396.6 %all-gather.5.cloned.1.call-start = ((), (), s32[]{:S(2)}) async-start(), calls=%async_computation.1 | async-start | bytes 2129920 | tf_op jit(solution)/shard_map/all_gather | solution.py:35
  178.0 32.7 %collective-permute-start.15 = (f32[6,2048]{1,0:T(8,128)S(1)}, f32[6,2048]{1,0:T(8,128)S(1)}, u32[]{:S(2)}, u32[]{:S(2)}) collective-permute-start(f32[6,2048]{1,0:T(8,128)S(1)} %slice), channel_id=1, source_target_pairs={{0,256},{16,272},{32,288},{48,304},{64,320},{80,336},{96,352},{112... | collective-permute-start | bytes 147464
  204.9 15.0 %collective-permute-start = (f32[8,2048]{1,0:T(8,128)S(1)}, f32[8,2048]{1,0:T(8,128)S(1)}, u32[]{:S(2)}, u32[]{:S(2)}) collective-permute-start(f32[8,2048]{1,0:T(8,128)S(1)} %get-tuple-element.15), channel_id=1, source_target_pairs={{0,16},{16,32},{32,48},{48,64},{64,80},{80,96},{96,112},{112,128},... | collective-permute-start | bytes 196616
  206.8 15.0 %collective-permute-start.1 = (f32[8,2048]{1,0:T(8,128)S(1)}, f32[8,2048]{1,0:T(8,128)S(1)}, u32[]{:S(2)}, u32[]{:S(2)}) collective-permute-start(f32[8,2048]{1,0:T(8,128)S(1)} %get-tuple-element.15), channel_id=1, source_target_pairs={{0,32},{16,48},{32,64},{48,80},{64,96},{80,112},{96,128},{112,144}... | collective-permute-start | bytes 196616
  208.8 15.0 %collective-permute-start.10 = (f32[8,2048]{1,0:T(8,128)S(1)}, f32[8,2048]{1,0:T(8,128)S(1)}, u32[]{:S(2)}, u32[]{:S(2)}) collective-permute-start(f32[8,2048]{1,0:T(8,128)S(1)} %get-tuple-element.15), channel_id=1, source_target_pairs={{0,176},{16,192},{32,208},{48,224},{64,240},{80,256},{96,272},{112... | collective-permute-start | bytes 196616
  210.7 15.3 %collective-permute-start.11 = (f32[8,2048]{1,0:T(8,128)S(1)}, f32[8,2048]{1,0:T(8,128)S(1)}, u32[]{:S(2)}, u32[]{:S(2)}) collective-permute-start(f32[8,2048]{1,0:T(8,128)S(1)} %get-tuple-element.15), channel_id=1, source_target_pairs={{0,192},{16,208},{32,224},{48,240},{64,256},{80,272},{96,288},{112... | collective-permute-start | bytes 196616
  212.9 16.8 %collective-permute-start.12 = (f32[8,2048]{1,0:T(8,128)S(1)}, f32[8,2048]{1,0:T(8,128)S(1)}, u32[]{:S(2)}, u32[]{:S(2)}) collective-permute-start(f32[8,2048]{1,0:T(8,128)S(1)} %get-tuple-element.15), channel_id=1, source_target_pairs={{0,208},{16,224},{32,240},{48,256},{64,272},{80,288},{96,304},{112... | collective-permute-start | bytes 196616
  221.9 15.5 %collective-permute-start.14 = (f32[8,2048]{1,0:T(8,128)S(1)}, f32[8,2048]{1,0:T(8,128)S(1)}, u32[]{:S(2)}, u32[]{:S(2)}) collective-permute-start(f32[8,2048]{1,0:T(8,128)S(1)} %get-tuple-element.15), channel_id=1, source_target_pairs={{0,240},{16,256},{32,272},{48,288},{64,304},{80,320},{96,336},{112... | collective-permute-start | bytes 196616
  223.8 15.6 %collective-permute-start.2 = (f32[8,2048]{1,0:T(8,128)S(1)}, f32[8,2048]{1,0:T(8,128)S(1)}, u32[]{:S(2)}, u32[]{:S(2)}) collective-permute-start(f32[8,2048]{1,0:T(8,128)S(1)} %get-tuple-element.15), channel_id=1, source_target_pairs={{0,48},{16,64},{32,80},{48,96},{64,112},{80,128},{96,144},{112,160... | collective-permute-start | bytes 196616
  226.0 17.1 %collective-permute-start.3 = (f32[8,2048]{1,0:T(8,128)S(1)}, f32[8,2048]{1,0:T(8,128)S(1)}, u32[]{:S(2)}, u32[]{:S(2)}) collective-permute-start(f32[8,2048]{1,0:T(8,128)S(1)} %get-tuple-element.15), channel_id=1, source_target_pairs={{0,64},{16,80},{32,96},{48,112},{64,128},{80,144},{96,160},{112,17... | collective-permute-start | bytes 196616
  229.8 15.3 %collective-permute-start.4 = (f32[8,2048]{1,0:T(8,128)S(1)}, f32[8,2048]{1,0:T(8,128)S(1)}, u32[]{:S(2)}, u32[]{:S(2)}) collective-permute-start(f32[8,2048]{1,0:T(8,128)S(1)} %get-tuple-element.15), channel_id=1, source_target_pairs={{0,80},{16,96},{32,112},{48,128},{64,144},{80,160},{96,176},{112,1... | collective-permute-start | bytes 196616
  239.5 14.2 %collective-permute-start.7 = (f32[8,2048]{1,0:T(8,128)S(1)}, f32[8,2048]{1,0:T(8,128)S(1)}, u32[]{:S(2)}, u32[]{:S(2)}) collective-permute-start(f32[8,2048]{1,0:T(8,128)S(1)} %get-tuple-element.15), channel_id=1, source_target_pairs={{0,128},{16,144},{32,160},{48,176},{64,192},{80,208},{96,224},{112... | collective-permute-start | bytes 196616
  243.1 14.7 %collective-permute-start.8 = (f32[8,2048]{1,0:T(8,128)S(1)}, f32[8,2048]{1,0:T(8,128)S(1)}, u32[]{:S(2)}, u32[]{:S(2)}) collective-permute-start(f32[8,2048]{1,0:T(8,128)S(1)} %get-tuple-element.15), channel_id=1, source_target_pairs={{0,144},{16,160},{32,176},{48,192},{64,208},{80,224},{96,240},{112... | collective-permute-start | bytes 196616
  245.1 15.3 %collective-permute-start.9 = (f32[8,2048]{1,0:T(8,128)S(1)}, f32[8,2048]{1,0:T(8,128)S(1)}, u32[]{:S(2)}, u32[]{:S(2)}) collective-permute-start(f32[8,2048]{1,0:T(8,128)S(1)} %get-tuple-element.15), channel_id=1, source_target_pairs={{0,160},{16,176},{32,192},{48,208},{64,224},{80,240},{96,256},{112... | collective-permute-start | bytes 196616
  247.0 17.4 %collective-permute-start.16 = (f32[8,2048]{1,0:T(8,128)S(1)}, f32[8,2048]{1,0:T(8,128)S(1)}, u32[]{:S(2)}, u32[]{:S(2)}) collective-permute-start(f32[8,2048]{1,0:T(8,128)S(1)} %get-tuple-element.14), channel_id=1, source_target_pairs={{0,16},{16,32},{32,48},{48,64},{64,80},{80,96},{96,112},{112,128},... | collective-permute-start | bytes 196616
  249.0 18.8 %collective-permute-start.17 = (f32[8,2048]{1,0:T(8,128)S(1)}, f32[8,2048]{1,0:T(8,128)S(1)}, u32[]{:S(2)}, u32[]{:S(2)}) collective-permute-start(f32[8,2048]{1,0:T(8,128)S(1)} %get-tuple-element.14), channel_id=1, source_target_pairs={{0,32},{16,48},{32,64},{48,80},{64,96},{80,112},{96,128},{112,144}... | collective-permute-start | bytes 196616
  253.7 16.1 %collective-permute-start.18 = (f32[8,2048]{1,0:T(8,128)S(1)}, f32[8,2048]{1,0:T(8,128)S(1)}, u32[]{:S(2)}, u32[]{:S(2)}) collective-permute-start(f32[8,2048]{1,0:T(8,128)S(1)} %get-tuple-element.14), channel_id=1, source_target_pairs={{0,48},{16,64},{32,80},{48,96},{64,112},{80,128},{96,144},{112,160... | collective-permute-start | bytes 196616
  257.8 13.9 %collective-permute-start.19 = (f32[8,2048]{1,0:T(8,128)S(1)}, f32[8,2048]{1,0:T(8,128)S(1)}, u32[]{:S(2)}, u32[]{:S(2)}) collective-permute-start(f32[8,2048]{1,0:T(8,128)S(1)} %get-tuple-element.14), channel_id=1, source_target_pairs={{0,64},{16,80},{32,96},{48,112},{64,128},{80,144},{96,160},{112,17... | collective-permute-start | bytes 196616
  275.6 14.1 %collective-permute-start.26 = (f32[8,2048]{1,0:T(8,128)S(1)}, f32[8,2048]{1,0:T(8,128)}, u32[]{:S(2)}, u32[]{:S(2)}) collective-permute-start(f32[8,2048]{1,0:T(8,128)S(1)} %get-tuple-element.14), channel_id=1, source_target_pairs={{0,176},{16,192},{32,208},{48,224},{64,240},{80,256},{96,272},{112... | collective-permute-start | bytes 196616
  277.6 16.9 %collective-permute-start.27 = (f32[8,2048]{1,0:T(8,128)S(1)}, f32[8,2048]{1,0:T(8,128)}, u32[]{:S(2)}, u32[]{:S(2)}) collective-permute-start(f32[8,2048]{1,0:T(8,128)S(1)} %get-tuple-element.14), channel_id=1, source_target_pairs={{0,192},{16,208},{32,224},{48,240},{64,256},{80,272},{96,288},{112... | collective-permute-start | bytes 196616
  279.5 15.0 %collective-permute-start.28 = (f32[8,2048]{1,0:T(8,128)S(1)}, f32[8,2048]{1,0:T(8,128)}, u32[]{:S(2)}, u32[]{:S(2)}) collective-permute-start(f32[8,2048]{1,0:T(8,128)S(1)} %get-tuple-element.14), channel_id=1, source_target_pairs={{0,208},{16,224},{32,240},{48,256},{64,272},{80,288},{96,304},{112... | collective-permute-start | bytes 196616
  281.5 14.0 %collective-permute-start.29 = (f32[8,2048]{1,0:T(8,128)S(1)}, f32[8,2048]{1,0:T(8,128)}, u32[]{:S(2)}, u32[]{:S(2)}) collective-permute-start(f32[8,2048]{1,0:T(8,128)S(1)} %get-tuple-element.14), channel_id=1, source_target_pairs={{0,224},{16,240},{32,256},{48,272},{64,288},{80,304},{96,320},{112... | collective-permute-start | bytes 196616
  307.5 189.9 %all-gather.7.cloned.1.call-start = ((), (), s32[]{:S(2)}) async-start(), calls=%async_computation.2 | async-start | bytes 2129920 | tf_op jit(solution)/shard_map/all_gather | solution.py:34
  308.3 264.1 %reduce-scatter.9.cloned.1.call-start = ((), (), s32[]{:S(2)}) async-start(), calls=%async_computation.3 | async-start | bytes 208896
  (20 other events, 301.0 us)
Sparse Core Ops, SparseCore 0:
  307.7 96.1 all-gather.4
  408.9 88.5 all-gather.6
  500.8 71.5 reduce-scatter.8
where the time goes:
time: 582 us; the launch traced here: 580 us
  waiting for transfers between devices  261 us (45%)
  blocking collectives  165 us (28%)
  starting transfers between devices  107 us (18%)
  local copies, waits for them, and re-layouts  21.2 us (4%)
  between operations  15 us (3%)
  matrix products  9.06 us (2%)
    unnamed x1, blocking collectives  165 us
    unnamed x33, starting transfers between devices  107 us
    all_gather x1, waiting for transfers between devices, per_device(): lax.all_gather(grad_pre, 'gx', axis=0, tiled=True)  95.5 us
    all_gather x1, waiting for transfers between devices, per_device(): lax.all_gather(activation, 'gx', axis=0, tiled=True)  87.8 us
    unnamed x36, waiting for transfers between devices  77.7 us
    unnamed x26, local copies, waits for them, and re-layouts  21.2 us
  transfers between devices with their start and end apart: 35, of which 6 were waited for; matrix products, arithmetic and copies ran while one was open for 2% of the time, Pallas kernels for 0%

commit v1 on v0

v1 whole, which is shorter than its diff:
```python
import functools

import jax
import jax.numpy as jnp
import numpy as np
from jax import lax
from jax.experimental import pallas as pl
from jax.experimental.pallas import tpu as pltpu
from jax.sharding import Mesh, PartitionSpec as P

F32, BF16 = jnp.float32, jnp.bfloat16
PARAMS = pltpu.CompilerParams(vmem_limit_bytes=40 * 1024 * 1024)
OTHER = ((0, 1), (1, 0))
T, B = 384, 128
N = 8


def call(body, outs, *operands):
    vmem = pl.BlockSpec(memory_space=pltpu.VMEM)
    return pl.pallas_call(
        body,
        out_shape=outs,
        in_specs=[vmem] * len(operands),
        out_specs=jax.tree.map(lambda _: vmem, outs),
        compiler_params=PARAMS,
    )(*operands)


def columns(core, j):
    return pl.ds(pl.multiple_of(core * (N * B) + j * B, B), B)


def dot(a, b, dims):
    return lax.dot_general(a, b, (dims, ((), ())), preferred_element_type=F32)


def pack_in(x, w, out):
    other = 1 - lax.axis_index("c")
    out[:T] = x[...]
    for j in range(N):
        out[T + j * B : T + (j + 1) * B] = w[:, columns(other, j)]


def pack_out(x, w, out):
    other = 1 - lax.axis_index("c")
    out[:T] = x[...]
    for j in range(N):
        out[T + j * B : T + (j + 1) * B] = w[columns(other, j), :]


def hidden_part(x, w, theirs, out):
    core = lax.axis_index("c")
    for j in range(N):
        out[j] = (
            dot(x[...], w[:, columns(core, j)], ((1,), (0,)))
            + dot(theirs[:T], theirs[T + j * B : T + (j + 1) * B], ((1,), (0,)))
        ).astype(BF16)


def grad_part(x, w, theirs, out):
    core = lax.axis_index("c")
    for j in range(N):
        out[j] = (
            dot(x[...], w[columns(core, j), :], ((1,), (1,)))
            + dot(theirs[:T], theirs[T + j * B : T + (j + 1) * B], ((1,), (1,)))
        ).astype(BF16)


def add_blocks(parts, out):
    total = parts[0].astype(F32)
    for j in range(1, parts.shape[0]):
        total = total + parts[j].astype(F32)
    out[...] = total


def activate(parts, act, slope):
    v = parts[0]
    for j in range(1, parts.shape[0]):
        v = v + parts[j]
    k = np.float32(np.sqrt(2 / np.pi))
    cube = np.float32(0.044715)
    t = jnp.tanh(k * (v + cube * (v * v * v)))
    a = (0.5 * v * (1.0 + t)).astype(BF16)
    slope[...] = 0.5 * (1.0 + t) + 0.5 * v * (1.0 - t * t) * (
        k * (1.0 + 3.0 * cube * (v * v))
    )
    for j in range(N):
        act[j] = a


def back(parts, slope, out):
    g = parts[0]
    for j in range(1, parts.shape[0]):
        g = g + parts[j]
    p = (g * slope[...]).astype(BF16)
    for j in range(N):
        out[j] = p


def weight_out(mine, theirs, x, out):
    core = lax.axis_index("c")
    for j in range(N):
        out[columns(core, j), :] = dot(mine[j], x[...], ((0,), (0,)))
        out[columns(1 - core, j), :] = dot(theirs[j], x[...], ((0,), (0,)))


def weight_in(mine, theirs, x, out):
    core = lax.axis_index("c")
    for j in range(N):
        out[:, columns(core, j)] = dot(x[...], mine[j], ((0,), (0,)))
        out[:, columns(1 - core, j)] = dot(x[...], theirs[j], ((0,), (0,)))


def input_part(mine, theirs, w, out):
    core = lax.axis_index("c")
    total = jnp.zeros((T, B), F32)
    for j in range(N):
        total += dot(mine[j], w[:, columns(core, j)], ((1,), (1,)))
        total += dot(theirs[j], w[:, columns(1 - core, j)], ((1,), (1,)))
    out[...] = total


def finish(parts, out):
    total = parts[0]
    for j in range(1, parts.shape[0]):
        total = total + parts[j]
    out[...] = total.astype(BF16)


def per_device(inputs, grad_out, w_in, w_out):
    s = jax.ShapeDtypeStruct
    blocks = s((N, T, B), BF16)
    swap = lambda v: lax.ppermute(v, "c", OTHER)
    over_x = lambda v: lax.all_to_all(v, "x", 0, 0, tiled=True)
    over_z = lambda v: lax.all_gather(v, "zh", axis=0, tiled=False)

    theirs_in = swap(call(pack_in, s((T + N * B, B), BF16), inputs, w_in))
    theirs_out = swap(call(pack_out, s((T + N * B, B), BF16), grad_out, w_out))
    hidden = over_x(call(hidden_part, blocks, inputs, w_in, theirs_in))
    grad = over_x(call(grad_part, blocks, grad_out, w_out, theirs_out))
    hidden = over_z(call(add_blocks, s((T, B), F32), hidden))
    act, slope = call(activate, (blocks, s((T, B), F32)), hidden)
    act = over_x(act)
    grad = over_z(call(add_blocks, s((T, B), F32), grad))
    pre = over_x(call(back, blocks, grad, slope))
    act_theirs = swap(act)
    grad_w_out = call(weight_out, s((2 * N * B, B), F32), act, act_theirs, grad_out)
    pre_theirs = swap(pre)
    part = call(input_part, s((T, B), F32), pre, pre_theirs, w_in)
    part = lax.all_to_all(
        part.reshape(16, T // 16, B), ("y", "zl"), 0, 0, tiled=True
    )
    grad_w_in = call(weight_in, s((B, 2 * N * B), F32), pre, pre_theirs, inputs)
    grad_inputs = call(finish, s((T // 16, B), BF16), part)
    return (grad_inputs, grad_w_in, grad_w_out)


def solution(mesh):
    fine = Mesh(mesh.devices.reshape(8, 4, 2, 8, 2), ("x", "zh", "c", "y", "zl"))
    gx, gy = ("x", "zh", "c"), ("y", "zl")
    return jax.shard_map(
        per_device,
        mesh=fine,
        in_specs=(P(None, gx), P(None, gx), P(gx, gy), P(gy, gx)),
        out_specs=(P(gy, gx), P(gx, gy), P(gy, gx)),
        check_vma=False,
    )
```

time: 582 us -> 169 us (0.29)
  the two profiles are of different devices: /device:TPU:4 before, /device:TPU:1 now
where the time goes in v1:
time: 169 us; the launch traced here: 168 us
  blocking collectives  57.8 us (34%)
  starting transfers between devices  57.3 us (34%)
  waiting for transfers between devices  40 us (24%)
  Pallas kernels  10.5 us (6%)
  local copies, waits for them, and re-layouts  1.94 us (1%)
    all_gather x2, blocking collectives, per_device(): over_z = lambda v: lax.all_gather(v, 'zh', axis=0, tiled=False)  37.6 us
    ppermute x4, starting transfers between devices, per_device(): swap = lambda v: lax.ppermute(v, 'c', OTHER)  34.8 us
    all_to_all x3, waiting for transfers between devices, per_device(): over_x = lambda v: lax.all_to_all(v, 'x', 0, 0, tiled=True)  31.6 us
    all_to_all x1, blocking collectives, per_device(): over_x = lambda v: lax.all_to_all(v, 'x', 0, 0, tiled=True)  20.2 us
    all_to_all x1, starting transfers between devices, per_device(): lax.all_to_all(part.reshape(16, T // 16, B), ('y', 'zl'), 0, 0, tiled=True)  11.5 us
    all_to_all x3, starting transfers between devices, per_device(): over_x = lambda v: lax.all_to_all(v, 'x', 0, 0, tiled=True)  11 us
    pallas_call x12, Pallas kernels, call(): pl.pallas_call(body, out_shape=outs, in_specs=[vmem] * len(operands), out...  10.5 us
    all_to_all x1, waiting for transfers between devices, per_device(): lax.all_to_all(part.reshape(16, T // 16, B), ('y', 'zl'), 0, 0, tiled=True)  5.83 us
  transfers between devices with their start and end apart: 8, of which 6 were waited for; matrix products, arithmetic and copies ran while one was open for 0% of the time, Pallas kernels for 5%

profile of v1, /device:TPU:1, one launch (start us, length us, event | category | flops | bytes accessed | tf_op | source)
XLA Modules:
  0.0 168.3 jit_solution(509582758624334050)
XLA Ops:
  0.6 1.0 copy-done
  2.6 16.1 %collective-permute-start.1 = (bf16[1408,128]{1,0:T(8,128)(2,1)S(1)}, bf16[1408,128]{1,0:T(8,128)(2,1)S(1)}, u32[]{:S(2)}, u32[]{:S(2)}) collective-permute-start(bf16[1408,128]{1,0:T(8,128)(2,1)S(1)} %shard_map.70), channel_id=1, source_target_pairs={{0,16},{16,0},{1,17},{17,1},{2,18},{18,2},{3,19},{19,3},{4,20},{20... | collective-permute-start | bytes 1081352 | tf_op jit(solution)/shard_map/ppermute | solution.py:133
  18.7 1.3 collective-permute-done.1.theirs
  20.0 1.4 shard_map.71
  21.4 3.7 %all-to-all-start.1 = ((bf16[8,384,128]{2,1,0:T(8,128)(2,1)}), bf16[8,384,128]{2,1,0:T(8,128)(2,1)S(1)}, u32[]{:S(2)}, u32[]{:S(2)}) async-start(bf16[8,384,128]{2,1,0:T(8,128)(2,1)} %shard_map.71), calls=%async_computation.1 | async-start | bytes 1572864 | tf_op jit(solution)/shard_map/all_to_all | solution.py:134
  25.2 2.3 %collective-permute-start = (bf16[1408,128]{1,0:T(8,128)(2,1)S(1)}, bf16[1408,128]{1,0:T(8,128)(2,1)S(1)}, u32[]{:S(2)}, u32[]{:S(2)}) collective-permute-start(bf16[1408,128]{1,0:T(8,128)(2,1)S(1)} %shard_map.67), channel_id=1, source_target_pairs={{0,16},{16,0},{1,17},{17,1},{2,18},{18,2},{3,19},{19,3},{4,20},{20... | collective-permute-start | bytes 1081352 | tf_op jit(solution)/shard_map/ppermute | solution.py:133
  27.5 1.3 collective-permute-done.theirs
  28.8 1.5 shard_map.68
  30.2 18.5 %all-to-all-done.1.parts = bf16[8,384,128]{2,1,0:T(8,128)(2,1)S(1)} async-done(((bf16[8,384,128]{2,1,0:T(8,128)(2,1)}), bf16[8,384,128]{2,1,0:T(8,128)(2,1)S(1)}, u32[]{:S(2)}, u32[]{:S(2)}) %all-to-all-start.1) | async-done | bytes 786464 | tf_op jit(solution)/shard_map/all_to_all | solution.py:134
  48.7 3.5 %all-to-all-start = ((bf16[8,384,128]{2,1,0:T(8,128)(2,1)}), bf16[8,384,128]{2,1,0:T(8,128)(2,1)S(1)}, u32[]{:S(2)}, u32[]{:S(2)}) async-start(bf16[8,384,128]{2,1,0:T(8,128)(2,1)} %shard_map.68), calls=%async_computation | async-start | bytes 1572864 | tf_op jit(solution)/shard_map/all_to_all | solution.py:134
  52.3 18.8 %all-gather.1 = f32[1536,128]{1,0:T(8,128)S(1)} all-gather(f32[384,128]{1,0:T(8,128)S(1)} %shard_map.72), channel_id=3, replica_groups=mesh['x'=8,'zh'=4,'c'=2,'y'=8,'zl'=2] {'zh'}, dimensions={0}, use_global_device_ids=true | all-gather | bytes 983040 | tf_op jit(solution)/shard_map/all_gather | solution.py:135
  71.1 1.0 shard_map.73
  72.1 3.6 %all-to-all-done.parts = bf16[8,384,128]{2,1,0:T(8,128)(2,1)S(1)} async-done(((bf16[8,384,128]{2,1,0:T(8,128)(2,1)}), bf16[8,384,128]{2,1,0:T(8,128)(2,1)S(1)}, u32[]{:S(2)}, u32[]{:S(2)}) %all-to-all-start) | async-done | bytes 786464 | tf_op jit(solution)/shard_map/all_to_all | solution.py:134
  75.9 18.8 %all-gather = f32[1536,128]{1,0:T(8,128)S(1)} all-gather(f32[384,128]{1,0:T(8,128)S(1)} %shard_map.69), channel_id=2, replica_groups=mesh['x'=8,'zh'=4,'c'=2,'y'=8,'zl'=2] {'zh'}, dimensions={0}, use_global_device_ids=true | all-gather | bytes 983040 | tf_op jit(solution)/shard_map/all_gather | solution.py:135
  94.8 20.2 %all_to_all.25.mine = bf16[8,384,128]{2,1,0:T(8,128)(2,1)S(1)} all-to-all(bf16[8,384,128]{2,1,0:T(8,128)(2,1)S(1)} %shard_map.74), channel_id=1, replica_groups=mesh['x'=8,'zh'=4,'c'=2,'y'=8,'zl'=2] {'x'}, dimensions={0} | all-to-all | bytes 1572864 | tf_op jit(solution)/shard_map/all_to_all | solution.py:134
  115.0 3.8 %all-to-all-start.4 = ((bf16[8,384,128]{2,1,0:T(8,128)(2,1)}), bf16[8,384,128]{2,1,0:T(8,128)(2,1)S(1)}, u32[]{:S(2)}, u32[]{:S(2)}) async-start(bf16[8,384,128]{2,1,0:T(8,128)(2,1)} %get-tuple-element.6), calls=%async_computation.4 | async-start | bytes 1572864 | tf_op jit(solution)/shard_map/all_to_all | solution.py:134
  118.7 8.1 %collective-permute-start.2 = (bf16[8,384,128]{2,1,0:T(8,128)(2,1)S(1)}, bf16[8,384,128]{2,1,0:T(8,128)(2,1)S(1)}, u32[]{:S(2)}, u32[]{:S(2)}) collective-permute-start(bf16[8,384,128]{2,1,0:T(8,128)(2,1)S(1)} %all_to_all.25.mine), channel_id=1, source_target_pairs={{0,16},{16,0},{1,17},{17,1},{2,18},{18,2},{3,19},{19,3},{4,20},{20... | collective-permute-start | bytes 2359304 | tf_op jit(solution)/shard_map/ppermute | solution.py:133
  126.8 9.5 %all-to-all-done.4.mine = bf16[8,384,128]{2,1,0:T(8,128)(2,1)S(1)} async-done(((bf16[8,384,128]{2,1,0:T(8,128)(2,1)}), bf16[8,384,128]{2,1,0:T(8,128)(2,1)S(1)}, u32[]{:S(2)}, u32[]{:S(2)}) %all-to-all-start.4) | async-done | bytes 786464 | tf_op jit(solution)/shard_map/all_to_all | solution.py:134
  136.3 8.4 %collective-permute-start.3 = (bf16[8,384,128]{2,1,0:T(8,128)(2,1)S(1)}, bf16[8,384,128]{2,1,0:T(8,128)(2,1)}, u32[]{:S(2)}, u32[]{:S(2)}) collective-permute-start(bf16[8,384,128]{2,1,0:T(8,128)(2,1)S(1)} %all-to-all-done.4.mine), channel_id=1, source_target_pairs={{0,16},{16,0},{1,17},{17,1},{2,18},{18,2},{3,19},{19,3},{4,20},{20... | collective-permute-start | bytes 2359304 | tf_op jit(solution)/shard_map/ppermute | solution.py:133
  144.8 1.3 shard_map.75
  146.1 11.5 %all-to-all-start.3 = ((f32[16,24,128]{2,1,0:T(8,128)}), f32[16,24,128]{2,1,0:T(8,128)S(1)}, u32[]{:S(2)}, u32[]{:S(2)}) async-start(f32[16,24,128]{2,1,0:T(8,128)} %bitcast.2), calls=%async_computation.3 | async-start | bytes 393216 | tf_op jit(solution)/shard_map/all_to_all | solution.py:150
  157.5 1.6 shard_map.77
  159.1 2.7 %shard_map.78 = f32[2048,128]{1,0:T(8,128)} custom-call(bf16[8,384,128]{2,1,0:T(8,128)(2,1)S(1)} %all-to-all-done.4.mine, bf16[8,384,128]{2,1,0:T(8,128)(2,1)} %collective-permute-done.3.theirs, bf16[384,128]{1,0:T(8,128)(2,1)S(1)} %copy-done.5), custom_call_target="tpu_custom_call" | custom-call | tf_op jit(solution)/shard_map/pallas_call | solution.py:20
  161.8 5.8 %all-to-all-done.3.parts = f32[16,24,128]{2,1,0:T(8,128)S(1)} async-done(((f32[16,24,128]{2,1,0:T(8,128)}), f32[16,24,128]{2,1,0:T(8,128)S(1)}, u32[]{:S(2)}, u32[]{:S(2)}) %all-to-all-start.3) | async-done | bytes 196640 | tf_op jit(solution)/shard_map/all_to_all | solution.py:150
  (19 shorter events, 1.9 us)
Async XLA Ops:
  0.6 1.0 copy-start
  1.7 0.9 copy-start.3
  2.6 17.4 %collective-permute-start.1 = (bf16[1408,128]{1,0:T(8,128)(2,1)S(1)}, bf16[1408,128]{1,0:T(8,128)(2,1)S(1)}, u32[]{:S(2)}, u32[]{:S(2)}) collective-permute-start(bf16[1408,128]{1,0:T(8,128)(2,1)S(1)} %shard_map.70), channel_id=1, source_target_pairs={{0,16},{16,0},{1,17},{17,1},{2,18},{18,2},{3,19},{19,3},{4,20},{20... | collective-permute-start | bytes 1081352 | tf_op jit(solution)/shard_map/ppermute | solution.py:133
  21.4 3.7 %copy-start.2 = (bf16[2048,128]{1,0:T(8,128)(2,1)S(1)}, bf16[2048,128]{1,0:T(8,128)(2,1)}, u32[]{:S(2)}) copy-start(bf16[2048,128]{1,0:T(8,128)(2,1)} %w.6) | copy-start | bytes 1572868
  21.4 3.7 %copy-start.5 = (bf16[384,128]{1,0:T(8,128)(2,1)S(1)}, bf16[384,128]{1,0:T(8,128)(2,1)}, u32[]{:S(2)}) copy-start(bf16[384,128]{1,0:T(8,128)(2,1)} %x.11) | copy-start | bytes 294916
  21.4 27.2 %all-to-all-start.1 = ((bf16[8,384,128]{2,1,0:T(8,128)(2,1)}), bf16[8,384,128]{2,1,0:T(8,128)(2,1)S(1)}, u32[]{:S(2)}, u32[]{:S(2)}) async-start(bf16[8,384,128]{2,1,0:T(8,128)(2,1)} %shard_map.71), calls=%async_computation.1 | async-start | bytes 1572864 | tf_op jit(solution)/shard_map/all_to_all | solution.py:134
  25.2 3.6 %collective-permute-start = (bf16[1408,128]{1,0:T(8,128)(2,1)S(1)}, bf16[1408,128]{1,0:T(8,128)(2,1)S(1)}, u32[]{:S(2)}, u32[]{:S(2)}) collective-permute-start(bf16[1408,128]{1,0:T(8,128)(2,1)S(1)} %shard_map.67), channel_id=1, source_target_pairs={{0,16},{16,0},{1,17},{17,1},{2,18},{18,2},{3,19},{19,3},{4,20},{20... | collective-permute-start | bytes 1081352 | tf_op jit(solution)/shard_map/ppermute | solution.py:133
  48.7 27.1 %all-to-all-start = ((bf16[8,384,128]{2,1,0:T(8,128)(2,1)}), bf16[8,384,128]{2,1,0:T(8,128)(2,1)S(1)}, u32[]{:S(2)}, u32[]{:S(2)}) async-start(bf16[8,384,128]{2,1,0:T(8,128)(2,1)} %shard_map.68), calls=%async_computation | async-start | bytes 1572864 | tf_op jit(solution)/shard_map/all_to_all | solution.py:134
  115.0 29.8 %copy-start.1 = (bf16[128,2048]{1,0:T(8,128)(2,1)S(1)}, bf16[128,2048]{1,0:T(8,128)(2,1)}, u32[]{:S(2)}) copy-start(bf16[128,2048]{1,0:T(8,128)(2,1)} %w.9) | copy-start | bytes 1572868
  115.0 21.4 %all-to-all-start.4 = ((bf16[8,384,128]{2,1,0:T(8,128)(2,1)}), bf16[8,384,128]{2,1,0:T(8,128)(2,1)S(1)}, u32[]{:S(2)}, u32[]{:S(2)}) async-start(bf16[8,384,128]{2,1,0:T(8,128)(2,1)} %get-tuple-element.6), calls=%async_computation.4 | async-start | bytes 1572864 | tf_op jit(solution)/shard_map/all_to_all | solution.py:134
  118.7 26.0 %collective-permute-start.2 = (bf16[8,384,128]{2,1,0:T(8,128)(2,1)S(1)}, bf16[8,384,128]{2,1,0:T(8,128)(2,1)S(1)}, u32[]{:S(2)}, u32[]{:S(2)}) collective-permute-start(bf16[8,384,128]{2,1,0:T(8,128)(2,1)S(1)} %all_to_all.25.mine), channel_id=1, source_target_pairs={{0,16},{16,0},{1,17},{17,1},{2,18},{18,2},{3,19},{19,3},{4,20},{20... | collective-permute-start | bytes 2359304 | tf_op jit(solution)/shard_map/ppermute | solution.py:133
  136.3 22.8 %collective-permute-start.3 = (bf16[8,384,128]{2,1,0:T(8,128)(2,1)S(1)}, bf16[8,384,128]{2,1,0:T(8,128)(2,1)}, u32[]{:S(2)}, u32[]{:S(2)}) collective-permute-start(bf16[8,384,128]{2,1,0:T(8,128)(2,1)S(1)} %all-to-all-done.4.mine), channel_id=1, source_target_pairs={{0,16},{16,0},{1,17},{17,1},{2,18},{18,2},{3,19},{19,3},{4,20},{20... | collective-permute-start | bytes 2359304 | tf_op jit(solution)/shard_map/ppermute | solution.py:133
  146.1 11.5 %copy-start.4 = (bf16[384,128]{1,0:T(8,128)(2,1)S(1)}, bf16[384,128]{1,0:T(8,128)(2,1)}, u32[]{:S(2)}) copy-start(bf16[384,128]{1,0:T(8,128)(2,1)} %x.10) | copy-start | bytes 294916
  146.1 21.6 %all-to-all-start.3 = ((f32[16,24,128]{2,1,0:T(8,128)}), f32[16,24,128]{2,1,0:T(8,128)S(1)}, u32[]{:S(2)}, u32[]{:S(2)}) async-start(f32[16,24,128]{2,1,0:T(8,128)} %bitcast.2), calls=%async_computation.3 | async-start | bytes 393216 | tf_op jit(solution)/shard_map/all_to_all | solution.py:150

commit v2 on v1

--- a/solution.py
+++ b/solution.py
@@ -15,12 +15,12 @@
 N = 8
 
 
-def call(body, outs, *operands):
-    vmem = pl.BlockSpec(memory_space=pltpu.VMEM)
+def call(body, outs, *operands, unread=0):
+    vmem, stay = (pl.BlockSpec(memory_space=m) for m in (pltpu.VMEM, pl.ANY))
     return pl.pallas_call(
         body,
         out_shape=outs,
-        in_specs=[vmem] * len(operands),
+        in_specs=[vmem] * (len(operands) - unread) + [stay] * unread,
         out_specs=jax.tree.map(lambda _: vmem, outs),
         compiler_params=PARAMS,
     )(*operands)
@@ -66,17 +66,23 @@
         ).astype(BF16)
 
 
-def add_blocks(parts, out):
+def add_blocks(parts, out, rounded):
     total = parts[0].astype(F32)
-    for j in range(1, parts.shape[0]):
+    for j in range(1, N):
         total = total + parts[j].astype(F32)
     out[...] = total
+    rounded[...] = total.astype(BF16)
 
 
-def activate(parts, act, slope):
-    v = parts[0]
-    for j in range(1, parts.shape[0]):
-        v = v + parts[j]
+def add_all(own, others):
+    total = own[...]
+    for other in others:
+        total = total + other[...].astype(F32)
+    return total
+
+
+def activate(own, p1, p2, p3, act, slope):
+    v = add_all(own, (p1, p2, p3))
     k = np.float32(np.sqrt(2 / np.pi))
     cube = np.float32(0.044715)
     t = jnp.tanh(k * (v + cube * (v * v * v)))
@@ -88,11 +94,8 @@
         act[j] = a
 
 
-def back(parts, slope, out):
-    g = parts[0]
-    for j in range(1, parts.shape[0]):
-        g = g + parts[j]
-    p = (g * slope[...]).astype(BF16)
+def back(own, p1, p2, p3, slope, after, out):
+    p = (add_all(own, (p1, p2, p3)) * slope[...]).astype(BF16)
     for j in range(N):
         out[j] = p
 
@@ -132,17 +135,23 @@
     blocks = s((N, T, B), BF16)
     swap = lambda v: lax.ppermute(v, "c", OTHER)
     over_x = lambda v: lax.all_to_all(v, "x", 0, 0, tiled=True)
-    over_z = lambda v: lax.all_gather(v, "zh", axis=0, tiled=False)
+
+    def over_z(own):
+        return own[0], *(
+            lax.ppermute(own[1], "zh", [(i, (i + step) % 4) for i in range(4)])
+            for step in (1, 3, 2)
+        )
 
     theirs_in = swap(call(pack_in, s((T + N * B, B), BF16), inputs, w_in))
     theirs_out = swap(call(pack_out, s((T + N * B, B), BF16), grad_out, w_out))
     hidden = over_x(call(hidden_part, blocks, inputs, w_in, theirs_in))
     grad = over_x(call(grad_part, blocks, grad_out, w_out, theirs_out))
-    hidden = over_z(call(add_blocks, s((T, B), F32), hidden))
-    act, slope = call(activate, (blocks, s((T, B), F32)), hidden)
+    summed = (s((T, B), F32), s((T, B), BF16))
+    hidden = over_z(call(add_blocks, summed, hidden))
+    act, slope = call(activate, (blocks, s((T, B), F32)), *hidden)
     act = over_x(act)
-    grad = over_z(call(add_blocks, s((T, B), F32), grad))
-    pre = over_x(call(back, blocks, grad, slope))
+    grad = over_z(call(add_blocks, summed, grad))
+    pre = over_x(call(back, blocks, *grad, slope, act, unread=1))
     act_theirs = swap(act)
     grad_w_out = call(weight_out, s((2 * N * B, B), F32), act, act_theirs, grad_out)
     pre_theirs = swap(pre)

time: 169 us -> 153 us (0.905)
  blocking collectives: 57.8 us -> 25.9 us
  starting transfers between devices: 57.3 us -> 65.9 us
  waiting for transfers between devices: 40 us -> 48.5 us
    all_gather x2 -> x0, blocking collectives: 37.6 us -> none  [per_device(): over_z = lambda v: lax.all_gather(v, 'zh', axis=0, tiled=False)]
    ppermute x0 -> x6, starting transfers between devices: none -> 24.6 us  [over_z(): lax.ppermute(own[1], 'zh', [(i, (i + step) % 4) for i in range(4)])]
    ppermute x4, starting transfers between devices: 34.8 us -> 22.8 us  [per_device(): swap = lambda v: lax.ppermute(v, 'c', OTHER)]
    ppermute x0 -> x6, waiting for transfers between devices: none -> 11.4 us  [over_z(): lax.ppermute(own[1], 'zh', [(i, (i + step) % 4) for i in range(4)])]
    all_to_all x1, blocking collectives: 20.2 us -> 25.9 us  [per_device(): over_x = lambda v: lax.all_to_all(v, 'x', 0, 0, tiled=True)]
    all_to_all x1, starting transfers between devices: 11.5 us -> 7.65 us  [per_device(): lax.all_to_all(part.reshape(16, T // 16, B), ('y', 'zl'), 0, 0, tiled=True)]
    all_to_all x3, waiting for transfers between devices: 31.6 us -> 28.2 us  [per_device(): over_x = lambda v: lax.all_to_all(v, 'x', 0, 0, tiled=True)]
  transfers between devices with their start and end apart: 8 -> 14, of which waited for: 6 -> 8; matrix products, arithmetic and copies ran while one was open for 0% -> 0% of each run, Pallas kernels for 5% -> 5%
where the time goes in v2:
time: 153 us; the launch traced here: 152 us
  starting transfers between devices  65.9 us (43%)
  waiting for transfers between devices  48.5 us (32%)
  blocking collectives  25.9 us (17%)
  Pallas kernels  9.36 us (6%)
  local copies, waits for them, and re-layouts  1.95 us (1%)
    all_to_all x3, waiting for transfers between devices, per_device(): over_x = lambda v: lax.all_to_all(v, 'x', 0, 0, tiled=True)  28.2 us
    all_to_all x1, blocking collectives, per_device(): over_x = lambda v: lax.all_to_all(v, 'x', 0, 0, tiled=True)  25.9 us
    ppermute x6, starting transfers between devices, over_z(): lax.ppermute(own[1], 'zh', [(i, (i + step) % 4) for i in range(4)])  24.6 us
    ppermute x4, starting transfers between devices, per_device(): swap = lambda v: lax.ppermute(v, 'c', OTHER)  22.8 us
    ppermute x6, waiting for transfers between devices, over_z(): lax.ppermute(own[1], 'zh', [(i, (i + step) % 4) for i in range(4)])  11.4 us
    all_to_all x3, starting transfers between devices, per_device(): over_x = lambda v: lax.all_to_all(v, 'x', 0, 0, tiled=True)  10.8 us
    pallas_call x12, Pallas kernels, call(): pl.pallas_call(body, out_shape=outs, in_specs=[vmem] * (len(operands) - u...  9.36 us
    all_to_all x1, starting transfers between devices, per_device(): lax.all_to_all(part.reshape(16, T // 16, B), ('y', 'zl'), 0, 0, tiled=True)  7.65 us
  transfers between devices with their start and end apart: 14, of which 8 were waited for; matrix products, arithmetic and copies ran while one was open for 0% of the time, Pallas kernels for 5%

profile of v2, /device:TPU:1, one launch (start us, length us, event | category | flops | bytes accessed | tf_op | source)
XLA Modules:
  0.0 152.5 jit_solution(8153855130493037398)
XLA Ops:
  2.6 16.1 %collective-permute-start.4 = (bf16[1408,128]{1,0:T(8,128)(2,1)S(1)}, bf16[1408,128]{1,0:T(8,128)(2,1)S(1)}, u32[]{:S(2)}, u32[]{:S(2)}) collective-permute-start(bf16[1408,128]{1,0:T(8,128)(2,1)S(1)} %shard_map.70), channel_id=1, source_target_pairs={{0,16},{16,0},{1,17},{17,1},{2,18},{18,2},{3,19},{19,3},{4,20},{20... | collective-permute-start | bytes 1081352 | tf_op jit(solution)/shard_map/ppermute | solution.py:136
  21.4 3.7 %all-to-all-start.1 = ((bf16[8,384,128]{2,1,0:T(8,128)(2,1)}), bf16[8,384,128]{2,1,0:T(8,128)(2,1)S(1)}, u32[]{:S(2)}, u32[]{:S(2)}) async-start(bf16[8,384,128]{2,1,0:T(8,128)(2,1)} %shard_map.71), calls=%async_computation.1 | async-start | bytes 1572864 | tf_op jit(solution)/shard_map/all_to_all | solution.py:137
  25.2 2.3 %collective-permute-start = (bf16[1408,128]{1,0:T(8,128)(2,1)S(1)}, bf16[1408,128]{1,0:T(8,128)(2,1)S(1)}, u32[]{:S(2)}, u32[]{:S(2)}) collective-permute-start(bf16[1408,128]{1,0:T(8,128)(2,1)S(1)} %shard_map.67), channel_id=1, source_target_pairs={{0,16},{16,0},{1,17},{17,1},{2,18},{18,2},{3,19},{19,3},{4,20},{20... | collective-permute-start | bytes 1081352 | tf_op jit(solution)/shard_map/ppermute | solution.py:136
  28.8 1.5 shard_map.68
  30.2 18.5 %all-to-all-done.1.parts = bf16[8,384,128]{2,1,0:T(8,128)(2,1)S(1)} async-done(((bf16[8,384,128]{2,1,0:T(8,128)(2,1)}), bf16[8,384,128]{2,1,0:T(8,128)(2,1)S(1)}, u32[]{:S(2)}, u32[]{:S(2)}) %all-to-all-start.1) | async-done | bytes 786464 | tf_op jit(solution)/shard_map/all_to_all | solution.py:137
  48.7 3.5 %all-to-all-start = ((bf16[8,384,128]{2,1,0:T(8,128)(2,1)}), bf16[8,384,128]{2,1,0:T(8,128)(2,1)S(1)}, u32[]{:S(2)}, u32[]{:S(2)}) async-start(bf16[8,384,128]{2,1,0:T(8,128)(2,1)} %shard_map.68), calls=%async_computation | async-start | bytes 1572864 | tf_op jit(solution)/shard_map/all_to_all | solution.py:137
  52.4 4.6 %collective-permute-start.7 = (bf16[384,128]{1,0:T(8,128)(2,1)S(1)}, bf16[384,128]{1,0:T(8,128)(2,1)S(1)}, u32[]{:S(2)}, u32[]{:S(2)}) collective-permute-start(bf16[384,128]{1,0:T(8,128)(2,1)S(1)} %get-tuple-element.12), channel_id=1, source_target_pairs={{0,64},{32,96},{64,0},{96,32},{1,65},{33,97},{65,1},{97,33},{2,66}... | collective-permute-start | bytes 294920 | tf_op jit(solution)/shard_map/ppermute | solution.py:141
  56.9 3.8 %collective-permute-start.6 = (bf16[384,128]{1,0:T(8,128)(2,1)S(1)}, bf16[384,128]{1,0:T(8,128)(2,1)S(1)}, u32[]{:S(2)}, u32[]{:S(2)}) collective-permute-start(bf16[384,128]{1,0:T(8,128)(2,1)S(1)} %get-tuple-element.12), channel_id=1, source_target_pairs={{0,96},{32,0},{64,32},{96,64},{1,97},{33,1},{65,33},{97,65},{2,98}... | collective-permute-start | bytes 294920 | tf_op jit(solution)/shard_map/ppermute | solution.py:141
  60.7 4.0 %collective-permute-start.5 = (bf16[384,128]{1,0:T(8,128)(2,1)S(1)}, bf16[384,128]{1,0:T(8,128)(2,1)S(1)}, u32[]{:S(2)}, u32[]{:S(2)}) collective-permute-start(bf16[384,128]{1,0:T(8,128)(2,1)S(1)} %get-tuple-element.12), channel_id=1, source_target_pairs={{0,32},{32,64},{64,96},{96,0},{1,33},{33,65},{65,97},{97,1},{2,34}... | collective-permute-start | bytes 294920 | tf_op jit(solution)/shard_map/ppermute | solution.py:141
  64.7 5.5 %collective-permute-done.6.p2 = bf16[384,128]{1,0:T(8,128)(2,1)S(1)} collective-permute-done((bf16[384,128]{1,0:T(8,128)(2,1)S(1)}, bf16[384,128]{1,0:T(8,128)(2,1)S(1)}, u32[]{:S(2)}, u32[]{:S(2)}) %collective-permute-start.6) | collective-permute-done | bytes 98336 | tf_op jit(solution)/shard_map/ppermute | solution.py:141
  71.2 4.6 %all-to-all-done.parts = bf16[8,384,128]{2,1,0:T(8,128)(2,1)S(1)} async-done(((bf16[8,384,128]{2,1,0:T(8,128)(2,1)}), bf16[8,384,128]{2,1,0:T(8,128)(2,1)S(1)}, u32[]{:S(2)}, u32[]{:S(2)}) %all-to-all-start) | async-done | bytes 786464 | tf_op jit(solution)/shard_map/all_to_all | solution.py:137
  75.8 3.5 %all-to-all-start.2 = ((bf16[8,384,128]{2,1,0:T(8,128)(2,1)}), bf16[8,384,128]{2,1,0:T(8,128)(2,1)S(1)}, u32[]{:S(2)}, u32[]{:S(2)}) async-start(bf16[8,384,128]{2,1,0:T(8,128)(2,1)} %get-tuple-element.14), calls=%async_computation.2 | async-start | bytes 1572864 | tf_op jit(solution)/shard_map/all_to_all | solution.py:137
  79.4 4.6 %collective-permute-start.3 = (bf16[384,128]{1,0:T(8,128)(2,1)S(1)}, bf16[384,128]{1,0:T(8,128)(2,1)S(1)}, u32[]{:S(2)}, u32[]{:S(2)}) collective-permute-start(bf16[384,128]{1,0:T(8,128)(2,1)S(1)} %get-tuple-element.10), channel_id=1, source_target_pairs={{0,64},{32,96},{64,0},{96,32},{1,65},{33,97},{65,1},{97,33},{2,66}... | collective-permute-start | bytes 294920 | tf_op jit(solution)/shard_map/ppermute | solution.py:141
  84.0 3.8 %collective-permute-start.2 = (bf16[384,128]{1,0:T(8,128)(2,1)S(1)}, bf16[384,128]{1,0:T(8,128)(2,1)S(1)}, u32[]{:S(2)}, u32[]{:S(2)}) collective-permute-start(bf16[384,128]{1,0:T(8,128)(2,1)S(1)} %get-tuple-element.10), channel_id=1, source_target_pairs={{0,96},{32,0},{64,32},{96,64},{1,97},{33,1},{65,33},{97,65},{2,98}... | collective-permute-start | bytes 294920 | tf_op jit(solution)/shard_map/ppermute | solution.py:141
  87.8 4.0 %collective-permute-start.1 = (bf16[384,128]{1,0:T(8,128)(2,1)S(1)}, bf16[384,128]{1,0:T(8,128)(2,1)S(1)}, u32[]{:S(2)}, u32[]{:S(2)}) collective-permute-start(bf16[384,128]{1,0:T(8,128)(2,1)S(1)} %get-tuple-element.10), channel_id=1, source_target_pairs={{0,32},{32,64},{64,96},{96,0},{1,33},{33,65},{65,97},{97,1},{2,34}... | collective-permute-start | bytes 294920 | tf_op jit(solution)/shard_map/ppermute | solution.py:141
  91.8 5.9 %collective-permute-done.2.p2 = bf16[384,128]{1,0:T(8,128)(2,1)S(1)} collective-permute-done((bf16[384,128]{1,0:T(8,128)(2,1)S(1)}, bf16[384,128]{1,0:T(8,128)(2,1)S(1)}, u32[]{:S(2)}, u32[]{:S(2)}) %collective-permute-start.2) | collective-permute-done | bytes 98336 | tf_op jit(solution)/shard_map/ppermute | solution.py:141
  97.7 5.2 %all-to-all-done.2.after.mine = bf16[8,384,128]{2,1,0:T(8,128)(2,1)S(1)} async-done(((bf16[8,384,128]{2,1,0:T(8,128)(2,1)}), bf16[8,384,128]{2,1,0:T(8,128)(2,1)S(1)}, u32[]{:S(2)}, u32[]{:S(2)}) %all-to-all-start.2) | async-done | bytes 786464 | tf_op jit(solution)/shard_map/all_to_all | solution.py:137
  102.9 25.9 %all_to_all.25.mine = bf16[8,384,128]{2,1,0:T(8,128)(2,1)S(1)} all-to-all(bf16[8,384,128]{2,1,0:T(8,128)(2,1)S(1)} %shard_map.74), channel_id=1, replica_groups=mesh['x'=8,'zh'=4,'c'=2,'y'=8,'zl'=2] {'x'}, dimensions={0} | all-to-all | bytes 1572864 | tf_op jit(solution)/shard_map/all_to_all | solution.py:137
  128.9 2.6 %collective-permute-start.8 = (bf16[8,384,128]{2,1,0:T(8,128)(2,1)S(1)}, bf16[8,384,128]{2,1,0:T(8,128)(2,1)S(1)}, u32[]{:S(2)}, u32[]{:S(2)}) collective-permute-start(bf16[8,384,128]{2,1,0:T(8,128)(2,1)S(1)} %all_to_all.25.mine), channel_id=1, source_target_pairs={{0,16},{16,0},{1,17},{17,1},{2,18},{18,2},{3,19},{19,3},{4,20},{20... | collective-permute-start | bytes 2359304 | tf_op jit(solution)/shard_map/ppermute | solution.py:136
  131.5 1.9 %collective-permute-start.9 = (bf16[8,384,128]{2,1,0:T(8,128)(2,1)S(1)}, bf16[8,384,128]{2,1,0:T(8,128)(2,1)S(1)}, u32[]{:S(2)}, u32[]{:S(2)}) collective-permute-start(bf16[8,384,128]{2,1,0:T(8,128)(2,1)S(1)} %all-to-all-done.2.after.mine), channel_id=1, source_target_pairs={{0,16},{16,0},{1,17},{17,1},{2,18},{18,2},{3,19},{19,3},{4,20},{20... | collective-permute-start | bytes 2359304 | tf_op jit(solution)/shard_map/ppermute | solution.py:136
  134.7 7.7 %all-to-all-start.4 = ((f32[16,24,128]{2,1,0:T(8,128)}), f32[16,24,128]{2,1,0:T(8,128)S(1)}, u32[]{:S(2)}, u32[]{:S(2)}) async-start(f32[16,24,128]{2,1,0:T(8,128)} %bitcast), calls=%async_computation.4 | async-start | bytes 393216 | tf_op jit(solution)/shard_map/all_to_all | solution.py:159
  142.4 1.6 %shard_map.78 = f32[2048,128]{1,0:T(8,128)} custom-call(bf16[8,384,128]{2,1,0:T(8,128)(2,1)S(1)} %all-to-all-done.2.after.mine, bf16[8,384,128]{2,1,0:T(8,128)(2,1)S(1)} %collective-permute-done.9.theirs, bf16[384,128]{1,0:T(8,128)(2,1)S(1)} %copy-done.3), custom_call_target="tpu_custom_call" | custom-call | tf_op jit(solution)/shard_map/pallas_call | solution.py:20
  144.0 1.6 %shard_map.77 = f32[128,2048]{1,0:T(8,128)} custom-call(bf16[8,384,128]{2,1,0:T(8,128)(2,1)S(1)} %all_to_all.25.mine, bf16[8,384,128]{2,1,0:T(8,128)(2,1)S(1)} %collective-permute-done.8.theirs, bf16[384,128]{1,0:T(8,128)(2,1)S(1)} %copy-done.5), custom_call_target="tpu_custom_call" | custom-call | tf_op jit(solution)/shard_map/pallas_call | solution.py:20
  145.6 6.3 %all-to-all-done.4.parts = f32[16,24,128]{2,1,0:T(8,128)S(1)} async-done(((f32[16,24,128]{2,1,0:T(8,128)}), f32[16,24,128]{2,1,0:T(8,128)S(1)}, u32[]{:S(2)}, u32[]{:S(2)}) %all-to-all-start.4) | async-done | bytes 196640 | tf_op jit(solution)/shard_map/all_to_all | solution.py:159
  (29 shorter events, 9.3 us)
Async XLA Ops:
  0.6 1.0 copy-start
  1.7 0.9 copy-start.4
  2.6 17.4 %collective-permute-start.4 = (bf16[1408,128]{1,0:T(8,128)(2,1)S(1)}, bf16[1408,128]{1,0:T(8,128)(2,1)S(1)}, u32[]{:S(2)}, u32[]{:S(2)}) collective-permute-start(bf16[1408,128]{1,0:T(8,128)(2,1)S(1)} %shard_map.70), channel_id=1, source_target_pairs={{0,16},{16,0},{1,17},{17,1},{2,18},{18,2},{3,19},{19,3},{4,20},{20... | collective-permute-start | bytes 1081352 | tf_op jit(solution)/shard_map/ppermute | solution.py:136
  21.4 3.7 %copy-start.2 = (bf16[2048,128]{1,0:T(8,128)(2,1)S(1)}, bf16[2048,128]{1,0:T(8,128)(2,1)}, u32[]{:S(2)}) copy-start(bf16[2048,128]{1,0:T(8,128)(2,1)} %w.6) | copy-start | bytes 1572868
  21.4 3.7 %copy-start.3 = (bf16[384,128]{1,0:T(8,128)(2,1)S(1)}, bf16[384,128]{1,0:T(8,128)(2,1)}, u32[]{:S(2)}) copy-start(bf16[384,128]{1,0:T(8,128)(2,1)} %x.11) | copy-start | bytes 294916
  21.4 27.2 %all-to-all-start.1 = ((bf16[8,384,128]{2,1,0:T(8,128)(2,1)}), bf16[8,384,128]{2,1,0:T(8,128)(2,1)S(1)}, u32[]{:S(2)}, u32[]{:S(2)}) async-start(bf16[8,384,128]{2,1,0:T(8,128)(2,1)} %shard_map.71), calls=%async_computation.1 | async-start | bytes 1572864 | tf_op jit(solution)/shard_map/all_to_all | solution.py:137
  25.2 3.6 %collective-permute-start = (bf16[1408,128]{1,0:T(8,128)(2,1)S(1)}, bf16[1408,128]{1,0:T(8,128)(2,1)S(1)}, u32[]{:S(2)}, u32[]{:S(2)}) collective-permute-start(bf16[1408,128]{1,0:T(8,128)(2,1)S(1)} %shard_map.67), channel_id=1, source_target_pairs={{0,16},{16,0},{1,17},{17,1},{2,18},{18,2},{3,19},{19,3},{4,20},{20... | collective-permute-start | bytes 1081352 | tf_op jit(solution)/shard_map/ppermute | solution.py:136
  48.7 27.1 %all-to-all-start = ((bf16[8,384,128]{2,1,0:T(8,128)(2,1)}), bf16[8,384,128]{2,1,0:T(8,128)(2,1)S(1)}, u32[]{:S(2)}, u32[]{:S(2)}) async-start(bf16[8,384,128]{2,1,0:T(8,128)(2,1)} %shard_map.68), calls=%async_computation | async-start | bytes 1572864 | tf_op jit(solution)/shard_map/all_to_all | solution.py:137
  52.4 12.3 %collective-permute-start.7 = (bf16[384,128]{1,0:T(8,128)(2,1)S(1)}, bf16[384,128]{1,0:T(8,128)(2,1)S(1)}, u32[]{:S(2)}, u32[]{:S(2)}) collective-permute-start(bf16[384,128]{1,0:T(8,128)(2,1)S(1)} %get-tuple-element.12), channel_id=1, source_target_pairs={{0,64},{32,96},{64,0},{96,32},{1,65},{33,97},{65,1},{97,33},{2,66}... | collective-permute-start | bytes 294920 | tf_op jit(solution)/shard_map/ppermute | solution.py:141
  56.9 13.3 %collective-permute-start.6 = (bf16[384,128]{1,0:T(8,128)(2,1)S(1)}, bf16[384,128]{1,0:T(8,128)(2,1)S(1)}, u32[]{:S(2)}, u32[]{:S(2)}) collective-permute-start(bf16[384,128]{1,0:T(8,128)(2,1)S(1)} %get-tuple-element.12), channel_id=1, source_target_pairs={{0,96},{32,0},{64,32},{96,64},{1,97},{33,1},{65,33},{97,65},{2,98}... | collective-permute-start | bytes 294920 | tf_op jit(solution)/shard_map/ppermute | solution.py:141
  60.7 9.5 %collective-permute-start.5 = (bf16[384,128]{1,0:T(8,128)(2,1)S(1)}, bf16[384,128]{1,0:T(8,128)(2,1)S(1)}, u32[]{:S(2)}, u32[]{:S(2)}) collective-permute-start(bf16[384,128]{1,0:T(8,128)(2,1)S(1)} %get-tuple-element.12), channel_id=1, source_target_pairs={{0,32},{32,64},{64,96},{96,0},{1,33},{33,65},{65,97},{97,1},{2,34}... | collective-permute-start | bytes 294920 | tf_op jit(solution)/shard_map/ppermute | solution.py:141
  75.8 27.1 %all-to-all-start.2 = ((bf16[8,384,128]{2,1,0:T(8,128)(2,1)}), bf16[8,384,128]{2,1,0:T(8,128)(2,1)S(1)}, u32[]{:S(2)}, u32[]{:S(2)}) async-start(bf16[8,384,128]{2,1,0:T(8,128)(2,1)} %get-tuple-element.14), calls=%async_computation.2 | async-start | bytes 1572864 | tf_op jit(solution)/shard_map/all_to_all | solution.py:137
  79.4 12.3 %collective-permute-start.3 = (bf16[384,128]{1,0:T(8,128)(2,1)S(1)}, bf16[384,128]{1,0:T(8,128)(2,1)S(1)}, u32[]{:S(2)}, u32[]{:S(2)}) collective-permute-start(bf16[384,128]{1,0:T(8,128)(2,1)S(1)} %get-tuple-element.10), channel_id=1, source_target_pairs={{0,64},{32,96},{64,0},{96,32},{1,65},{33,97},{65,1},{97,33},{2,66}... | collective-permute-start | bytes 294920 | tf_op jit(solution)/shard_map/ppermute | solution.py:141
  84.0 13.6 %collective-permute-start.2 = (bf16[384,128]{1,0:T(8,128)(2,1)S(1)}, bf16[384,128]{1,0:T(8,128)(2,1)S(1)}, u32[]{:S(2)}, u32[]{:S(2)}) collective-permute-start(bf16[384,128]{1,0:T(8,128)(2,1)S(1)} %get-tuple-element.10), channel_id=1, source_target_pairs={{0,96},{32,0},{64,32},{96,64},{1,97},{33,1},{65,33},{97,65},{2,98}... | collective-permute-start | bytes 294920 | tf_op jit(solution)/shard_map/ppermute | solution.py:141
  87.8 9.9 %collective-permute-start.1 = (bf16[384,128]{1,0:T(8,128)(2,1)S(1)}, bf16[384,128]{1,0:T(8,128)(2,1)S(1)}, u32[]{:S(2)}, u32[]{:S(2)}) collective-permute-start(bf16[384,128]{1,0:T(8,128)(2,1)S(1)} %get-tuple-element.10), channel_id=1, source_target_pairs={{0,32},{32,64},{64,96},{96,0},{1,33},{33,65},{65,97},{97,1},{2,34}... | collective-permute-start | bytes 294920 | tf_op jit(solution)/shard_map/ppermute | solution.py:141
  102.9 30.5 %copy-start.1 = (bf16[128,2048]{1,0:T(8,128)(2,1)S(1)}, bf16[128,2048]{1,0:T(8,128)(2,1)}, u32[]{:S(2)}) copy-start(bf16[128,2048]{1,0:T(8,128)(2,1)} %w.9) | copy-start | bytes 1572868
  128.9 4.5 %collective-permute-start.8 = (bf16[8,384,128]{2,1,0:T(8,128)(2,1)S(1)}, bf16[8,384,128]{2,1,0:T(8,128)(2,1)S(1)}, u32[]{:S(2)}, u32[]{:S(2)}) collective-permute-start(bf16[8,384,128]{2,1,0:T(8,128)(2,1)S(1)} %all_to_all.25.mine), channel_id=1, source_target_pairs={{0,16},{16,0},{1,17},{17,1},{2,18},{18,2},{3,19},{19,3},{4,20},{20... | collective-permute-start | bytes 2359304 | tf_op jit(solution)/shard_map/ppermute | solution.py:136
  131.5 10.9 %collective-permute-start.9 = (bf16[8,384,128]{2,1,0:T(8,128)(2,1)S(1)}, bf16[8,384,128]{2,1,0:T(8,128)(2,1)S(1)}, u32[]{:S(2)}, u32[]{:S(2)}) collective-permute-start(bf16[8,384,128]{2,1,0:T(8,128)(2,1)S(1)} %all-to-all-done.2.after.mine), channel_id=1, source_target_pairs={{0,16},{16,0},{1,17},{17,1},{2,18},{18,2},{3,19},{19,3},{4,20},{20... | collective-permute-start | bytes 2359304 | tf_op jit(solution)/shard_map/ppermute | solution.py:136
  134.7 17.2 %all-to-all-start.4 = ((f32[16,24,128]{2,1,0:T(8,128)}), f32[16,24,128]{2,1,0:T(8,128)S(1)}, u32[]{:S(2)}, u32[]{:S(2)}) async-start(f32[16,24,128]{2,1,0:T(8,128)} %bitcast), calls=%async_computation.4 | async-start | bytes 393216 | tf_op jit(solution)/shard_map/all_to_all | solution.py:159
  142.3 1.6 %copy-start.5 = (bf16[384,128]{1,0:T(8,128)(2,1)S(1)}, bf16[384,128]{1,0:T(8,128)(2,1)}, u32[]{:S(2)}) copy-start(bf16[384,128]{1,0:T(8,128)(2,1)} %x.10) | copy-start | bytes 294916

commit v3 on v0

v3 whole, which is shorter than its diff:
```python
import jax
import jax.numpy as jnp
import numpy as np
from jax import lax
from jax.experimental import pallas as pl
from jax.experimental.pallas import tpu as pltpu
from jax.sharding import PartitionSpec as P

F32, BF16 = jnp.float32, jnp.bfloat16
PARAMS = pltpu.CompilerParams(vmem_limit_bytes=40 * 1024 * 1024)
T, B = 384, 128
X, Z, C = 8, 4, 2
Q = T // Z

at = lambda x, z, c: (x * Z + z) * C + c
FOURS = [[at(2 * a + b, z, 0) for a in range(4)] for b in range(2) for z in range(Z)]
FOURS += [[at(x, z, 1) for z in range(Z)] for x in range(X)]
EIGHTS = [[at(2 * a + b, z, 0) for b in range(2) for z in range(Z)] for a in range(4)]
EIGHTS += [[at(x, z, 1) for x in range(X)] for z in range(Z)]
SWAP = [(i, i ^ 1) for i in range(X * Z * C)]


def place(core, x, z):
    first = core == 0
    return jnp.where(first, x // 2, z), jnp.where(first, x % 2 * Z + z, x)


def call(body, outs, *operands):
    vmem = pl.BlockSpec(memory_space=pltpu.VMEM)
    return pl.pallas_call(
        body,
        out_shape=outs,
        in_specs=[vmem] * len(operands),
        out_specs=jax.tree.map(lambda _: vmem, outs),
        compiler_params=PARAMS,
    )(*operands)


def this_core():
    return lax.rem(lax.axis_index("gx"), C)


def columns(core, x):
    return pl.ds(pl.multiple_of((core * X + x) * B, B), B)


def dot(a, b, dims):
    return lax.dot_general(a, b, (dims, ((), ())), preferred_element_type=F32)


def pack(x, w_in, y, w_out, out):
    other = 1 - this_core()
    out[0, :T] = x[...]
    out[1, :T] = y[...]
    for j in range(X):
        rows = slice(T + j * B, T + (j + 1) * B)
        out[0, rows] = w_in[:, columns(other, j)]
        out[1, rows] = w_out[columns(other, j), :]


def partial_sums(x, w_in, y, w_out, theirs, out):
    core = this_core()
    for j in range(X):
        rows = slice(T + j * B, T + (j + 1) * B)
        h = dot(x[...], w_in[:, columns(core, j)], ((1,), (0,)))
        h = h + dot(theirs[0, :T], theirs[0, rows], ((1,), (0,)))
        g = dot(y[...], w_out[columns(core, j), :], ((1,), (1,)))
        g = g + dot(theirs[1, :T], theirs[1, rows], ((1,), (1,)))
        h, g = h.astype(BF16), g.astype(BF16)
        for z in range(Z):
            four, eight = place(core, j, z)
            out[four, eight, 0] = h[z * Q : (z + 1) * Q]
            out[four, eight, 1] = g[z * Q : (z + 1) * Q]


def total(parts):
    value = parts[0].astype(F32)
    for j in range(1, parts.shape[0]):
        value = value + parts[j].astype(F32)
    return value


def add_fours(parts, out):
    out[...] = total(parts).astype(BF16)


def middle(parts, out):
    both = total(parts)
    v, g = both[0], both[1]
    k = np.float32(np.sqrt(2 / np.pi))
    cube = np.float32(0.044715)
    t = jnp.tanh(k * (v + cube * (v * v * v)))
    act = (0.5 * v * (1.0 + t)).astype(BF16)
    slope = 0.5 * (1.0 + t) + 0.5 * v * (1.0 - t * t) * (
        k * (1.0 + 3.0 * cube * (v * v))
    )
    pre = (g * slope).astype(BF16)
    for j in range(X):
        out[j, 0] = act
        out[j, 1] = pre


def copies(part, out):
    for j in range(4):
        out[j] = part[...]


def tokens(ref, core, x, which):
    blocks = [ref[(*place(core, x, z), which)] for z in range(Z)]
    return jnp.concatenate(blocks, axis=0)


def input_part(mine, theirs, w, out):
    core = this_core()
    value = jnp.zeros((T, B), F32)
    for who, ref in ((core, mine), (1 - core, theirs)):
        for j in range(X):
            value += dot(tokens(ref, who, j, 1), w[:, columns(who, j)], ((1,), (1,)))
    out[...] = value


def weights(mine, theirs, x, y, out_in, out_out):
    core = this_core()
    for who, ref in ((core, mine), (1 - core, theirs)):
        for j in range(X):
            there = columns(who, j)
            out_in[:, there] = dot(x[...], tokens(ref, who, j, 1), ((0,), (0,)))
            out_out[there, :] = dot(tokens(ref, who, j, 0), y[...], ((0,), (0,)))


def finish(parts, out):
    out[...] = total(parts).astype(BF16)


def per_device(inputs, grad_out, w_in, w_out):
    s = jax.ShapeDtypeStruct
    swap = lambda v: lax.ppermute(v, "gx", SWAP)

    def exchange(v, groups):
        return lax.all_to_all(v, "gx", 0, 0, axis_index_groups=groups, tiled=True)

    both = (4, X, 2, Q, B)
    theirs = swap(call(pack, s((2, T + X * B, B), BF16), inputs, w_in, grad_out, w_out))
    sums = call(partial_sums, s(both, BF16), inputs, w_in, grad_out, w_out, theirs)
    sums = call(add_fours, s(both[1:], BF16), exchange(sums, FOURS))
    mine = call(middle, s(both[1:], BF16), exchange(sums, EIGHTS))
    mine = exchange(call(copies, s(both, BF16), exchange(mine, EIGHTS)), FOURS)
    theirs = swap(mine)
    part = call(input_part, s((T, B), F32), mine, theirs, w_in)
    part = lax.all_to_all(part.reshape(16, T // 16, B), "gy", 0, 0, tiled=True)
    outs = (s((B, 2 * X * B), F32), s((2 * X * B, B), F32))
    grad_w_in, grad_w_out = call(weights, outs, mine, theirs, inputs, grad_out)
    grad_inputs = call(finish, s((T // 16, B), BF16), part)
    return (grad_inputs, grad_w_in, grad_w_out)


def solution(mesh):
    return jax.shard_map(
        per_device,
        mesh=mesh,
        in_specs=(P(None, "gx"), P(None, "gx"), P("gx", "gy"), P("gy", "gx")),
        out_specs=(P("gy", "gx"), P("gx", "gy"), P("gy", "gx")),
        check_vma=False,
    )
```

time: 582 us -> 138 us (0.24)
  the two profiles are of different devices: /device:TPU:4 before, /device:TPU:1 now
where the time goes in v3:
time: 138 us; the launch traced here: 137 us
  blocking collectives  83.2 us (60%)
  starting transfers between devices  31.4 us (23%)
  waiting for transfers between devices  12.1 us (9%)
  Pallas kernels  5.06 us (4%)
  local copies, waits for them, and re-layouts  4.55 us (3%)
    all_to_all x4, blocking collectives, exchange(): return lax.all_to_all(v, 'gx', 0, 0, axis_index_groups=groups, tiled=True)  83.2 us
    ppermute x2, starting transfers between devices, per_device(): swap = lambda v: lax.ppermute(v, 'gx', SWAP)  23.2 us
    all_to_all x1, starting transfers between devices, per_device(): part = lax.all_to_all(part.reshape(16, T // 16, B), 'gy', 0, 0, tiled=True)  8.23 us
    all_to_all x1, waiting for transfers between devices, per_device(): part = lax.all_to_all(part.reshape(16, T // 16, B), 'gy', 0, 0, tiled=True)  7.29 us
    pallas_call x8, Pallas kernels, call(): pl.pallas_call(body, out_shape=outs, in_specs=[vmem] * len(operands), out...  5.06 us
    ppermute x2, waiting for transfers between devices, per_device(): swap = lambda v: lax.ppermute(v, 'gx', SWAP)  4.81 us
    unnamed x16, local copies, waits for them, and re-layouts  4.55 us
  transfers between devices with their start and end apart: 3, of which 3 were waited for; matrix products, arithmetic and copies ran while one was open for 0% of the time, Pallas kernels for 2%

profile of v3, /device:TPU:1, one launch (start us, length us, event | category | flops | bytes accessed | tf_op | source)
XLA Modules:
  0.0 137.0 jit_solution(12868880732090822339)
XLA Ops:
  0.6 0.0 copy-start
  0.6 1.0 copy-done
  1.7 1.0 copy-done.2
  2.7 0.9 copy-done.3
  3.6 0.9 copy-done.5
  4.5 0.1 shard_map.67
  4.6 16.1 %collective-permute-start = (bf16[2,1408,128]{2,1,0:T(8,128)(2,1)S(1)}, bf16[2,1408,128]{2,1,0:T(8,128)(2,1)S(1)}, u32[]{:S(2)}, u32[]{:S(2)}) collective-permute-start(bf16[2,1408,128]{2,1,0:T(8,128)(2,1)S(1)} %shard_map.67), channel_id=1, source_target_pairs={{0,16},{16,0},{32,48},{48,32},{64,80},{80,64},{96,112},{112,96},{1... | collective-permute-start | bytes 2162696 | tf_op jit(solution)/shard_map/ppermute | solution.py:137
  20.7 1.8 %collective-permute-done.theirs = bf16[2,1408,128]{2,1,0:T(8,128)(2,1)S(1)} collective-permute-done((bf16[2,1408,128]{2,1,0:T(8,128)(2,1)S(1)}, bf16[2,1408,128]{2,1,0:T(8,128)(2,1)S(1)}, u32[]{:S(2)}, u32[]{:S(2)}) %collective-permute-start) | collective-permute-done | bytes 720928 | tf_op jit(solution)/shard_map/ppermute | solution.py:137
  22.5 1.0 shard_map.68
  23.4 24.2 %all_to_all.25.parts = bf16[4,8,2,96,128]{4,3,2,1,0:T(8,128)(2,1)S(1)} all-to-all(bf16[4,8,2,96,128]{4,3,2,1,0:T(8,128)(2,1)S(1)} %shard_map.68), channel_id=1, replica_groups={{0,256,512,768},{32,288,544,800},{64,320,576,832},{96,352,608,864},{128..., dimensions={0} | all-to-all | bytes 3145728 | tf_op jit(solution)/shard_map/all_to_all | solution.py:140
  47.7 0.2 shard_map.69
  47.9 18.1 %all_to_all.26.parts = bf16[8,2,96,128]{3,2,1,0:T(8,128)(2,1)S(1)} all-to-all(bf16[8,2,96,128]{3,2,1,0:T(8,128)(2,1)S(1)} %shard_map.69), channel_id=1, replica_groups={{0,32,64,96,128,160,192,224},{256,288,320,352,384,416,448,480},{512,544..., dimensions={0} | all-to-all | bytes 786432 | tf_op jit(solution)/shard_map/all_to_all | solution.py:140
  66.0 0.1 shard_map.70
  66.1 15.3 %all_to_all.27.part = bf16[8,2,96,128]{3,2,1,0:T(8,128)(2,1)S(1)} all-to-all(bf16[8,2,96,128]{3,2,1,0:T(8,128)(2,1)S(1)} %shard_map.70), channel_id=1, replica_groups={{0,32,64,96,128,160,192,224},{256,288,320,352,384,416,448,480},{512,544..., dimensions={0} | all-to-all | bytes 786432 | tf_op jit(solution)/shard_map/all_to_all | solution.py:140
  81.3 0.2 shard_map.71
  81.6 25.6 %all_to_all.28.mine = bf16[4,8,2,96,128]{4,3,2,1,0:T(8,128)(2,1)S(1)} all-to-all(bf16[4,8,2,96,128]{4,3,2,1,0:T(8,128)(2,1)S(1)} %shard_map.71), channel_id=1, replica_groups={{0,256,512,768},{32,288,544,800},{64,320,576,832},{96,352,608,864},{128..., dimensions={0} | all-to-all | bytes 3145728 | tf_op jit(solution)/shard_map/all_to_all | solution.py:140
  107.1 7.1 %collective-permute-start.1 = (bf16[4,8,2,96,128]{4,3,2,1,0:T(8,128)(2,1)S(1)}, bf16[4,8,2,96,128]{4,3,2,1,0:T(8,128)(2,1)S(1)}, u32[]{:S(2)}, u32[]{:S(2)}) collective-permute-start(bf16[4,8,2,96,128]{4,3,2,1,0:T(8,128)(2,1)S(1)} %all_to_all.28.mine), channel_id=1, source_target_pairs={{0,16},{16,0},{32,48},{48,32},{64,80},{80,64},{96,112},{112,96},{1... | collective-permute-start | bytes 4718600 | tf_op jit(solution)/shard_map/ppermute | solution.py:137
  114.2 3.0 %collective-permute-done.1.theirs = bf16[4,8,2,96,128]{4,3,2,1,0:T(8,128)(2,1)S(1)} collective-permute-done((bf16[4,8,2,96,128]{4,3,2,1,0:T(8,128)(2,1)S(1)}, bf16[4,8,2,96,128]{4,3,2,1,0:T(8,128)(2,1)S(1)}, u32[]{:S(2)}, u32[]{:S(2)}) %collective-permute-start.1) | collective-permute-done | bytes 1572896 | tf_op jit(solution)/shard_map/ppermute | solution.py:137
  117.3 0.6 shard_map.72
  117.8 0.7 copy-done.7
  118.5 8.2 %all-to-all-start.4 = ((f32[16,24,128]{2,1,0:T(8,128)}), f32[16,24,128]{2,1,0:T(8,128)S(1)}, u32[]{:S(2)}, u32[]{:S(2)}) async-start(f32[16,24,128]{2,1,0:T(8,128)} %bitcast.1), calls=%async_computation.4 | async-start | bytes 393216 | tf_op jit(solution)/shard_map/all_to_all | solution.py:150
  126.8 2.3 %shard_map.74 = (f32[128,2048]{1,0:T(8,128)}, f32[2048,128]{1,0:T(8,128)}) custom-call(bf16[4,8,2,96,128]{4,3,2,1,0:T(8,128)(2,1)S(1)} %all_to_all.28.mine, bf16[4,8,2,96,128]{4,3,2,1,0:T(8,128)(2,1)S(1)} %collective-permute-done.1.theirs, bf16[384,128]{1,0:T(8,128)(2,1)S(1)} %copy-done.4, bf16[384,128]{1,0:T(8,128)(2,1)S(1)} %copy-done.6), custom_call_target="tpu_custom_call" | custom-call | tf_op jit(solution)/shard_map/pallas_call | solution.py:30
  129.1 7.3 %all-to-all-done.4.parts = f32[16,24,128]{2,1,0:T(8,128)S(1)} async-done(((f32[16,24,128]{2,1,0:T(8,128)}), f32[16,24,128]{2,1,0:T(8,128)S(1)}, u32[]{:S(2)}, u32[]{:S(2)}) %all-to-all-start.4) | async-done | bytes 196640 | tf_op jit(solution)/shard_map/all_to_all | solution.py:150
  136.4 0.6 shard_map.73
  (10 shorter events, 0.0 us)
Async XLA Ops:
  0.6 1.0 copy-start
  1.7 1.0 copy-start.2
  2.7 0.9 copy-start.3
  3.6 0.9 copy-start.5
  4.6 17.9 %collective-permute-start = (bf16[2,1408,128]{2,1,0:T(8,128)(2,1)S(1)}, bf16[2,1408,128]{2,1,0:T(8,128)(2,1)S(1)}, u32[]{:S(2)}, u32[]{:S(2)}) collective-permute-start(bf16[2,1408,128]{2,1,0:T(8,128)(2,1)S(1)} %shard_map.67), channel_id=1, source_target_pairs={{0,16},{16,0},{32,48},{48,32},{64,80},{80,64},{96,112},{112,96},{1... | collective-permute-start | bytes 2162696 | tf_op jit(solution)/shard_map/ppermute | solution.py:137
  81.5 35.7 %copy-start.1 = (bf16[128,2048]{1,0:T(8,128)(2,1)S(1)}, bf16[128,2048]{1,0:T(8,128)(2,1)}, u32[]{:S(2)}) copy-start(bf16[128,2048]{1,0:T(8,128)(2,1)} %w.1) | copy-start | bytes 1572868
  107.1 19.6 %copy-start.4 = (bf16[384,128]{1,0:T(8,128)(2,1)S(1)}, bf16[384,128]{1,0:T(8,128)(2,1)}, u32[]{:S(2)}) copy-start(bf16[384,128]{1,0:T(8,128)(2,1)} %x.5) | copy-start | bytes 294916
  107.1 19.6 %copy-start.6 = (bf16[384,128]{1,0:T(8,128)(2,1)S(1)}, bf16[384,128]{1,0:T(8,128)(2,1)}, u32[]{:S(2)}) copy-start(bf16[384,128]{1,0:T(8,128)(2,1)} %y.5) | copy-start | bytes 294916
  107.1 10.1 %collective-permute-start.1 = (bf16[4,8,2,96,128]{4,3,2,1,0:T(8,128)(2,1)S(1)}, bf16[4,8,2,96,128]{4,3,2,1,0:T(8,128)(2,1)S(1)}, u32[]{:S(2)}, u32[]{:S(2)}) collective-permute-start(bf16[4,8,2,96,128]{4,3,2,1,0:T(8,128)(2,1)S(1)} %all_to_all.28.mine), channel_id=1, source_target_pairs={{0,16},{16,0},{32,48},{48,32},{64,80},{80,64},{96,112},{112,96},{1... | collective-permute-start | bytes 4718600 | tf_op jit(solution)/shard_map/ppermute | solution.py:137
  117.8 0.7 copy-start.7
  118.5 17.9 %all-to-all-start.4 = ((f32[16,24,128]{2,1,0:T(8,128)}), f32[16,24,128]{2,1,0:T(8,128)S(1)}, u32[]{:S(2)}, u32[]{:S(2)}) async-start(f32[16,24,128]{2,1,0:T(8,128)} %bitcast.1), calls=%async_computation.4 | async-start | bytes 393216 | tf_op jit(solution)/shard_map/all_to_all | solution.py:150

commit v4 on v3

--- a/solution.py
+++ b/solution.py
@@ -13,16 +13,16 @@
 Q = T // Z
 
 at = lambda x, z, c: (x * Z + z) * C + c
-FOURS = [[at(2 * a + b, z, 0) for a in range(4)] for b in range(2) for z in range(Z)]
-FOURS += [[at(x, z, 1) for z in range(Z)] for x in range(X)]
-EIGHTS = [[at(2 * a + b, z, 0) for b in range(2) for z in range(Z)] for a in range(4)]
-EIGHTS += [[at(x, z, 1) for x in range(X)] for z in range(Z)]
+EIGHTS = [[at(x, z, 0) for x in range(X)] for z in range(Z)]
+EIGHTS += [[at(2 * a + b, z, 1) for b in range(2) for z in range(Z)] for a in range(4)]
+FOURS = [[at(x, z, 0) for z in range(Z)] for x in range(X)]
+FOURS += [[at(2 * a + b, z, 1) for a in range(4)] for b in range(2) for z in range(Z)]
 SWAP = [(i, i ^ 1) for i in range(X * Z * C)]
 
 
 def place(core, x, z):
     first = core == 0
-    return jnp.where(first, x // 2, z), jnp.where(first, x % 2 * Z + z, x)
+    return jnp.where(first, x, x % 2 * Z + z), jnp.where(first, z, x // 2)
 
 
 def call(body, outs, *operands):
@@ -68,9 +68,9 @@
         g = g + dot(theirs[1, :T], theirs[1, rows], ((1,), (1,)))
         h, g = h.astype(BF16), g.astype(BF16)
         for z in range(Z):
-            four, eight = place(core, j, z)
-            out[four, eight, 0] = h[z * Q : (z + 1) * Q]
-            out[four, eight, 1] = g[z * Q : (z + 1) * Q]
+            eight, four = place(core, j, z)
+            out[eight, four, 0] = h[z * Q : (z + 1) * Q]
+            out[eight, four, 1] = g[z * Q : (z + 1) * Q]
 
 
 def total(parts):
@@ -80,13 +80,15 @@
     return value
 
 
-def add_fours(parts, out):
-    out[...] = total(parts).astype(BF16)
+def add_eights(parts, out):
+    value = total(parts).astype(BF16)
+    for j in range(4):
+        out[j] = value
 
 
 def middle(parts, out):
     both = total(parts)
-    v, g = both[0], both[1]
+    v, g = both[:, 0], both[:, 1]
     k = np.float32(np.sqrt(2 / np.pi))
     cube = np.float32(0.044715)
     t = jnp.tanh(k * (v + cube * (v * v * v)))
@@ -95,14 +97,9 @@
         k * (1.0 + 3.0 * cube * (v * v))
     )
     pre = (g * slope).astype(BF16)
-    for j in range(X):
-        out[j, 0] = act
-        out[j, 1] = pre
-
-
-def copies(part, out):
-    for j in range(4):
-        out[j] = part[...]
+    for j in range(8):
+        out[j, :, 0] = act
+        out[j, :, 1] = pre
 
 
 def tokens(ref, core, x, which):
@@ -139,12 +136,12 @@
     def exchange(v, groups):
         return lax.all_to_all(v, "gx", 0, 0, axis_index_groups=groups, tiled=True)
 
-    both = (4, X, 2, Q, B)
+    blocks = (4, 2, Q, B)
     theirs = swap(call(pack, s((2, T + X * B, B), BF16), inputs, w_in, grad_out, w_out))
-    sums = call(partial_sums, s(both, BF16), inputs, w_in, grad_out, w_out, theirs)
-    sums = call(add_fours, s(both[1:], BF16), exchange(sums, FOURS))
-    mine = call(middle, s(both[1:], BF16), exchange(sums, EIGHTS))
-    mine = exchange(call(copies, s(both, BF16), exchange(mine, EIGHTS)), FOURS)
+    sums = call(partial_sums, s((8, *blocks), BF16), inputs, w_in, grad_out, w_out, theirs)
+    sums = call(add_eights, s((4, *blocks), BF16), exchange(sums, EIGHTS))
+    mine = call(middle, s((8, *blocks), BF16), exchange(sums, FOURS))
+    mine = exchange(mine, EIGHTS)
     theirs = swap(mine)
     part = call(input_part, s((T, B), F32), mine, theirs, w_in)
     part = lax.all_to_all(part.reshape(16, T // 16, B), "gy", 0, 0, tiled=True)

time: 138 us -> 137 us (level)
  starting transfers between devices: 31.4 us -> 27 us
  blocking collectives: 83.2 us -> 86 us
    ppermute x2, starting transfers between devices: 23.2 us -> 18.1 us  [per_device(): swap = lambda v: lax.ppermute(v, 'gx', SWAP)]
    all_to_all x4 -> x3, blocking collectives: 83.2 us -> 86 us  [exchange(): return lax.all_to_all(v, 'gx', 0, 0, axis_index_groups=groups, tiled=True)]
    pallas_call x8 -> x7, Pallas kernels: 5.06 us -> 5.02 us  [call(): pl.pallas_call(body, out_shape=outs, in_specs=[vmem] * len(operands), out...]
where the time goes in v4:
time: 137 us; the launch traced here: 136 us
  blocking collectives  86 us (63%)
  starting transfers between devices  27 us (20%)
  waiting for transfers between devices  12.8 us (9%)
  Pallas kernels  5.02 us (4%)
  local copies, waits for them, and re-layouts  4.55 us (3%)
    all_to_all x3, blocking collectives, exchange(): return lax.all_to_all(v, 'gx', 0, 0, axis_index_groups=groups, tiled=True)  86 us
    ppermute x2, starting transfers between devices, per_device(): swap = lambda v: lax.ppermute(v, 'gx', SWAP)  18.1 us
    all_to_all x1, starting transfers between devices, per_device(): part = lax.all_to_all(part.reshape(16, T // 16, B), 'gy', 0, 0, tiled=True)  8.9 us
    all_to_all x1, waiting for transfers between devices, per_device(): part = lax.all_to_all(part.reshape(16, T // 16, B), 'gy', 0, 0, tiled=True)  7.58 us
    ppermute x2, waiting for transfers between devices, per_device(): swap = lambda v: lax.ppermute(v, 'gx', SWAP)  5.17 us
    pallas_call x7, Pallas kernels, call(): pl.pallas_call(body, out_shape=outs, in_specs=[vmem] * len(operands), out...  5.02 us
    unnamed x16, local copies, waits for them, and re-layouts  4.55 us
  transfers between devices with their start and end apart: 3, of which 3 were waited for; matrix products, arithmetic and copies ran while one was open for 0% of the time, Pallas kernels for 2%

profile of v4, /device:TPU:1, one launch (start us, length us, event | category | flops | bytes accessed | tf_op | source)
XLA Modules:
  0.0 136.0 jit_solution(14544278786770072558)
XLA Ops:
  0.6 0.0 copy-start
  0.6 1.0 copy-done
  1.7 1.0 copy-done.2
  2.7 0.9 copy-done.3
  3.6 0.9 copy-done.5
  4.5 0.1 shard_map.67
  4.6 16.1 %collective-permute-start = (bf16[2,1408,128]{2,1,0:T(8,128)(2,1)S(1)}, bf16[2,1408,128]{2,1,0:T(8,128)(2,1)S(1)}, u32[]{:S(2)}, u32[]{:S(2)}) collective-permute-start(bf16[2,1408,128]{2,1,0:T(8,128)(2,1)S(1)} %shard_map.67), channel_id=1, source_target_pairs={{0,16},{16,0},{32,48},{48,32},{64,80},{80,64},{96,112},{112,96},{1... | collective-permute-start | bytes 2162696 | tf_op jit(solution)/shard_map/ppermute | solution.py:134
  20.7 1.8 %collective-permute-done.theirs = bf16[2,1408,128]{2,1,0:T(8,128)(2,1)S(1)} collective-permute-done((bf16[2,1408,128]{2,1,0:T(8,128)(2,1)S(1)}, bf16[2,1408,128]{2,1,0:T(8,128)(2,1)S(1)}, u32[]{:S(2)}, u32[]{:S(2)}) %collective-permute-start) | collective-permute-done | bytes 720928 | tf_op jit(solution)/shard_map/ppermute | solution.py:134
  22.5 1.0 shard_map.68
  23.4 33.8 %all_to_all.20.parts = bf16[8,4,2,96,128]{4,3,2,1,0:T(8,128)(2,1)S(1)} all-to-all(bf16[8,4,2,96,128]{4,3,2,1,0:T(8,128)(2,1)S(1)} %shard_map.68), channel_id=1, replica_groups={{0,128,256,384,512,640,768,896},{32,160,288,416,544,672,800,928},{64,19..., dimensions={0} | all-to-all | bytes 3145728 | tf_op jit(solution)/shard_map/all_to_all | solution.py:137
  57.3 0.2 shard_map.69
  57.5 19.9 %all_to_all.21.parts = bf16[4,4,2,96,128]{4,3,2,1,0:T(8,128)(2,1)S(1)} all-to-all(bf16[4,4,2,96,128]{4,3,2,1,0:T(8,128)(2,1)S(1)} %shard_map.69), channel_id=1, replica_groups={{0,32,64,96},{128,160,192,224},{256,288,320,352},{384,416,448,480},{512..., dimensions={0} | all-to-all | bytes 1572864 | tf_op jit(solution)/shard_map/all_to_all | solution.py:137
  77.4 0.2 shard_map.70
  77.6 0.0 copy-start.1
  77.7 32.2 %all_to_all.22.mine = bf16[8,4,2,96,128]{4,3,2,1,0:T(8,128)(2,1)S(1)} all-to-all(bf16[8,4,2,96,128]{4,3,2,1,0:T(8,128)(2,1)S(1)} %shard_map.70), channel_id=1, replica_groups={{0,128,256,384,512,640,768,896},{32,160,288,416,544,672,800,928},{64,19..., dimensions={0} | all-to-all | bytes 3145728 | tf_op jit(solution)/shard_map/all_to_all | solution.py:137
  109.9 2.0 %collective-permute-start.1 = (bf16[8,4,2,96,128]{4,3,2,1,0:T(8,128)(2,1)S(1)}, bf16[8,4,2,96,128]{4,3,2,1,0:T(8,128)(2,1)S(1)}, u32[]{:S(2)}, u32[]{:S(2)}) collective-permute-start(bf16[8,4,2,96,128]{4,3,2,1,0:T(8,128)(2,1)S(1)} %all_to_all.22.mine), channel_id=1, source_target_pairs={{0,16},{16,0},{32,48},{48,32},{64,80},{80,64},{96,112},{112,96},{1... | collective-permute-start | bytes 4718600 | tf_op jit(solution)/shard_map/ppermute | solution.py:134
  111.9 3.4 %collective-permute-done.1.theirs = bf16[8,4,2,96,128]{4,3,2,1,0:T(8,128)(2,1)S(1)} collective-permute-done((bf16[8,4,2,96,128]{4,3,2,1,0:T(8,128)(2,1)S(1)}, bf16[8,4,2,96,128]{4,3,2,1,0:T(8,128)(2,1)S(1)}, u32[]{:S(2)}, u32[]{:S(2)}) %collective-permute-start.1) | collective-permute-done | bytes 1572896 | tf_op jit(solution)/shard_map/ppermute | solution.py:134
  115.3 0.0 copy-done.1
  115.3 0.6 shard_map.71
  115.9 0.7 copy-done.7
  116.6 8.9 %all-to-all-start.3 = ((f32[16,24,128]{2,1,0:T(8,128)}), f32[16,24,128]{2,1,0:T(8,128)S(1)}, u32[]{:S(2)}, u32[]{:S(2)}) async-start(f32[16,24,128]{2,1,0:T(8,128)} %bitcast.1), calls=%async_computation.3 | async-start | bytes 393216 | tf_op jit(solution)/shard_map/all_to_all | solution.py:147
  125.5 2.3 %shard_map.73 = (f32[128,2048]{1,0:T(8,128)}, f32[2048,128]{1,0:T(8,128)}) custom-call(bf16[8,4,2,96,128]{4,3,2,1,0:T(8,128)(2,1)S(1)} %all_to_all.22.mine, bf16[8,4,2,96,128]{4,3,2,1,0:T(8,128)(2,1)S(1)} %collective-permute-done.1.theirs, bf16[384,128]{1,0:T(8,128)(2,1)S(1)} %copy-done.4, bf16[384,128]{1,0:T(8,128)(2,1)S(1)} %copy-done.6), custom_call_target="tpu_custom_call" | custom-call | tf_op jit(solution)/shard_map/pallas_call | solution.py:30
  127.8 7.6 %all-to-all-done.3.parts = f32[16,24,128]{2,1,0:T(8,128)S(1)} async-done(((f32[16,24,128]{2,1,0:T(8,128)}), f32[16,24,128]{2,1,0:T(8,128)S(1)}, u32[]{:S(2)}, u32[]{:S(2)}) %all-to-all-start.3) | async-done | bytes 196640 | tf_op jit(solution)/shard_map/all_to_all | solution.py:147
  135.4 0.6 shard_map.72
  (8 shorter events, 0.0 us)
Async XLA Ops:
  0.6 1.0 copy-start
  1.7 1.0 copy-start.2
  2.7 0.9 copy-start.3
  3.6 0.9 copy-start.5
  4.6 17.9 %collective-permute-start = (bf16[2,1408,128]{2,1,0:T(8,128)(2,1)S(1)}, bf16[2,1408,128]{2,1,0:T(8,128)(2,1)S(1)}, u32[]{:S(2)}, u32[]{:S(2)}) collective-permute-start(bf16[2,1408,128]{2,1,0:T(8,128)(2,1)S(1)} %shard_map.67), channel_id=1, source_target_pairs={{0,16},{16,0},{32,48},{48,32},{64,80},{80,64},{96,112},{112,96},{1... | collective-permute-start | bytes 2162696 | tf_op jit(solution)/shard_map/ppermute | solution.py:134
  77.6 37.7 %copy-start.1 = (bf16[128,2048]{1,0:T(8,128)(2,1)S(1)}, bf16[128,2048]{1,0:T(8,128)(2,1)}, u32[]{:S(2)}) copy-start(bf16[128,2048]{1,0:T(8,128)(2,1)} %w.1) | copy-start | bytes 1572868
  109.9 15.6 %copy-start.4 = (bf16[384,128]{1,0:T(8,128)(2,1)S(1)}, bf16[384,128]{1,0:T(8,128)(2,1)}, u32[]{:S(2)}) copy-start(bf16[384,128]{1,0:T(8,128)(2,1)} %x.5) | copy-start | bytes 294916
  109.9 15.6 %copy-start.6 = (bf16[384,128]{1,0:T(8,128)(2,1)S(1)}, bf16[384,128]{1,0:T(8,128)(2,1)}, u32[]{:S(2)}) copy-start(bf16[384,128]{1,0:T(8,128)(2,1)} %y.5) | copy-start | bytes 294916
  109.9 5.4 %collective-permute-start.1 = (bf16[8,4,2,96,128]{4,3,2,1,0:T(8,128)(2,1)S(1)}, bf16[8,4,2,96,128]{4,3,2,1,0:T(8,128)(2,1)S(1)}, u32[]{:S(2)}, u32[]{:S(2)}) collective-permute-start(bf16[8,4,2,96,128]{4,3,2,1,0:T(8,128)(2,1)S(1)} %all_to_all.22.mine), channel_id=1, source_target_pairs={{0,16},{16,0},{32,48},{48,32},{64,80},{80,64},{96,112},{112,96},{1... | collective-permute-start | bytes 4718600 | tf_op jit(solution)/shard_map/ppermute | solution.py:134
  115.9 0.7 copy-start.7
  116.6 18.8 %all-to-all-start.3 = ((f32[16,24,128]{2,1,0:T(8,128)}), f32[16,24,128]{2,1,0:T(8,128)S(1)}, u32[]{:S(2)}, u32[]{:S(2)}) async-start(f32[16,24,128]{2,1,0:T(8,128)} %bitcast.1), calls=%async_computation.3 | async-start | bytes 393216 | tf_op jit(solution)/shard_map/all_to_all | solution.py:147

commit v5 on v4

v5 whole, which is shorter than its diff:
```python
import jax
import jax.numpy as jnp
import numpy as np
from jax import lax
from jax.experimental import pallas as pl
from jax.experimental.pallas import tpu as pltpu
from jax.sharding import PartitionSpec as P

F32, BF16 = jnp.float32, jnp.bfloat16
PARAMS = pltpu.CompilerParams(vmem_limit_bytes=40 * 1024 * 1024)
T, B = 384, 128
X, Z, C = 8, 4, 2
Q = T // Z

at = lambda x, z, c: (x * Z + z) * C + c
EIGHTS = [[at(x, z, 0) for x in range(X)] for z in range(Z)]
EIGHTS += [[at(2 * a + b, z, 1) for b in range(2) for z in range(Z)] for a in range(4)]
FOURS = [[at(x, z, 0) for z in range(Z)] for x in range(X)]
FOURS += [[at(2 * a + b, z, 1) for a in range(4)] for b in range(2) for z in range(Z)]
ROUND = [[(g[i], g[(i + s) % 4]) for g in FOURS for i in range(4)] for s in (1, 3, 2)]
SWAP = [(i, i ^ 1) for i in range(X * Z * C)]


def place(core, x, z):
    first = core == 0
    return jnp.where(first, x, x % 2 * Z + z), jnp.where(first, z, x // 2)


def call(body, outs, *operands, unread=0, where=pltpu.VMEM, scratch=()):
    vmem, stay = (pl.BlockSpec(memory_space=m) for m in (pltpu.VMEM, pl.ANY))
    read = pl.BlockSpec(memory_space=where)
    return pl.pallas_call(
        body,
        out_shape=outs,
        in_specs=[read] * (len(operands) - unread) + [stay] * unread,
        out_specs=jax.tree.map(lambda _: vmem, outs),
        scratch_shapes=scratch,
        compiler_params=PARAMS,
    )(*operands)


def this_core():
    return lax.rem(lax.axis_index("gx"), C)


def columns(core, x):
    return pl.ds(pl.multiple_of((core * X + x) * B, B), B)


def dot(a, b, dims):
    return lax.dot_general(a, b, (dims, ((), ())), preferred_element_type=F32)


def rows(x):
    return pl.ds(T + x * B, B)


def pack_in(x, w, out, sem):
    other = 1 - this_core()
    pairs = [(x, out.at[pl.ds(0, T)])]
    pairs += [(w.at[:, columns(other, j)], out.at[rows(j)]) for j in range(X)]
    move(pairs, sem)


def pack_out(x, w, out, sem):
    start = pl.multiple_of((1 - this_core()) * (X * B), B)
    pairs = [(x, out.at[pl.ds(0, T)])]
    pairs += [(w.at[pl.ds(start, X * B)], out.at[pl.ds(T, X * B)])]
    move(pairs, sem)


def move(pairs, sem):
    copies = [pltpu.make_async_copy(a, b, sem.at[i]) for i, (a, b) in enumerate(pairs)]
    for copy in copies:
        copy.start()
    for copy in copies:
        copy.wait()


def scatter(value, out, core, x):
    value = value.astype(BF16)
    for z in range(Z):
        eight, four = place(core, x, z)
        out[eight, four] = value[z * Q : (z + 1) * Q]


def hidden_part(x, w, theirs, out):
    core = this_core()
    for j in range(X):
        value = dot(x[...], w[:, columns(core, j)], ((1,), (0,)))
        value += dot(theirs[:T], theirs[rows(j)], ((1,), (0,)))
        scatter(value, out, core, j)


def grad_part(x, w, theirs, out):
    core = this_core()
    for j in range(X):
        value = dot(x[...], w[columns(core, j), :], ((1,), (1,)))
        value += dot(theirs[:T], theirs[rows(j)], ((1,), (1,)))
        scatter(value, out, core, j)


def total(parts):
    value = parts[0].astype(F32)
    for j in range(1, parts.shape[0]):
        value = value + parts[j].astype(F32)
    return value


def add_eight(parts, out, rounded):
    value = total(parts)
    out[...] = value
    rounded[...] = value.astype(BF16)


def add_four(own, others):
    value = own[...]
    for other in others:
        value = value + other[...].astype(F32)
    return value


def activate(own, p1, p2, p3, act, slope):
    v = add_four(own, (p1, p2, p3))
    k = np.float32(np.sqrt(2 / np.pi))
    cube = np.float32(0.044715)
    t = jnp.tanh(k * (v + cube * (v * v * v)))
    a = (0.5 * v * (1.0 + t)).astype(BF16)
    slope[...] = 0.5 * (1.0 + t) + 0.5 * v * (1.0 - t * t) * (
        k * (1.0 + 3.0 * cube * (v * v))
    )
    for j in range(8):
        act[j] = a


def back(own, p1, p2, p3, slope, after, out):
    p = (add_four(own, (p1, p2, p3)) * slope[...]).astype(BF16)
    for j in range(8):
        out[j] = p


def tokens(ref, core, x):
    return jnp.concatenate([ref[place(core, x, z)] for z in range(Z)], axis=0)


def weight_out(mine, theirs, x, out):
    core = this_core()
    for who, ref in ((core, mine), (1 - core, theirs)):
        for j in range(X):
            out[columns(who, j), :] = dot(tokens(ref, who, j), x[...], ((0,), (0,)))


def weight_in(mine, theirs, x, out):
    core = this_core()
    for who, ref in ((core, mine), (1 - core, theirs)):
        for j in range(X):
            out[:, columns(who, j)] = dot(x[...], tokens(ref, who, j), ((0,), (0,)))


def input_part(mine, theirs, w, out):
    core = this_core()
    value = jnp.zeros((T, B), F32)
    for who, ref in ((core, mine), (1 - core, theirs)):
        for j in range(X):
            value += dot(tokens(ref, who, j), w[:, columns(who, j)], ((1,), (1,)))
    out[...] = value


def finish(parts, out):
    out[...] = total(parts).astype(BF16)


def per_device(inputs, grad_out, w_in, w_out):
    s = jax.ShapeDtypeStruct
    four = (4, Q, B)
    eight = s((8, *four), BF16)
    packed = s((T + X * B, B), BF16)
    summed = (s(four, F32), s(four, BF16))
    swap = lambda v: lax.ppermute(v, "gx", SWAP)

    def exchange(v):
        return lax.all_to_all(v, "gx", 0, 0, axis_index_groups=EIGHTS, tiled=True)

    def around(own, rounded):
        return own, *(lax.ppermute(rounded, "gx", pairs) for pairs in ROUND)

    def packs(body, copies, x, w):
        sems = (pltpu.SemaphoreType.DMA((copies,)),)
        return swap(call(body, packed, x, w, where=pltpu.HBM, scratch=sems))

    theirs_in = packs(pack_in, 1 + X, inputs, w_in)
    theirs_out = packs(pack_out, 2, grad_out, w_out)
    hidden = exchange(call(hidden_part, eight, inputs, w_in, theirs_in))
    grad = exchange(call(grad_part, eight, grad_out, w_out, theirs_out))
    hidden = around(*call(add_eight, summed, hidden))
    act, slope = call(activate, (eight, s(four, F32)), *hidden)
    act = exchange(act)
    grad = around(*call(add_eight, summed, grad))
    pre = exchange(call(back, eight, *grad, slope, act, unread=1))
    act_theirs = swap(act)
    grad_w_out = call(weight_out, s((2 * X * B, B), F32), act, act_theirs, grad_out)
    pre_theirs = swap(pre)
    part = call(input_part, s((T, B), F32), pre, pre_theirs, w_in)
    part = lax.all_to_all(part.reshape(16, T // 16, B), "gy", 0, 0, tiled=True)
    grad_w_in = call(weight_in, s((B, 2 * X * B), F32), pre, pre_theirs, inputs)
    grad_inputs = call(finish, s((T // 16, B), BF16), part)
    return (grad_inputs, grad_w_in, grad_w_out)


def solution(mesh):
    return jax.shard_map(
        per_device,
        mesh=mesh,
        in_specs=(P(None, "gx"), P(None, "gx"), P("gx", "gy"), P("gy", "gx")),
        out_specs=(P("gy", "gx"), P("gx", "gy"), P("gy", "gx")),
        check_vma=False,
    )
```

time: 137 us -> 144 us (1.051)
  blocking collectives: 86 us -> 22.1 us
  starting transfers between devices: 27 us -> 74.3 us
  waiting for transfers between devices: 12.8 us -> 34.3 us
  Pallas kernels: 5.02 us -> 9.74 us
  local copies, waits for them, and re-layouts: 4.55 us -> 1.95 us
    all_to_all x3 -> x1, blocking collectives: 86 us -> 22.1 us  [exchange(): return lax.all_to_all(v, 'gx', 0, 0, axis_index_groups=EIGHTS, tiled=True)]
    ppermute x0 -> x6, starting transfers between devices: none -> 23.4 us  [around(): return (own, *(lax.ppermute(rounded, 'gx', pairs) for pairs in ROUND))]
    all_to_all x0 -> x3, starting transfers between devices: none -> 18.3 us  [exchange(): return lax.all_to_all(v, 'gx', 0, 0, axis_index_groups=EIGHTS, tiled=True)]
    ppermute x0 -> x6, waiting for transfers between devices: none -> 14.8 us  [around(): return (own, *(lax.ppermute(rounded, 'gx', pairs) for pairs in ROUND))]
    all_to_all x0 -> x3, waiting for transfers between devices: none -> 10.2 us  [exchange(): return lax.all_to_all(v, 'gx', 0, 0, axis_index_groups=EIGHTS, tiled=True)]
    ppermute x2 -> x4, starting transfers between devices: 18.1 us -> 22.9 us  [per_device(): swap = lambda v: lax.ppermute(v, 'gx', SWAP)]
    pallas_call x7 -> x12, Pallas kernels: 5.02 us -> 9.74 us  [call(): pl.pallas_call(body, out_shape=outs, in_specs=[read] * (len(operands) - u...]
    unnamed x16 -> x12, local copies, waits for them, and re-layouts: 4.55 us -> 1.95 us
  transfers between devices with their start and end apart: 3 -> 14, of which waited for: 3 -> 8; matrix products, arithmetic and copies ran while one was open for 0% -> 0% of each run, Pallas kernels for 2% -> 5%
where the time goes in v5:
time: 144 us; the launch traced here: 143 us
  starting transfers between devices  74.3 us (52%)
  waiting for transfers between devices  34.3 us (24%)
  blocking collectives  22.1 us (15%)
  Pallas kernels  9.74 us (7%)
  local copies, waits for them, and re-layouts  1.95 us (1%)
    ppermute x6, starting transfers between devices, around(): return (own, *(lax.ppermute(rounded, 'gx', pairs) for pairs in ROUND))  23.4 us
    ppermute x4, starting transfers between devices, per_device(): swap = lambda v: lax.ppermute(v, 'gx', SWAP)  22.9 us
    all_to_all x1, blocking collectives, exchange(): return lax.all_to_all(v, 'gx', 0, 0, axis_index_groups=EIGHTS, tiled=True)  22.1 us
    all_to_all x3, starting transfers between devices, exchange(): return lax.all_to_all(v, 'gx', 0, 0, axis_index_groups=EIGHTS, tiled=True)  18.3 us
    ppermute x6, waiting for transfers between devices, around(): return (own, *(lax.ppermute(rounded, 'gx', pairs) for pairs in ROUND))  14.8 us
    all_to_all x3, waiting for transfers between devices, exchange(): return lax.all_to_all(v, 'gx', 0, 0, axis_index_groups=EIGHTS, tiled=True)  10.2 us
    all_to_all x1, starting transfers between devices, per_device(): part = lax.all_to_all(part.reshape(16, T // 16, B), 'gy', 0, 0, tiled=True)  9.8 us
    pallas_call x12, Pallas kernels, call(): pl.pallas_call(body, out_shape=outs, in_specs=[read] * (len(operands) - u...  9.74 us
  transfers between devices with their start and end apart: 14, of which 8 were waited for; matrix products, arithmetic and copies ran while one was open for 0% of the time, Pallas kernels for 5%

profile of v5, /device:TPU:1, one launch (start us, length us, event | category | flops | bytes accessed | tf_op | source)
XLA Modules:
  0.0 143.2 jit_solution(2237999794288362801)
XLA Ops:
  2.8 16.1 %collective-permute-start.4 = (bf16[1408,128]{1,0:T(8,128)(2,1)S(1)}, bf16[1408,128]{1,0:T(8,128)(2,1)S(1)}, u32[]{:S(2)}, u32[]{:S(2)}) collective-permute-start(bf16[1408,128]{1,0:T(8,128)(2,1)S(1)} %shard_map.70), channel_id=1, source_target_pairs={{0,16},{16,0},{32,48},{48,32},{64,80},{80,64},{96,112},{112,96},{1... | collective-permute-start | bytes 1081352 | tf_op jit(solution)/shard_map/ppermute | solution.py:179
  21.6 3.9 %all-to-all-start.1 = ((bf16[8,4,96,128]{3,2,1,0:T(8,128)(2,1)}), bf16[8,4,96,128]{3,2,1,0:T(8,128)(2,1)S(1)}, u32[]{:S(2)}, u32[]{:S(2)}) async-start(bf16[8,4,96,128]{3,2,1,0:T(8,128)(2,1)} %shard_map.71), calls=%async_computation.1 | async-start | bytes 1572864 | tf_op jit(solution)/shard_map/all_to_all | solution.py:182
  25.7 2.1 %collective-permute-start = (bf16[1408,128]{1,0:T(8,128)(2,1)S(1)}, bf16[1408,128]{1,0:T(8,128)(2,1)S(1)}, u32[]{:S(2)}, u32[]{:S(2)}) collective-permute-start(bf16[1408,128]{1,0:T(8,128)(2,1)S(1)} %shard_map.67), channel_id=1, source_target_pairs={{0,16},{16,0},{32,48},{48,32},{64,80},{80,64},{96,112},{112,96},{1... | collective-permute-start | bytes 1081352 | tf_op jit(solution)/shard_map/ppermute | solution.py:179
  27.8 1.5 %collective-permute-done.theirs = bf16[1408,128]{1,0:T(8,128)(2,1)S(1)} collective-permute-done((bf16[1408,128]{1,0:T(8,128)(2,1)S(1)}, bf16[1408,128]{1,0:T(8,128)(2,1)S(1)}, u32[]{:S(2)}, u32[]{:S(2)}) %collective-permute-start) | collective-permute-done | bytes 360480 | tf_op jit(solution)/shard_map/ppermute | solution.py:179
  30.8 10.2 %all-to-all-done.1.parts = bf16[8,4,96,128]{3,2,1,0:T(8,128)(2,1)S(1)} async-done(((bf16[8,4,96,128]{3,2,1,0:T(8,128)(2,1)}), bf16[8,4,96,128]{3,2,1,0:T(8,128)(2,1)S(1)}, u32[]{:S(2)}, u32[]{:S(2)}) %all-to-all-start.1) | async-done | bytes 786464 | tf_op jit(solution)/shard_map/all_to_all | solution.py:182
  41.0 4.7 %all-to-all-start = ((bf16[8,4,96,128]{3,2,1,0:T(8,128)(2,1)}), bf16[8,4,96,128]{3,2,1,0:T(8,128)(2,1)S(1)}, u32[]{:S(2)}, u32[]{:S(2)}) async-start(bf16[8,4,96,128]{3,2,1,0:T(8,128)(2,1)} %shard_map.68), calls=%async_computation | async-start | bytes 1572864 | tf_op jit(solution)/shard_map/all_to_all | solution.py:182
  45.7 7.0 %collective-permute-start.7 = (bf16[4,96,128]{2,1,0:T(8,128)(2,1)S(1)}, bf16[4,96,128]{2,1,0:T(8,128)(2,1)S(1)}, u32[]{:S(2)}, u32[]{:S(2)}) collective-permute-start(bf16[4,96,128]{2,1,0:T(8,128)(2,1)S(1)} %get-tuple-element.12), channel_id=1, source_target_pairs={{0,64},{32,96},{64,0},{96,32},{128,192},{160,224},{192,128},{224,1... | collective-permute-start | bytes 294920 | tf_op jit(solution)/shard_map/ppermute | solution.py:185
  52.7 2.2 %collective-permute-start.6 = (bf16[4,96,128]{2,1,0:T(8,128)(2,1)S(1)}, bf16[4,96,128]{2,1,0:T(8,128)(2,1)S(1)}, u32[]{:S(2)}, u32[]{:S(2)}) collective-permute-start(bf16[4,96,128]{2,1,0:T(8,128)(2,1)S(1)} %get-tuple-element.12), channel_id=1, source_target_pairs={{0,96},{32,0},{64,32},{96,64},{128,224},{160,128},{192,160},{224,1... | collective-permute-start | bytes 294920 | tf_op jit(solution)/shard_map/ppermute | solution.py:185
  55.0 4.0 %collective-permute-start.5 = (bf16[4,96,128]{2,1,0:T(8,128)(2,1)S(1)}, bf16[4,96,128]{2,1,0:T(8,128)(2,1)S(1)}, u32[]{:S(2)}, u32[]{:S(2)}) collective-permute-start(bf16[4,96,128]{2,1,0:T(8,128)(2,1)S(1)} %get-tuple-element.12), channel_id=1, source_target_pairs={{0,32},{32,64},{64,96},{96,0},{128,160},{160,192},{192,224},{224,1... | collective-permute-start | bytes 294920 | tf_op jit(solution)/shard_map/ppermute | solution.py:185
  58.9 5.1 %collective-permute-done.7.p3 = bf16[4,96,128]{2,1,0:T(8,128)(2,1)S(1)} collective-permute-done((bf16[4,96,128]{2,1,0:T(8,128)(2,1)S(1)}, bf16[4,96,128]{2,1,0:T(8,128)(2,1)S(1)}, u32[]{:S(2)}, u32[]{:S(2)}) %collective-permute-start.7) | collective-permute-done | bytes 98336 | tf_op jit(solution)/shard_map/ppermute | solution.py:185
  64.1 1.6 %collective-permute-done.5.p1 = bf16[4,96,128]{2,1,0:T(8,128)(2,1)S(1)} collective-permute-done((bf16[4,96,128]{2,1,0:T(8,128)(2,1)S(1)}, bf16[4,96,128]{2,1,0:T(8,128)(2,1)S(1)}, u32[]{:S(2)}, u32[]{:S(2)}) %collective-permute-start.5) | collective-permute-done | bytes 98336 | tf_op jit(solution)/shard_map/ppermute | solution.py:185
  66.7 9.7 %all-to-all-start.2 = ((bf16[8,4,96,128]{3,2,1,0:T(8,128)(2,1)}), bf16[8,4,96,128]{3,2,1,0:T(8,128)(2,1)S(1)}, u32[]{:S(2)}, u32[]{:S(2)}) async-start(bf16[8,4,96,128]{3,2,1,0:T(8,128)(2,1)} %get-tuple-element.14), calls=%async_computation.2 | async-start | bytes 1572864 | tf_op jit(solution)/shard_map/all_to_all | solution.py:182
  76.6 2.4 %collective-permute-start.3 = (bf16[4,96,128]{2,1,0:T(8,128)(2,1)S(1)}, bf16[4,96,128]{2,1,0:T(8,128)(2,1)S(1)}, u32[]{:S(2)}, u32[]{:S(2)}) collective-permute-start(bf16[4,96,128]{2,1,0:T(8,128)(2,1)S(1)} %get-tuple-element.10), channel_id=1, source_target_pairs={{0,64},{32,96},{64,0},{96,32},{128,192},{160,224},{192,128},{224,1... | collective-permute-start | bytes 294920 | tf_op jit(solution)/shard_map/ppermute | solution.py:185
  79.0 5.9 %collective-permute-start.2 = (bf16[4,96,128]{2,1,0:T(8,128)(2,1)S(1)}, bf16[4,96,128]{2,1,0:T(8,128)(2,1)S(1)}, u32[]{:S(2)}, u32[]{:S(2)}) collective-permute-start(bf16[4,96,128]{2,1,0:T(8,128)(2,1)S(1)} %get-tuple-element.10), channel_id=1, source_target_pairs={{0,96},{32,0},{64,32},{96,64},{128,224},{160,128},{192,160},{224,1... | collective-permute-start | bytes 294920 | tf_op jit(solution)/shard_map/ppermute | solution.py:185
  84.9 1.9 %collective-permute-start.1 = (bf16[4,96,128]{2,1,0:T(8,128)(2,1)S(1)}, bf16[4,96,128]{2,1,0:T(8,128)(2,1)S(1)}, u32[]{:S(2)}, u32[]{:S(2)}) collective-permute-start(bf16[4,96,128]{2,1,0:T(8,128)(2,1)S(1)} %get-tuple-element.10), channel_id=1, source_target_pairs={{0,32},{32,64},{64,96},{96,0},{128,160},{160,192},{192,224},{224,1... | collective-permute-start | bytes 294920 | tf_op jit(solution)/shard_map/ppermute | solution.py:185
  86.8 2.7 %collective-permute-done.3.p3 = bf16[4,96,128]{2,1,0:T(8,128)(2,1)S(1)} collective-permute-done((bf16[4,96,128]{2,1,0:T(8,128)(2,1)S(1)}, bf16[4,96,128]{2,1,0:T(8,128)(2,1)S(1)}, u32[]{:S(2)}, u32[]{:S(2)}) %collective-permute-start.3) | collective-permute-done | bytes 98336 | tf_op jit(solution)/shard_map/ppermute | solution.py:185
  89.5 5.3 %collective-permute-done.1.p1 = bf16[4,96,128]{2,1,0:T(8,128)(2,1)S(1)} collective-permute-done((bf16[4,96,128]{2,1,0:T(8,128)(2,1)S(1)}, bf16[4,96,128]{2,1,0:T(8,128)(2,1)S(1)}, u32[]{:S(2)}, u32[]{:S(2)}) %collective-permute-start.1) | collective-permute-done | bytes 98336 | tf_op jit(solution)/shard_map/ppermute | solution.py:185
  94.9 22.1 %all_to_all.25.mine = bf16[8,4,96,128]{3,2,1,0:T(8,128)(2,1)S(1)} all-to-all(bf16[8,4,96,128]{3,2,1,0:T(8,128)(2,1)S(1)} %shard_map.74), channel_id=1, replica_groups={{0,128,256,384,512,640,768,896},{32,160,288,416,544,672,800,928},{64,19..., dimensions={0} | all-to-all | bytes 1572864 | tf_op jit(solution)/shard_map/all_to_all | solution.py:182
  117.0 2.8 %collective-permute-start.8 = (bf16[8,4,96,128]{3,2,1,0:T(8,128)(2,1)S(1)}, bf16[8,4,96,128]{3,2,1,0:T(8,128)(2,1)S(1)}, u32[]{:S(2)}, u32[]{:S(2)}) collective-permute-start(bf16[8,4,96,128]{3,2,1,0:T(8,128)(2,1)S(1)} %all_to_all.25.mine), channel_id=1, source_target_pairs={{0,16},{16,0},{32,48},{48,32},{64,80},{80,64},{96,112},{112,96},{1... | collective-permute-start | bytes 2359304 | tf_op jit(solution)/shard_map/ppermute | solution.py:179
  119.8 1.9 %collective-permute-start.9 = (bf16[8,4,96,128]{3,2,1,0:T(8,128)(2,1)S(1)}, bf16[8,4,96,128]{3,2,1,0:T(8,128)(2,1)S(1)}, u32[]{:S(2)}, u32[]{:S(2)}) collective-permute-start(bf16[8,4,96,128]{3,2,1,0:T(8,128)(2,1)S(1)} %all-to-all-done.2.after.mine), channel_id=1, source_target_pairs={{0,16},{16,0},{32,48},{48,32},{64,80},{80,64},{96,112},{112,96},{1... | collective-permute-start | bytes 2359304 | tf_op jit(solution)/shard_map/ppermute | solution.py:179
  123.0 9.8 %all-to-all-start.4 = ((f32[16,24,128]{2,1,0:T(8,128)}), f32[16,24,128]{2,1,0:T(8,128)S(1)}, u32[]{:S(2)}, u32[]{:S(2)}) async-start(f32[16,24,128]{2,1,0:T(8,128)} %bitcast), calls=%async_computation.4 | async-start | bytes 393216 | tf_op jit(solution)/shard_map/all_to_all | solution.py:204
  132.8 1.6 %shard_map.78 = f32[2048,128]{1,0:T(8,128)} custom-call(bf16[8,4,96,128]{3,2,1,0:T(8,128)(2,1)S(1)} %all-to-all-done.2.after.mine, bf16[8,4,96,128]{3,2,1,0:T(8,128)(2,1)S(1)} %collective-permute-done.9.theirs, bf16[384,128]{1,0:T(8,128)(2,1)S(1)} %copy-done.3), custom_call_target="tpu_custom_call" | custom-call | tf_op jit(solution)/shard_map/pallas_call | solution.py:32
  134.4 1.6 %shard_map.77 = f32[128,2048]{1,0:T(8,128)} custom-call(bf16[8,4,96,128]{3,2,1,0:T(8,128)(2,1)S(1)} %all_to_all.25.mine, bf16[8,4,96,128]{3,2,1,0:T(8,128)(2,1)S(1)} %collective-permute-done.8.theirs, bf16[384,128]{1,0:T(8,128)(2,1)S(1)} %copy-done.5), custom_call_target="tpu_custom_call" | custom-call | tf_op jit(solution)/shard_map/pallas_call | solution.py:32
  136.0 6.6 %all-to-all-done.4.parts = f32[16,24,128]{2,1,0:T(8,128)S(1)} async-done(((f32[16,24,128]{2,1,0:T(8,128)}), f32[16,24,128]{2,1,0:T(8,128)S(1)}, u32[]{:S(2)}, u32[]{:S(2)}) %all-to-all-start.4) | async-done | bytes 196640 | tf_op jit(solution)/shard_map/all_to_all | solution.py:204
  (29 shorter events, 9.8 us)
Async XLA Ops:
  0.6 1.0 copy-start
  1.7 0.9 copy-start.4
  2.8 17.4 %collective-permute-start.4 = (bf16[1408,128]{1,0:T(8,128)(2,1)S(1)}, bf16[1408,128]{1,0:T(8,128)(2,1)S(1)}, u32[]{:S(2)}, u32[]{:S(2)}) collective-permute-start(bf16[1408,128]{1,0:T(8,128)(2,1)S(1)} %shard_map.70), channel_id=1, source_target_pairs={{0,16},{16,0},{32,48},{48,32},{64,80},{80,64},{96,112},{112,96},{1... | collective-permute-start | bytes 1081352 | tf_op jit(solution)/shard_map/ppermute | solution.py:179
  21.6 3.9 %copy-start.2 = (bf16[2048,128]{1,0:T(8,128)(2,1)S(1)}, bf16[2048,128]{1,0:T(8,128)(2,1)}, u32[]{:S(2)}) copy-start(bf16[2048,128]{1,0:T(8,128)(2,1)} %w.6) | copy-start | bytes 1572868
  21.6 3.9 %copy-start.3 = (bf16[384,128]{1,0:T(8,128)(2,1)S(1)}, bf16[384,128]{1,0:T(8,128)(2,1)}, u32[]{:S(2)}) copy-start(bf16[384,128]{1,0:T(8,128)(2,1)} %x.11) | copy-start | bytes 294916
  21.6 19.3 %all-to-all-start.1 = ((bf16[8,4,96,128]{3,2,1,0:T(8,128)(2,1)}), bf16[8,4,96,128]{3,2,1,0:T(8,128)(2,1)S(1)}, u32[]{:S(2)}, u32[]{:S(2)}) async-start(bf16[8,4,96,128]{3,2,1,0:T(8,128)(2,1)} %shard_map.71), calls=%async_computation.1 | async-start | bytes 1572864 | tf_op jit(solution)/shard_map/all_to_all | solution.py:182
  25.7 3.6 %collective-permute-start = (bf16[1408,128]{1,0:T(8,128)(2,1)S(1)}, bf16[1408,128]{1,0:T(8,128)(2,1)S(1)}, u32[]{:S(2)}, u32[]{:S(2)}) collective-permute-start(bf16[1408,128]{1,0:T(8,128)(2,1)S(1)} %shard_map.67), channel_id=1, source_target_pairs={{0,16},{16,0},{32,48},{48,32},{64,80},{80,64},{96,112},{112,96},{1... | collective-permute-start | bytes 1081352 | tf_op jit(solution)/shard_map/ppermute | solution.py:179
  41.0 25.7 %all-to-all-start = ((bf16[8,4,96,128]{3,2,1,0:T(8,128)(2,1)}), bf16[8,4,96,128]{3,2,1,0:T(8,128)(2,1)S(1)}, u32[]{:S(2)}, u32[]{:S(2)}) async-start(bf16[8,4,96,128]{3,2,1,0:T(8,128)(2,1)} %shard_map.68), calls=%async_computation | async-start | bytes 1572864 | tf_op jit(solution)/shard_map/all_to_all | solution.py:182
  45.7 18.3 %collective-permute-start.7 = (bf16[4,96,128]{2,1,0:T(8,128)(2,1)S(1)}, bf16[4,96,128]{2,1,0:T(8,128)(2,1)S(1)}, u32[]{:S(2)}, u32[]{:S(2)}) collective-permute-start(bf16[4,96,128]{2,1,0:T(8,128)(2,1)S(1)} %get-tuple-element.12), channel_id=1, source_target_pairs={{0,64},{32,96},{64,0},{96,32},{128,192},{160,224},{192,128},{224,1... | collective-permute-start | bytes 294920 | tf_op jit(solution)/shard_map/ppermute | solution.py:185
  52.7 11.3 %collective-permute-start.6 = (bf16[4,96,128]{2,1,0:T(8,128)(2,1)S(1)}, bf16[4,96,128]{2,1,0:T(8,128)(2,1)S(1)}, u32[]{:S(2)}, u32[]{:S(2)}) collective-permute-start(bf16[4,96,128]{2,1,0:T(8,128)(2,1)S(1)} %get-tuple-element.12), channel_id=1, source_target_pairs={{0,96},{32,0},{64,32},{96,64},{128,224},{160,128},{192,160},{224,1... | collective-permute-start | bytes 294920 | tf_op jit(solution)/shard_map/ppermute | solution.py:185
  55.0 10.7 %collective-permute-start.5 = (bf16[4,96,128]{2,1,0:T(8,128)(2,1)S(1)}, bf16[4,96,128]{2,1,0:T(8,128)(2,1)S(1)}, u32[]{:S(2)}, u32[]{:S(2)}) collective-permute-start(bf16[4,96,128]{2,1,0:T(8,128)(2,1)S(1)} %get-tuple-element.12), channel_id=1, source_target_pairs={{0,32},{32,64},{64,96},{96,0},{128,160},{160,192},{192,224},{224,1... | collective-permute-start | bytes 294920 | tf_op jit(solution)/shard_map/ppermute | solution.py:185
  66.7 28.1 %all-to-all-start.2 = ((bf16[8,4,96,128]{3,2,1,0:T(8,128)(2,1)}), bf16[8,4,96,128]{3,2,1,0:T(8,128)(2,1)S(1)}, u32[]{:S(2)}, u32[]{:S(2)}) async-start(bf16[8,4,96,128]{3,2,1,0:T(8,128)(2,1)} %get-tuple-element.14), calls=%async_computation.2 | async-start | bytes 1572864 | tf_op jit(solution)/shard_map/all_to_all | solution.py:182
  76.6 12.9 %collective-permute-start.3 = (bf16[4,96,128]{2,1,0:T(8,128)(2,1)S(1)}, bf16[4,96,128]{2,1,0:T(8,128)(2,1)S(1)}, u32[]{:S(2)}, u32[]{:S(2)}) collective-permute-start(bf16[4,96,128]{2,1,0:T(8,128)(2,1)S(1)} %get-tuple-element.10), channel_id=1, source_target_pairs={{0,64},{32,96},{64,0},{96,32},{128,192},{160,224},{192,128},{224,1... | collective-permute-start | bytes 294920 | tf_op jit(solution)/shard_map/ppermute | solution.py:185
  79.0 10.5 %collective-permute-start.2 = (bf16[4,96,128]{2,1,0:T(8,128)(2,1)S(1)}, bf16[4,96,128]{2,1,0:T(8,128)(2,1)S(1)}, u32[]{:S(2)}, u32[]{:S(2)}) collective-permute-start(bf16[4,96,128]{2,1,0:T(8,128)(2,1)S(1)} %get-tuple-element.10), channel_id=1, source_target_pairs={{0,96},{32,0},{64,32},{96,64},{128,224},{160,128},{192,160},{224,1... | collective-permute-start | bytes 294920 | tf_op jit(solution)/shard_map/ppermute | solution.py:185
  84.9 9.9 %collective-permute-start.1 = (bf16[4,96,128]{2,1,0:T(8,128)(2,1)S(1)}, bf16[4,96,128]{2,1,0:T(8,128)(2,1)S(1)}, u32[]{:S(2)}, u32[]{:S(2)}) collective-permute-start(bf16[4,96,128]{2,1,0:T(8,128)(2,1)S(1)} %get-tuple-element.10), channel_id=1, source_target_pairs={{0,32},{32,64},{64,96},{96,0},{128,160},{160,192},{192,224},{224,1... | collective-permute-start | bytes 294920 | tf_op jit(solution)/shard_map/ppermute | solution.py:185
  94.9 26.9 %copy-start.1 = (bf16[128,2048]{1,0:T(8,128)(2,1)S(1)}, bf16[128,2048]{1,0:T(8,128)(2,1)}, u32[]{:S(2)}) copy-start(bf16[128,2048]{1,0:T(8,128)(2,1)} %w.9) | copy-start | bytes 1572868
  117.0 4.7 %collective-permute-start.8 = (bf16[8,4,96,128]{3,2,1,0:T(8,128)(2,1)S(1)}, bf16[8,4,96,128]{3,2,1,0:T(8,128)(2,1)S(1)}, u32[]{:S(2)}, u32[]{:S(2)}) collective-permute-start(bf16[8,4,96,128]{3,2,1,0:T(8,128)(2,1)S(1)} %all_to_all.25.mine), channel_id=1, source_target_pairs={{0,16},{16,0},{32,48},{48,32},{64,80},{80,64},{96,112},{112,96},{1... | collective-permute-start | bytes 2359304 | tf_op jit(solution)/shard_map/ppermute | solution.py:179
  119.8 13.0 %collective-permute-start.9 = (bf16[8,4,96,128]{3,2,1,0:T(8,128)(2,1)S(1)}, bf16[8,4,96,128]{3,2,1,0:T(8,128)(2,1)S(1)}, u32[]{:S(2)}, u32[]{:S(2)}) collective-permute-start(bf16[8,4,96,128]{3,2,1,0:T(8,128)(2,1)S(1)} %all-to-all-done.2.after.mine), channel_id=1, source_target_pairs={{0,16},{16,0},{32,48},{48,32},{64,80},{80,64},{96,112},{112,96},{1... | collective-permute-start | bytes 2359304 | tf_op jit(solution)/shard_map/ppermute | solution.py:179
  123.0 19.6 %all-to-all-start.4 = ((f32[16,24,128]{2,1,0:T(8,128)}), f32[16,24,128]{2,1,0:T(8,128)S(1)}, u32[]{:S(2)}, u32[]{:S(2)}) async-start(f32[16,24,128]{2,1,0:T(8,128)} %bitcast), calls=%async_computation.4 | async-start | bytes 393216 | tf_op jit(solution)/shard_map/all_to_all | solution.py:204
  132.8 1.6 %copy-start.5 = (bf16[384,128]{1,0:T(8,128)(2,1)S(1)}, bf16[384,128]{1,0:T(8,128)(2,1)}, u32[]{:S(2)}) copy-start(bf16[384,128]{1,0:T(8,128)(2,1)} %x.10) | copy-start | bytes 294916

commit v6 on v3

--- a/solution.py
+++ b/solution.py
@@ -13,26 +13,28 @@
 Q = T // Z
 
 at = lambda x, z, c: (x * Z + z) * C + c
-FOURS = [[at(2 * a + b, z, 0) for a in range(4)] for b in range(2) for z in range(Z)]
+fold = lambda a, b: a if b == 0 else X - 1 - a
+FOURS = [[at(fold(a, b), z, 0) for a in range(4)] for b in range(2) for z in range(Z)]
 FOURS += [[at(x, z, 1) for z in range(Z)] for x in range(X)]
-EIGHTS = [[at(2 * a + b, z, 0) for b in range(2) for z in range(Z)] for a in range(4)]
+EIGHTS = [[at(fold(a, b), z, 0) for b in range(2) for z in range(Z)] for a in range(4)]
 EIGHTS += [[at(x, z, 1) for x in range(X)] for z in range(Z)]
 SWAP = [(i, i ^ 1) for i in range(X * Z * C)]
 
 
 def place(core, x, z):
     first = core == 0
-    return jnp.where(first, x // 2, z), jnp.where(first, x % 2 * Z + z, x)
+    return jnp.where(first, min(x, X - 1 - x), z), jnp.where(first, x // 4 * Z + z, x)
 
 
-def call(body, outs, *operands):
-    vmem = pl.BlockSpec(memory_space=pltpu.VMEM)
+def call(body, outs, *operands, where=pltpu.VMEM, params=PARAMS, scratch=()):
+    vmem, read = (pl.BlockSpec(memory_space=m) for m in (pltpu.VMEM, where))
     return pl.pallas_call(
         body,
         out_shape=outs,
-        in_specs=[vmem] * len(operands),
+        in_specs=[read] * len(operands),
         out_specs=jax.tree.map(lambda _: vmem, outs),
-        compiler_params=PARAMS,
+        scratch_shapes=scratch,
+        compiler_params=params,
     )(*operands)
 
 
@@ -48,14 +50,18 @@
     return lax.dot_general(a, b, (dims, ((), ())), preferred_element_type=F32)
 
 
-def pack(x, w_in, y, w_out, out):
+def pack(x, w_in, y, w_out, out, sem):
     other = 1 - this_core()
-    out[0, :T] = x[...]
-    out[1, :T] = y[...]
+    half = pl.ds(pl.multiple_of(other * X * B, B), X * B)
+    pairs = [(x, out.at[0, pl.ds(0, T)]), (y, out.at[1, pl.ds(0, T)])]
+    pairs += [(w_out.at[half], out.at[1, pl.ds(T, X * B)])]
     for j in range(X):
-        rows = slice(T + j * B, T + (j + 1) * B)
-        out[0, rows] = w_in[:, columns(other, j)]
-        out[1, rows] = w_out[columns(other, j), :]
+        pairs += [(w_in.at[:, columns(other, j)], out.at[0, pl.ds(T + j * B, B)])]
+    copies = [pltpu.make_async_copy(a, b, sem.at[i]) for i, (a, b) in enumerate(pairs)]
+    for copy in copies:
+        copy.start()
+    for copy in copies:
+        copy.wait()
 
 
 def partial_sums(x, w_in, y, w_out, theirs, out):
@@ -140,7 +146,15 @@
         return lax.all_to_all(v, "gx", 0, 0, axis_index_groups=groups, tiled=True)
 
     both = (4, X, 2, Q, B)
-    theirs = swap(call(pack, s((2, T + X * B, B), BF16), inputs, w_in, grad_out, w_out))
+    theirs = call(
+        pack,
+        s((2, T + X * B, B), BF16),
+        *(inputs, w_in, grad_out, w_out),
+        where=pltpu.HBM,
+        params=pltpu.CompilerParams(vmem_limit_bytes=56 * 1024 * 1024),
+        scratch=(pltpu.SemaphoreType.DMA((3 + X,)),),
+    )
+    theirs = swap(theirs)
     sums = call(partial_sums, s(both, BF16), inputs, w_in, grad_out, w_out, theirs)
     sums = call(add_fours, s(both[1:], BF16), exchange(sums, FOURS))
     mine = call(middle, s(both[1:], BF16), exchange(sums, EIGHTS))

time: 138 us -> 137 us (level)
  local copies, waits for them, and re-layouts: 4.55 us -> 0.68 us
  Pallas kernels: 5.06 us -> 7.09 us
    unnamed x16 -> x10, local copies, waits for them, and re-layouts: 4.55 us -> 0.68 us
    pallas_call x8, Pallas kernels: 5.06 us -> 7.09 us  [call(): pl.pallas_call(body, out_shape=outs, in_specs=[read] * len(operands), out...]
where the time goes in v6:
time: 137 us; the launch traced here: 136 us
  blocking collectives  84.4 us (62%)
  starting transfers between devices  30.9 us (23%)
  waiting for transfers between devices  12.3 us (9%)
  Pallas kernels  7.09 us (5%)
    all_to_all x4, blocking collectives, exchange(): return lax.all_to_all(v, 'gx', 0, 0, axis_index_groups=groups, tiled=True)  84.4 us
    ppermute x2, starting transfers between devices, per_device(): swap = lambda v: lax.ppermute(v, 'gx', SWAP)  22.2 us
    all_to_all x1, starting transfers between devices, per_device(): part = lax.all_to_all(part.reshape(16, T // 16, B), 'gy', 0, 0, tiled=True)  8.7 us
    all_to_all x1, waiting for transfers between devices, per_device(): part = lax.all_to_all(part.reshape(16, T // 16, B), 'gy', 0, 0, tiled=True)  7.3 us
    pallas_call x8, Pallas kernels, call(): pl.pallas_call(body, out_shape=outs, in_specs=[read] * len(operands), out...  7.09 us
    ppermute x2, waiting for transfers between devices, per_device(): swap = lambda v: lax.ppermute(v, 'gx', SWAP)  5.02 us
  transfers between devices with their start and end apart: 3, of which 3 were waited for; matrix products, arithmetic and copies ran while one was open for 0% of the time, Pallas kernels for 2%

profile of v6, /device:TPU:1, one launch (start us, length us, event | category | flops | bytes accessed | tf_op | source)
XLA Modules:
  0.0 136.1 jit_solution(152168966276455883)
XLA Ops:
  0.6 0.0 copy-start.2
  0.6 0.0 copy-start
  0.7 0.0 copy-start.3
  0.7 2.1 %shard_map.67 = bf16[2,1408,128]{2,1,0:T(8,128)(2,1)} custom-call(bf16[384,128]{1,0:T(8,128)(2,1)} %x.5, bf16[128,2048]{1,0:T(8,128)(2,1)} %w.1, bf16[384,128]{1,0:T(8,128)(2,1)} %y.5, bf16[2048,128]{1,0:T(8,128)(2,1)} %w_out.3), custom_call_target="tpu_custom_call" | custom-call | tf_op jit(solution)/shard_map/pallas_call | solution.py:31
  2.8 16.1 %collective-permute-start = (bf16[2,1408,128]{2,1,0:T(8,128)(2,1)}, bf16[2,1408,128]{2,1,0:T(8,128)(2,1)S(1)}, u32[]{:S(2)}, u32[]{:S(2)}) collective-permute-start(bf16[2,1408,128]{2,1,0:T(8,128)(2,1)} %shard_map.67), channel_id=1, source_target_pairs={{0,16},{16,0},{32,48},{48,32},{64,80},{80,64},{96,112},{112,96},{1... | collective-permute-start | bytes 2162696 | tf_op jit(solution)/shard_map/ppermute | solution.py:143
  18.9 2.0 %collective-permute-done.theirs = bf16[2,1408,128]{2,1,0:T(8,128)(2,1)S(1)} collective-permute-done((bf16[2,1408,128]{2,1,0:T(8,128)(2,1)}, bf16[2,1408,128]{2,1,0:T(8,128)(2,1)S(1)}, u32[]{:S(2)}, u32[]{:S(2)}) %collective-permute-start) | collective-permute-done | bytes 720928 | tf_op jit(solution)/shard_map/ppermute | solution.py:143
  20.9 0.0 copy-done.1
  20.9 1.0 shard_map.68
  21.9 24.2 %all_to_all.25.parts = bf16[4,8,2,96,128]{4,3,2,1,0:T(8,128)(2,1)S(1)} all-to-all(bf16[4,8,2,96,128]{4,3,2,1,0:T(8,128)(2,1)S(1)} %shard_map.68), channel_id=1, replica_groups={{0,128,256,384},{32,160,288,416},{64,192,320,448},{96,224,352,480},{896..., dimensions={0} | all-to-all | bytes 3145728 | tf_op jit(solution)/shard_map/all_to_all | solution.py:146
  46.1 0.2 shard_map.69
  46.3 18.3 %all_to_all.26.parts = bf16[8,2,96,128]{3,2,1,0:T(8,128)(2,1)S(1)} all-to-all(bf16[8,2,96,128]{3,2,1,0:T(8,128)(2,1)S(1)} %shard_map.69), channel_id=1, replica_groups={{0,32,64,96,896,928,960,992},{128,160,192,224,768,800,832,864},{256,288..., dimensions={0} | all-to-all | bytes 786432 | tf_op jit(solution)/shard_map/all_to_all | solution.py:146
  64.5 0.1 shard_map.70
  64.6 15.6 %all_to_all.27.part = bf16[8,2,96,128]{3,2,1,0:T(8,128)(2,1)S(1)} all-to-all(bf16[8,2,96,128]{3,2,1,0:T(8,128)(2,1)S(1)} %shard_map.70), channel_id=1, replica_groups={{0,32,64,96,896,928,960,992},{128,160,192,224,768,800,832,864},{256,288..., dimensions={0} | all-to-all | bytes 786432 | tf_op jit(solution)/shard_map/all_to_all | solution.py:146
  80.2 0.2 shard_map.71
  80.4 26.3 %all_to_all.28.mine = bf16[4,8,2,96,128]{4,3,2,1,0:T(8,128)(2,1)S(1)} all-to-all(bf16[4,8,2,96,128]{4,3,2,1,0:T(8,128)(2,1)S(1)} %shard_map.71), channel_id=1, replica_groups={{0,128,256,384},{32,160,288,416},{64,192,320,448},{96,224,352,480},{896..., dimensions={0} | all-to-all | bytes 3145728 | tf_op jit(solution)/shard_map/all_to_all | solution.py:146
  106.7 6.2 %collective-permute-start.1 = (bf16[4,8,2,96,128]{4,3,2,1,0:T(8,128)(2,1)S(1)}, bf16[4,8,2,96,128]{4,3,2,1,0:T(8,128)(2,1)S(1)}, u32[]{:S(2)}, u32[]{:S(2)}) collective-permute-start(bf16[4,8,2,96,128]{4,3,2,1,0:T(8,128)(2,1)S(1)} %all_to_all.28.mine), channel_id=1, source_target_pairs={{0,16},{16,0},{32,48},{48,32},{64,80},{80,64},{96,112},{112,96},{1... | collective-permute-start | bytes 4718600 | tf_op jit(solution)/shard_map/ppermute | solution.py:143
  112.9 3.0 %collective-permute-done.1.theirs = bf16[4,8,2,96,128]{4,3,2,1,0:T(8,128)(2,1)S(1)} collective-permute-done((bf16[4,8,2,96,128]{4,3,2,1,0:T(8,128)(2,1)S(1)}, bf16[4,8,2,96,128]{4,3,2,1,0:T(8,128)(2,1)S(1)}, u32[]{:S(2)}, u32[]{:S(2)}) %collective-permute-start.1) | collective-permute-done | bytes 1572896 | tf_op jit(solution)/shard_map/ppermute | solution.py:143
  115.9 0.6 shard_map.72
  116.5 0.0 copy-start.4
  116.5 0.7 copy-done.4
  117.2 8.7 %all-to-all-start.4 = ((f32[16,24,128]{2,1,0:T(8,128)}), f32[16,24,128]{2,1,0:T(8,128)S(1)}, u32[]{:S(2)}, u32[]{:S(2)}) async-start(f32[16,24,128]{2,1,0:T(8,128)} %bitcast.1), calls=%async_computation.4 | async-start | bytes 393216 | tf_op jit(solution)/shard_map/all_to_all | solution.py:164
  125.9 2.3 %shard_map.74 = (f32[128,2048]{1,0:T(8,128)}, f32[2048,128]{1,0:T(8,128)}) custom-call(bf16[4,8,2,96,128]{4,3,2,1,0:T(8,128)(2,1)S(1)} %all_to_all.28.mine, bf16[4,8,2,96,128]{4,3,2,1,0:T(8,128)(2,1)S(1)} %collective-permute-done.1.theirs, bf16[384,128]{1,0:T(8,128)(2,1)S(1)} %copy-done.2, bf16[384,128]{1,0:T(8,128)(2,1)S(1)} %copy-done.3), custom_call_target="tpu_custom_call" | custom-call | tf_op jit(solution)/shard_map/pallas_call | solution.py:31
  128.2 7.3 %all-to-all-done.4.parts = f32[16,24,128]{2,1,0:T(8,128)S(1)} async-done(((f32[16,24,128]{2,1,0:T(8,128)}), f32[16,24,128]{2,1,0:T(8,128)S(1)}, u32[]{:S(2)}, u32[]{:S(2)}) %all-to-all-start.4) | async-done | bytes 196640 | tf_op jit(solution)/shard_map/all_to_all | solution.py:164
  135.5 0.6 shard_map.73
  (4 shorter events, 0.0 us)
Async XLA Ops:
  0.6 20.2 %copy-start.2 = (bf16[384,128]{1,0:T(8,128)(2,1)S(1)}, bf16[384,128]{1,0:T(8,128)(2,1)}, u32[]{:S(2)}) copy-start(bf16[384,128]{1,0:T(8,128)(2,1)} %x.5) | copy-start | bytes 294916
  0.6 20.2 %copy-start = (bf16[128,2048]{1,0:T(8,128)(2,1)S(1)}, bf16[128,2048]{1,0:T(8,128)(2,1)}, u32[]{:S(2)}) copy-start(bf16[128,2048]{1,0:T(8,128)(2,1)} %w.1) | copy-start | bytes 1572868
  0.7 20.2 %copy-start.3 = (bf16[384,128]{1,0:T(8,128)(2,1)S(1)}, bf16[384,128]{1,0:T(8,128)(2,1)}, u32[]{:S(2)}) copy-start(bf16[384,128]{1,0:T(8,128)(2,1)} %y.5) | copy-start | bytes 294916
  0.7 20.2 %copy-start.1 = (bf16[2048,128]{1,0:T(8,128)(2,1)S(1)}, bf16[2048,128]{1,0:T(8,128)(2,1)}, u32[]{:S(2)}) copy-start(bf16[2048,128]{1,0:T(8,128)(2,1)} %w_out.3) | copy-start | bytes 1572868
  2.8 18.1 %collective-permute-start = (bf16[2,1408,128]{2,1,0:T(8,128)(2,1)}, bf16[2,1408,128]{2,1,0:T(8,128)(2,1)S(1)}, u32[]{:S(2)}, u32[]{:S(2)}) collective-permute-start(bf16[2,1408,128]{2,1,0:T(8,128)(2,1)} %shard_map.67), channel_id=1, source_target_pairs={{0,16},{16,0},{32,48},{48,32},{64,80},{80,64},{96,112},{112,96},{1... | collective-permute-start | bytes 2162696 | tf_op jit(solution)/shard_map/ppermute | solution.py:143
  106.7 9.2 %collective-permute-start.1 = (bf16[4,8,2,96,128]{4,3,2,1,0:T(8,128)(2,1)S(1)}, bf16[4,8,2,96,128]{4,3,2,1,0:T(8,128)(2,1)S(1)}, u32[]{:S(2)}, u32[]{:S(2)}) collective-permute-start(bf16[4,8,2,96,128]{4,3,2,1,0:T(8,128)(2,1)S(1)} %all_to_all.28.mine), channel_id=1, source_target_pairs={{0,16},{16,0},{32,48},{48,32},{64,80},{80,64},{96,112},{112,96},{1... | collective-permute-start | bytes 4718600 | tf_op jit(solution)/shard_map/ppermute | solution.py:143
  116.5 0.7 copy-start.4
  117.2 18.3 %all-to-all-start.4 = ((f32[16,24,128]{2,1,0:T(8,128)}), f32[16,24,128]{2,1,0:T(8,128)S(1)}, u32[]{:S(2)}, u32[]{:S(2)}) async-start(f32[16,24,128]{2,1,0:T(8,128)} %bitcast.1), calls=%async_computation.4 | async-start | bytes 393216 | tf_op jit(solution)/shard_map/all_to_all | solution.py:164

commit v7 on v6

--- a/solution.py
+++ b/solution.py
@@ -12,18 +12,18 @@
 X, Z, C = 8, 4, 2
 Q = T // Z
 
+HALVES = ((0, 2, 3, 5), (7, 1, 4, 6))
 at = lambda x, z, c: (x * Z + z) * C + c
-fold = lambda a, b: a if b == 0 else X - 1 - a
-FOURS = [[at(fold(a, b), z, 0) for a in range(4)] for b in range(2) for z in range(Z)]
+FOURS = [[at(x, z, 0) for x in half] for half in HALVES for z in range(Z)]
 FOURS += [[at(x, z, 1) for z in range(Z)] for x in range(X)]
-EIGHTS = [[at(fold(a, b), z, 0) for b in range(2) for z in range(Z)] for a in range(4)]
+EIGHTS = [[at(half[a], z, 0) for half in HALVES for z in range(Z)] for a in range(4)]
 EIGHTS += [[at(x, z, 1) for x in range(X)] for z in range(Z)]
 SWAP = [(i, i ^ 1) for i in range(X * Z * C)]
 
 
 def place(core, x, z):
-    first = core == 0
-    return jnp.where(first, min(x, X - 1 - x), z), jnp.where(first, x // 4 * Z + z, x)
+    first, half = core == 0, int(x in HALVES[1])
+    return jnp.where(first, HALVES[half].index(x), z), jnp.where(first, half * Z + z, x)
 
 
 def call(body, outs, *operands, where=pltpu.VMEM, params=PARAMS, scratch=()):

time: 137 us -> 134 us (0.978); the launches traced: 136 us -> 132 us
  blocking collectives: 84.4 us -> 79.9 us
    all_to_all x4, blocking collectives: 84.4 us -> 79.9 us  [exchange(): return lax.all_to_all(v, 'gx', 0, 0, axis_index_groups=groups, tiled=True)]
where the time goes in v7:
time: 134 us; the launch traced here: 132 us
  blocking collectives  79.9 us (60%)
  starting transfers between devices  31 us (23%)
  waiting for transfers between devices  12.3 us (9%)
  Pallas kernels  7.09 us (5%)
    all_to_all x4, blocking collectives, exchange(): return lax.all_to_all(v, 'gx', 0, 0, axis_index_groups=groups, tiled=True)  79.9 us
    ppermute x2, starting transfers between devices, per_device(): swap = lambda v: lax.ppermute(v, 'gx', SWAP)  22.1 us
    all_to_all x1, starting transfers between devices, per_device(): part = lax.all_to_all(part.reshape(16, T // 16, B), 'gy', 0, 0, tiled=True)  8.88 us
    all_to_all x1, waiting for transfers between devices, per_device(): part = lax.all_to_all(part.reshape(16, T // 16, B), 'gy', 0, 0, tiled=True)  7.3 us
    pallas_call x8, Pallas kernels, call(): pl.pallas_call(body, out_shape=outs, in_specs=[read] * len(operands), out...  7.09 us
    ppermute x2, waiting for transfers between devices, per_device(): swap = lambda v: lax.ppermute(v, 'gx', SWAP)  5.02 us
  transfers between devices with their start and end apart: 3, of which 3 were waited for; matrix products, arithmetic and copies ran while one was open for 0% of the time, Pallas kernels for 2%

profile of v7, /device:TPU:1, one launch (start us, length us, event | category | flops | bytes accessed | tf_op | source)
XLA Modules:
  0.0 131.7 jit_solution(13370163175588282101)
XLA Ops:
  0.6 0.0 copy-start.2
  0.6 0.0 copy-start
  0.7 0.0 copy-start.3
  0.7 2.1 %shard_map.67 = bf16[2,1408,128]{2,1,0:T(8,128)(2,1)} custom-call(bf16[384,128]{1,0:T(8,128)(2,1)} %x.5, bf16[128,2048]{1,0:T(8,128)(2,1)} %w.1, bf16[384,128]{1,0:T(8,128)(2,1)} %y.5, bf16[2048,128]{1,0:T(8,128)(2,1)} %w_out.3), custom_call_target="tpu_custom_call" | custom-call | tf_op jit(solution)/shard_map/pallas_call | solution.py:31
  2.8 16.1 %collective-permute-start = (bf16[2,1408,128]{2,1,0:T(8,128)(2,1)}, bf16[2,1408,128]{2,1,0:T(8,128)(2,1)S(1)}, u32[]{:S(2)}, u32[]{:S(2)}) collective-permute-start(bf16[2,1408,128]{2,1,0:T(8,128)(2,1)} %shard_map.67), channel_id=1, source_target_pairs={{0,16},{16,0},{32,48},{48,32},{64,80},{80,64},{96,112},{112,96},{1... | collective-permute-start | bytes 2162696 | tf_op jit(solution)/shard_map/ppermute | solution.py:143
  18.9 2.0 %collective-permute-done.theirs = bf16[2,1408,128]{2,1,0:T(8,128)(2,1)S(1)} collective-permute-done((bf16[2,1408,128]{2,1,0:T(8,128)(2,1)}, bf16[2,1408,128]{2,1,0:T(8,128)(2,1)S(1)}, u32[]{:S(2)}, u32[]{:S(2)}) %collective-permute-start) | collective-permute-done | bytes 720928 | tf_op jit(solution)/shard_map/ppermute | solution.py:143
  20.9 0.0 copy-done.1
  20.9 1.0 shard_map.68
  21.9 24.2 %all_to_all.25.parts = bf16[4,8,2,96,128]{4,3,2,1,0:T(8,128)(2,1)S(1)} all-to-all(bf16[4,8,2,96,128]{4,3,2,1,0:T(8,128)(2,1)S(1)} %shard_map.68), channel_id=1, replica_groups={{0,256,384,640},{32,288,416,672},{64,320,448,704},{96,352,480,736},{896..., dimensions={0} | all-to-all | bytes 3145728 | tf_op jit(solution)/shard_map/all_to_all | solution.py:146
  46.1 0.2 shard_map.69
  46.3 17.1 %all_to_all.26.parts = bf16[8,2,96,128]{3,2,1,0:T(8,128)(2,1)S(1)} all-to-all(bf16[8,2,96,128]{3,2,1,0:T(8,128)(2,1)S(1)} %shard_map.69), channel_id=1, replica_groups={{0,32,64,96,896,928,960,992},{256,288,320,352,128,160,192,224},{384,416..., dimensions={0} | all-to-all | bytes 786432 | tf_op jit(solution)/shard_map/all_to_all | solution.py:146
  63.4 0.1 shard_map.70
  63.5 13.3 %all_to_all.27.part = bf16[8,2,96,128]{3,2,1,0:T(8,128)(2,1)S(1)} all-to-all(bf16[8,2,96,128]{3,2,1,0:T(8,128)(2,1)S(1)} %shard_map.70), channel_id=1, replica_groups={{0,32,64,96,896,928,960,992},{256,288,320,352,128,160,192,224},{384,416..., dimensions={0} | all-to-all | bytes 786432 | tf_op jit(solution)/shard_map/all_to_all | solution.py:146
  76.8 0.2 shard_map.71
  77.0 25.3 %all_to_all.28.mine = bf16[4,8,2,96,128]{4,3,2,1,0:T(8,128)(2,1)S(1)} all-to-all(bf16[4,8,2,96,128]{4,3,2,1,0:T(8,128)(2,1)S(1)} %shard_map.71), channel_id=1, replica_groups={{0,256,384,640},{32,288,416,672},{64,320,448,704},{96,352,480,736},{896..., dimensions={0} | all-to-all | bytes 3145728 | tf_op jit(solution)/shard_map/all_to_all | solution.py:146
  102.3 6.0 %collective-permute-start.1 = (bf16[4,8,2,96,128]{4,3,2,1,0:T(8,128)(2,1)S(1)}, bf16[4,8,2,96,128]{4,3,2,1,0:T(8,128)(2,1)S(1)}, u32[]{:S(2)}, u32[]{:S(2)}) collective-permute-start(bf16[4,8,2,96,128]{4,3,2,1,0:T(8,128)(2,1)S(1)} %all_to_all.28.mine), channel_id=1, source_target_pairs={{0,16},{16,0},{32,48},{48,32},{64,80},{80,64},{96,112},{112,96},{1... | collective-permute-start | bytes 4718600 | tf_op jit(solution)/shard_map/ppermute | solution.py:143
  108.3 3.0 %collective-permute-done.1.theirs = bf16[4,8,2,96,128]{4,3,2,1,0:T(8,128)(2,1)S(1)} collective-permute-done((bf16[4,8,2,96,128]{4,3,2,1,0:T(8,128)(2,1)S(1)}, bf16[4,8,2,96,128]{4,3,2,1,0:T(8,128)(2,1)S(1)}, u32[]{:S(2)}, u32[]{:S(2)}) %collective-permute-start.1) | collective-permute-done | bytes 1572896 | tf_op jit(solution)/shard_map/ppermute | solution.py:143
  111.3 0.6 shard_map.72
  111.9 0.0 copy-start.4
  111.9 0.7 copy-done.4
  112.6 8.9 %all-to-all-start.4 = ((f32[16,24,128]{2,1,0:T(8,128)}), f32[16,24,128]{2,1,0:T(8,128)S(1)}, u32[]{:S(2)}, u32[]{:S(2)}) async-start(f32[16,24,128]{2,1,0:T(8,128)} %bitcast.1), calls=%async_computation.4 | async-start | bytes 393216 | tf_op jit(solution)/shard_map/all_to_all | solution.py:164
  121.5 2.3 %shard_map.74 = (f32[128,2048]{1,0:T(8,128)}, f32[2048,128]{1,0:T(8,128)}) custom-call(bf16[4,8,2,96,128]{4,3,2,1,0:T(8,128)(2,1)S(1)} %all_to_all.28.mine, bf16[4,8,2,96,128]{4,3,2,1,0:T(8,128)(2,1)S(1)} %collective-permute-done.1.theirs, bf16[384,128]{1,0:T(8,128)(2,1)S(1)} %copy-done.2, bf16[384,128]{1,0:T(8,128)(2,1)S(1)} %copy-done.3), custom_call_target="tpu_custom_call" | custom-call | tf_op jit(solution)/shard_map/pallas_call | solution.py:31
  123.8 7.3 %all-to-all-done.4.parts = f32[16,24,128]{2,1,0:T(8,128)S(1)} async-done(((f32[16,24,128]{2,1,0:T(8,128)}), f32[16,24,128]{2,1,0:T(8,128)S(1)}, u32[]{:S(2)}, u32[]{:S(2)}) %all-to-all-start.4) | async-done | bytes 196640 | tf_op jit(solution)/shard_map/all_to_all | solution.py:164
  131.1 0.6 shard_map.73
  (4 shorter events, 0.0 us)
Async XLA Ops:
  0.6 20.2 %copy-start.2 = (bf16[384,128]{1,0:T(8,128)(2,1)S(1)}, bf16[384,128]{1,0:T(8,128)(2,1)}, u32[]{:S(2)}) copy-start(bf16[384,128]{1,0:T(8,128)(2,1)} %x.5) | copy-start | bytes 294916
  0.6 20.2 %copy-start = (bf16[128,2048]{1,0:T(8,128)(2,1)S(1)}, bf16[128,2048]{1,0:T(8,128)(2,1)}, u32[]{:S(2)}) copy-start(bf16[128,2048]{1,0:T(8,128)(2,1)} %w.1) | copy-start | bytes 1572868
  0.7 20.2 %copy-start.3 = (bf16[384,128]{1,0:T(8,128)(2,1)S(1)}, bf16[384,128]{1,0:T(8,128)(2,1)}, u32[]{:S(2)}) copy-start(bf16[384,128]{1,0:T(8,128)(2,1)} %y.5) | copy-start | bytes 294916
  0.7 20.2 %copy-start.1 = (bf16[2048,128]{1,0:T(8,128)(2,1)S(1)}, bf16[2048,128]{1,0:T(8,128)(2,1)}, u32[]{:S(2)}) copy-start(bf16[2048,128]{1,0:T(8,128)(2,1)} %w_out.3) | copy-start | bytes 1572868
  2.8 18.1 %collective-permute-start = (bf16[2,1408,128]{2,1,0:T(8,128)(2,1)}, bf16[2,1408,128]{2,1,0:T(8,128)(2,1)S(1)}, u32[]{:S(2)}, u32[]{:S(2)}) collective-permute-start(bf16[2,1408,128]{2,1,0:T(8,128)(2,1)} %shard_map.67), channel_id=1, source_target_pairs={{0,16},{16,0},{32,48},{48,32},{64,80},{80,64},{96,112},{112,96},{1... | collective-permute-start | bytes 2162696 | tf_op jit(solution)/shard_map/ppermute | solution.py:143
  102.3 9.0 %collective-permute-start.1 = (bf16[4,8,2,96,128]{4,3,2,1,0:T(8,128)(2,1)S(1)}, bf16[4,8,2,96,128]{4,3,2,1,0:T(8,128)(2,1)S(1)}, u32[]{:S(2)}, u32[]{:S(2)}) collective-permute-start(bf16[4,8,2,96,128]{4,3,2,1,0:T(8,128)(2,1)S(1)} %all_to_all.28.mine), channel_id=1, source_target_pairs={{0,16},{16,0},{32,48},{48,32},{64,80},{80,64},{96,112},{112,96},{1... | collective-permute-start | bytes 4718600 | tf_op jit(solution)/shard_map/ppermute | solution.py:143
  111.9 0.7 copy-start.4
  112.6 18.5 %all-to-all-start.4 = ((f32[16,24,128]{2,1,0:T(8,128)}), f32[16,24,128]{2,1,0:T(8,128)S(1)}, u32[]{:S(2)}, u32[]{:S(2)}) async-start(f32[16,24,128]{2,1,0:T(8,128)} %bitcast.1), calls=%async_computation.4 | async-start | bytes 393216 | tf_op jit(solution)/shard_map/all_to_all | solution.py:164

commit v8 on v7

--- a/solution.py
+++ b/solution.py
@@ -14,15 +14,21 @@
 
 HALVES = ((0, 2, 3, 5), (7, 1, 4, 6))
 at = lambda x, z, c: (x * Z + z) * C + c
-FOURS = [[at(x, z, 0) for x in half] for half in HALVES for z in range(Z)]
-FOURS += [[at(x, z, 1) for z in range(Z)] for x in range(X)]
-EIGHTS = [[at(half[a], z, 0) for half in HALVES for z in range(Z)] for a in range(4)]
-EIGHTS += [[at(x, z, 1) for x in range(X)] for z in range(Z)]
+
+
+def groups(c):
+    fours = [[at(x, z, c) for x in half] for half in HALVES for z in range(Z)]
+    fours += [[at(x, z, 1 - c) for z in range(Z)] for x in range(X)]
+    eights = [[at(half[a], z, c) for half in HALVES for z in range(Z)] for a in range(4)]
+    eights += [[at(x, z, 1 - c) for x in range(X)] for z in range(Z)]
+    return fours, eights
+
+
 SWAP = [(i, i ^ 1) for i in range(X * Z * C)]
 
 
-def place(core, x, z):
-    first, half = core == 0, int(x in HALVES[1])
+def place(first, x, z):
+    half = int(x in HALVES[1])
     return jnp.where(first, HALVES[half].index(x), z), jnp.where(first, half * Z + z, x)
 
 
@@ -74,7 +80,7 @@
         g = g + dot(theirs[1, :T], theirs[1, rows], ((1,), (1,)))
         h, g = h.astype(BF16), g.astype(BF16)
         for z in range(Z):
-            four, eight = place(core, j, z)
+            four, eight = place(core == 0, j, z)
             out[four, eight, 0] = h[z * Q : (z + 1) * Q]
             out[four, eight, 1] = g[z * Q : (z + 1) * Q]
 
@@ -112,7 +118,7 @@
 
 
 def tokens(ref, core, x, which):
-    blocks = [ref[(*place(core, x, z), which)] for z in range(Z)]
+    blocks = [ref[(*place(core == 1, x, z), which)] for z in range(Z)]
     return jnp.concatenate(blocks, axis=0)
 
 
@@ -156,9 +162,11 @@
     )
     theirs = swap(theirs)
     sums = call(partial_sums, s(both, BF16), inputs, w_in, grad_out, w_out, theirs)
-    sums = call(add_fours, s(both[1:], BF16), exchange(sums, FOURS))
-    mine = call(middle, s(both[1:], BF16), exchange(sums, EIGHTS))
-    mine = exchange(call(copies, s(both, BF16), exchange(mine, EIGHTS)), FOURS)
+    fours, eights = groups(0)
+    sums = call(add_fours, s(both[1:], BF16), exchange(sums, fours))
+    mine = call(middle, s(both[1:], BF16), exchange(sums, eights))
+    fours, eights = groups(1)
+    mine = exchange(call(copies, s(both, BF16), exchange(mine, eights)), fours)
     theirs = swap(mine)
     part = call(input_part, s((T, B), F32), mine, theirs, w_in)
     part = lax.all_to_all(part.reshape(16, T // 16, B), "gy", 0, 0, tiled=True)

time: 134 us -> 134 us (level); the launches traced: 132 us -> 134 us
  starting transfers between devices: 31 us -> 33 us
    ppermute x2, starting transfers between devices: 22.1 us -> 25.6 us  [per_device(): swap = lambda v: lax.ppermute(v, 'gx', SWAP)]
    all_to_all x1, starting transfers between devices: 8.88 us -> 7.39 us  [per_device(): part = lax.all_to_all(part.reshape(16, T // 16, B), 'gy', 0, 0, tiled=True)]
where the time goes in v8:
time: 134 us
  blocking collectives  80.1 us (60%)
  starting transfers between devices  33 us (25%)
  waiting for transfers between devices  12.3 us (9%)
  Pallas kernels  7.09 us (5%)
    all_to_all x4, blocking collectives, exchange(): return lax.all_to_all(v, 'gx', 0, 0, axis_index_groups=groups, tiled=True)  80.1 us
    ppermute x2, starting transfers between devices, per_device(): swap = lambda v: lax.ppermute(v, 'gx', SWAP)  25.6 us
    all_to_all x1, starting transfers between devices, per_device(): part = lax.all_to_all(part.reshape(16, T // 16, B), 'gy', 0, 0, tiled=True)  7.39 us
    all_to_all x1, waiting for transfers between devices, per_device(): part = lax.all_to_all(part.reshape(16, T // 16, B), 'gy', 0, 0, tiled=True)  7.3 us
    pallas_call x8, Pallas kernels, call(): pl.pallas_call(body, out_shape=outs, in_specs=[read] * len(operands), out...  7.09 us
    ppermute x2, waiting for transfers between devices, per_device(): swap = lambda v: lax.ppermute(v, 'gx', SWAP)  5.02 us
  transfers between devices with their start and end apart: 3, of which 3 were waited for; matrix products, arithmetic and copies ran while one was open for 0% of the time, Pallas kernels for 2%

profile of v8, /device:TPU:1, one launch (start us, length us, event | category | flops | bytes accessed | tf_op | source)
XLA Modules:
  0.0 134.0 jit_solution(11414328199715825036)
XLA Ops:
  0.6 0.0 copy-start.2
  0.6 0.0 copy-start
  0.7 0.0 copy-start.3
  0.7 0.0 copy-start.1
  0.7 2.1 %shard_map.67 = bf16[2,1408,128]{2,1,0:T(8,128)(2,1)} custom-call(bf16[384,128]{1,0:T(8,128)(2,1)} %x.5, bf16[128,2048]{1,0:T(8,128)(2,1)} %w.1, bf16[384,128]{1,0:T(8,128)(2,1)} %y.5, bf16[2048,128]{1,0:T(8,128)(2,1)} %w_out.3), custom_call_target="tpu_custom_call" | custom-call | tf_op jit(solution)/shard_map/pallas_call | solution.py:37
  2.8 16.1 %collective-permute-start = (bf16[2,1408,128]{2,1,0:T(8,128)(2,1)}, bf16[2,1408,128]{2,1,0:T(8,128)(2,1)S(1)}, u32[]{:S(2)}, u32[]{:S(2)}) collective-permute-start(bf16[2,1408,128]{2,1,0:T(8,128)(2,1)} %shard_map.67), channel_id=1, source_target_pairs={{0,16},{16,0},{32,48},{48,32},{64,80},{80,64},{96,112},{112,96},{1... | collective-permute-start | bytes 2162696 | tf_op jit(solution)/shard_map/ppermute | solution.py:149
  18.9 2.0 %collective-permute-done.theirs = bf16[2,1408,128]{2,1,0:T(8,128)(2,1)S(1)} collective-permute-done((bf16[2,1408,128]{2,1,0:T(8,128)(2,1)}, bf16[2,1408,128]{2,1,0:T(8,128)(2,1)S(1)}, u32[]{:S(2)}, u32[]{:S(2)}) %collective-permute-start) | collective-permute-done | bytes 720928 | tf_op jit(solution)/shard_map/ppermute | solution.py:149
  20.9 0.0 copy-done.1
  20.9 1.0 shard_map.68
  21.9 24.2 %all_to_all.25.parts = bf16[4,8,2,96,128]{4,3,2,1,0:T(8,128)(2,1)S(1)} all-to-all(bf16[4,8,2,96,128]{4,3,2,1,0:T(8,128)(2,1)S(1)} %shard_map.68), channel_id=1, replica_groups={{0,256,384,640},{32,288,416,672},{64,320,448,704},{96,352,480,736},{896..., dimensions={0} | all-to-all | bytes 3145728 | tf_op jit(solution)/shard_map/all_to_all | solution.py:152
  46.1 0.2 shard_map.69
  46.3 17.1 %all_to_all.26.parts = bf16[8,2,96,128]{3,2,1,0:T(8,128)(2,1)S(1)} all-to-all(bf16[8,2,96,128]{3,2,1,0:T(8,128)(2,1)S(1)} %shard_map.69), channel_id=1, replica_groups={{0,32,64,96,896,928,960,992},{256,288,320,352,128,160,192,224},{384,416..., dimensions={0} | all-to-all | bytes 786432 | tf_op jit(solution)/shard_map/all_to_all | solution.py:152
  63.4 0.1 shard_map.70
  63.5 13.7 %all_to_all.27.part = bf16[8,2,96,128]{3,2,1,0:T(8,128)(2,1)S(1)} all-to-all(bf16[8,2,96,128]{3,2,1,0:T(8,128)(2,1)S(1)} %shard_map.70), channel_id=1, replica_groups={{16,48,80,112,912,944,976,1008},{272,304,336,368,144,176,208,240},{400,..., dimensions={0} | all-to-all | bytes 786432 | tf_op jit(solution)/shard_map/all_to_all | solution.py:152
  77.2 0.2 shard_map.71
  77.4 25.1 %all_to_all.28.mine = bf16[4,8,2,96,128]{4,3,2,1,0:T(8,128)(2,1)S(1)} all-to-all(bf16[4,8,2,96,128]{4,3,2,1,0:T(8,128)(2,1)S(1)} %shard_map.71), channel_id=1, replica_groups={{16,272,400,656},{48,304,432,688},{80,336,464,720},{112,368,496,752},{9..., dimensions={0} | all-to-all | bytes 3145728 | tf_op jit(solution)/shard_map/all_to_all | solution.py:152
  102.5 9.6 %collective-permute-start.1 = (bf16[4,8,2,96,128]{4,3,2,1,0:T(8,128)(2,1)S(1)}, bf16[4,8,2,96,128]{4,3,2,1,0:T(8,128)(2,1)S(1)}, u32[]{:S(2)}, u32[]{:S(2)}) collective-permute-start(bf16[4,8,2,96,128]{4,3,2,1,0:T(8,128)(2,1)S(1)} %all_to_all.28.mine), channel_id=1, source_target_pairs={{0,16},{16,0},{32,48},{48,32},{64,80},{80,64},{96,112},{112,96},{1... | collective-permute-start | bytes 4718600 | tf_op jit(solution)/shard_map/ppermute | solution.py:149
  112.0 3.0 %collective-permute-done.1.theirs = bf16[4,8,2,96,128]{4,3,2,1,0:T(8,128)(2,1)S(1)} collective-permute-done((bf16[4,8,2,96,128]{4,3,2,1,0:T(8,128)(2,1)S(1)}, bf16[4,8,2,96,128]{4,3,2,1,0:T(8,128)(2,1)S(1)}, u32[]{:S(2)}, u32[]{:S(2)}) %collective-permute-start.1) | collective-permute-done | bytes 1572896 | tf_op jit(solution)/shard_map/ppermute | solution.py:149
  115.0 0.6 shard_map.72
  115.6 0.7 copy-done.4
  116.3 7.4 %all-to-all-start.4 = ((f32[16,24,128]{2,1,0:T(8,128)}), f32[16,24,128]{2,1,0:T(8,128)S(1)}, u32[]{:S(2)}, u32[]{:S(2)}) async-start(f32[16,24,128]{2,1,0:T(8,128)} %bitcast.1), calls=%async_computation.4 | async-start | bytes 393216 | tf_op jit(solution)/shard_map/all_to_all | solution.py:172
  123.7 2.3 %shard_map.74 = (f32[128,2048]{1,0:T(8,128)}, f32[2048,128]{1,0:T(8,128)}) custom-call(bf16[4,8,2,96,128]{4,3,2,1,0:T(8,128)(2,1)S(1)} %all_to_all.28.mine, bf16[4,8,2,96,128]{4,3,2,1,0:T(8,128)(2,1)S(1)} %collective-permute-done.1.theirs, bf16[384,128]{1,0:T(8,128)(2,1)S(1)} %copy-done.2, bf16[384,128]{1,0:T(8,128)(2,1)S(1)} %copy-done.3), custom_call_target="tpu_custom_call" | custom-call | tf_op jit(solution)/shard_map/pallas_call | solution.py:37
  126.0 7.3 %all-to-all-done.4.parts = f32[16,24,128]{2,1,0:T(8,128)S(1)} async-done(((f32[16,24,128]{2,1,0:T(8,128)}), f32[16,24,128]{2,1,0:T(8,128)S(1)}, u32[]{:S(2)}, u32[]{:S(2)}) %all-to-all-start.4) | async-done | bytes 196640 | tf_op jit(solution)/shard_map/all_to_all | solution.py:172
  133.3 0.6 shard_map.73
  (4 shorter events, 0.0 us)
Async XLA Ops:
  0.6 20.2 %copy-start.2 = (bf16[384,128]{1,0:T(8,128)(2,1)S(1)}, bf16[384,128]{1,0:T(8,128)(2,1)}, u32[]{:S(2)}) copy-start(bf16[384,128]{1,0:T(8,128)(2,1)} %x.5) | copy-start | bytes 294916
  0.6 20.2 %copy-start = (bf16[128,2048]{1,0:T(8,128)(2,1)S(1)}, bf16[128,2048]{1,0:T(8,128)(2,1)}, u32[]{:S(2)}) copy-start(bf16[128,2048]{1,0:T(8,128)(2,1)} %w.1) | copy-start | bytes 1572868
  0.7 20.2 %copy-start.3 = (bf16[384,128]{1,0:T(8,128)(2,1)S(1)}, bf16[384,128]{1,0:T(8,128)(2,1)}, u32[]{:S(2)}) copy-start(bf16[384,128]{1,0:T(8,128)(2,1)} %y.5) | copy-start | bytes 294916
  0.7 20.2 %copy-start.1 = (bf16[2048,128]{1,0:T(8,128)(2,1)S(1)}, bf16[2048,128]{1,0:T(8,128)(2,1)}, u32[]{:S(2)}) copy-start(bf16[2048,128]{1,0:T(8,128)(2,1)} %w_out.3) | copy-start | bytes 1572868
  2.8 18.1 %collective-permute-start = (bf16[2,1408,128]{2,1,0:T(8,128)(2,1)}, bf16[2,1408,128]{2,1,0:T(8,128)(2,1)S(1)}, u32[]{:S(2)}, u32[]{:S(2)}) collective-permute-start(bf16[2,1408,128]{2,1,0:T(8,128)(2,1)} %shard_map.67), channel_id=1, source_target_pairs={{0,16},{16,0},{32,48},{48,32},{64,80},{80,64},{96,112},{112,96},{1... | collective-permute-start | bytes 2162696 | tf_op jit(solution)/shard_map/ppermute | solution.py:149
  102.5 12.6 %collective-permute-start.1 = (bf16[4,8,2,96,128]{4,3,2,1,0:T(8,128)(2,1)S(1)}, bf16[4,8,2,96,128]{4,3,2,1,0:T(8,128)(2,1)S(1)}, u32[]{:S(2)}, u32[]{:S(2)}) collective-permute-start(bf16[4,8,2,96,128]{4,3,2,1,0:T(8,128)(2,1)S(1)} %all_to_all.28.mine), channel_id=1, source_target_pairs={{0,16},{16,0},{32,48},{48,32},{64,80},{80,64},{96,112},{112,96},{1... | collective-permute-start | bytes 4718600 | tf_op jit(solution)/shard_map/ppermute | solution.py:149
  115.6 0.7 copy-start.4
  116.3 17.0 %all-to-all-start.4 = ((f32[16,24,128]{2,1,0:T(8,128)}), f32[16,24,128]{2,1,0:T(8,128)S(1)}, u32[]{:S(2)}, u32[]{:S(2)}) async-start(f32[16,24,128]{2,1,0:T(8,128)} %bitcast.1), calls=%async_computation.4 | async-start | bytes 393216 | tf_op jit(solution)/shard_map/all_to_all | solution.py:172

commit v9 on v7

--- a/solution.py
+++ b/solution.py
@@ -26,12 +26,12 @@
     return jnp.where(first, HALVES[half].index(x), z), jnp.where(first, half * Z + z, x)
 
 
-def call(body, outs, *operands, where=pltpu.VMEM, params=PARAMS, scratch=()):
-    vmem, read = (pl.BlockSpec(memory_space=m) for m in (pltpu.VMEM, where))
+def call(body, outs, *operands, unread=0, where=pltpu.VMEM, params=PARAMS, scratch=()):
+    vmem, read, stay = (pl.BlockSpec(memory_space=m) for m in (pltpu.VMEM, where, pl.ANY))
     return pl.pallas_call(
         body,
         out_shape=outs,
-        in_specs=[read] * len(operands),
+        in_specs=[read] * (len(operands) - unread) + [stay] * unread,
         out_specs=jax.tree.map(lambda _: vmem, outs),
         scratch_shapes=scratch,
         compiler_params=params,
@@ -116,17 +116,20 @@
     return jnp.concatenate(blocks, axis=0)
 
 
-def input_part(mine, theirs, w, out):
+def input_parts(mine, w, theirs, own, other):
     core = this_core()
-    value = jnp.zeros((T, B), F32)
-    for who, ref in ((core, mine), (1 - core, theirs)):
-        for j in range(X):
-            value += dot(tokens(ref, who, j, 1), w[:, columns(who, j)], ((1,), (1,)))
-    out[...] = value
+    here, there = jnp.zeros((T, B), F32), jnp.zeros((T, B), F32)
+    for j in range(X):
+        value = tokens(mine, core, j, 1)
+        here += dot(value, w[:, columns(core, j)], ((1,), (1,)))
+        there += dot(value, theirs[0, T + j * B : T + (j + 1) * B], ((1,), (1,)))
+    own[...] = here
+    other[...] = there
 
 
-def weights(mine, theirs, x, y, out_in, out_out):
+def weights(mine, theirs, x, y, out_in, out_out, done):
     core = this_core()
+    done[...] = jnp.zeros_like(done)
     for who, ref in ((core, mine), (1 - core, theirs)):
         for j in range(X):
             there = columns(who, j)
@@ -134,7 +137,7 @@
             out_out[there, :] = dot(tokens(ref, who, j, 0), y[...], ((0,), (0,)))
 
 
-def finish(parts, out):
+def finish(parts, after, out):
     out[...] = total(parts).astype(BF16)
 
 
@@ -159,12 +162,13 @@
     sums = call(add_fours, s(both[1:], BF16), exchange(sums, FOURS))
     mine = call(middle, s(both[1:], BF16), exchange(sums, EIGHTS))
     mine = exchange(call(copies, s(both, BF16), exchange(mine, EIGHTS)), FOURS)
+    own, other = call(input_parts, (s((T, B), F32),) * 2, mine, w_in, theirs)
+    part = own + swap(other)
+    part = lax.all_to_all(part.reshape(16, T // 16, B), "gy", 0, 0, tiled=True)
     theirs = swap(mine)
-    part = call(input_part, s((T, B), F32), mine, theirs, w_in)
-    part = lax.all_to_all(part.reshape(16, T // 16, B), "gy", 0, 0, tiled=True)
-    outs = (s((B, 2 * X * B), F32), s((2 * X * B, B), F32))
-    grad_w_in, grad_w_out = call(weights, outs, mine, theirs, inputs, grad_out)
-    grad_inputs = call(finish, s((T // 16, B), BF16), part)
+    outs = (s((B, 2 * X * B), F32), s((2 * X * B, B), F32), s((8, B), F32))
+    grad_w_in, grad_w_out, done = call(weights, outs, mine, theirs, inputs, grad_out)
+    grad_inputs = call(finish, s((T // 16, B), BF16), part, done, unread=1)
     return (grad_inputs, grad_w_in, grad_w_out)
 
 

time: 134 us -> 134 us (level)
  starting transfers between devices: 31 us -> 32.9 us
    ppermute x2 -> x3, starting transfers between devices: 22.1 us -> 24 us  [per_device(): swap = lambda v: lax.ppermute(v, 'gx', SWAP)]
    ppermute x2 -> x3, waiting for transfers between devices: 5.02 us -> 3.41 us  [per_device(): swap = lambda v: lax.ppermute(v, 'gx', SWAP)]
  transfers between devices with their start and end apart: 3 -> 4, of which waited for: 3 -> 3; matrix products, arithmetic and copies ran while one was open for 0% -> 1% of each run, Pallas kernels for 2% -> 2%
where the time goes in v9:
time: 134 us; the launch traced here: 132 us
  blocking collectives  79.9 us (60%)
  starting transfers between devices  32.9 us (25%)
  waiting for transfers between devices  11 us (8%)
  Pallas kernels  7.07 us (5%)
    all_to_all x4, blocking collectives, exchange(): return lax.all_to_all(v, 'gx', 0, 0, axis_index_groups=groups, tiled=True)  79.9 us
    ppermute x3, starting transfers between devices, per_device(): swap = lambda v: lax.ppermute(v, 'gx', SWAP)  24 us
    all_to_all x1, starting transfers between devices, per_device(): part = lax.all_to_all(part.reshape(16, T // 16, B), 'gy', 0, 0, tiled=True)  8.87 us
    all_to_all x1, waiting for transfers between devices, per_device(): part = lax.all_to_all(part.reshape(16, T // 16, B), 'gy', 0, 0, tiled=True)  7.59 us
    pallas_call x8, Pallas kernels, call(): pl.pallas_call(body, out_shape=outs, in_specs=[read] * (len(operands) - u...  7.07 us
    ppermute x3, waiting for transfers between devices, per_device(): swap = lambda v: lax.ppermute(v, 'gx', SWAP)  3.41 us
  transfers between devices with their start and end apart: 4, of which 3 were waited for; matrix products, arithmetic and copies ran while one was open for 1% of the time, Pallas kernels for 2%

profile of v9, /device:TPU:1, one launch (start us, length us, event | category | flops | bytes accessed | tf_op | source)
XLA Modules:
  0.0 132.4 jit_solution(4978917702740579442)
XLA Ops:
  0.6 0.0 copy-start
  0.7 2.1 %shard_map.67 = bf16[2,1408,128]{2,1,0:T(8,128)(2,1)} custom-call(bf16[384,128]{1,0:T(8,128)(2,1)} %x.5, bf16[128,2048]{1,0:T(8,128)(2,1)} %w.1, bf16[384,128]{1,0:T(8,128)(2,1)} %y.5, bf16[2048,128]{1,0:T(8,128)(2,1)} %w_out.3), custom_call_target="tpu_custom_call" | custom-call | tf_op jit(solution)/shard_map/pallas_call | solution.py:31
  2.8 16.1 %collective-permute-start = (bf16[2,1408,128]{2,1,0:T(8,128)(2,1)}, bf16[2,1408,128]{2,1,0:T(8,128)(2,1)S(1)}, u32[]{:S(2)}, u32[]{:S(2)}) collective-permute-start(bf16[2,1408,128]{2,1,0:T(8,128)(2,1)} %shard_map.67), channel_id=1, source_target_pairs={{0,16},{16,0},{32,48},{48,32},{64,80},{80,64},{96,112},{112,96},{1... | collective-permute-start | bytes 2162696 | tf_op jit(solution)/shard_map/ppermute | solution.py:146
  18.9 2.0 %collective-permute-done.theirs = bf16[2,1408,128]{2,1,0:T(8,128)(2,1)S(1)} collective-permute-done((bf16[2,1408,128]{2,1,0:T(8,128)(2,1)}, bf16[2,1408,128]{2,1,0:T(8,128)(2,1)S(1)}, u32[]{:S(2)}, u32[]{:S(2)}) %collective-permute-start) | collective-permute-done | bytes 720928 | tf_op jit(solution)/shard_map/ppermute | solution.py:146
  20.9 0.0 copy-done.3
  20.9 0.0 copy-done.1
  20.9 1.0 shard_map.68
  21.8 24.2 %all_to_all.25.parts = bf16[4,8,2,96,128]{4,3,2,1,0:T(8,128)(2,1)S(1)} all-to-all(bf16[4,8,2,96,128]{4,3,2,1,0:T(8,128)(2,1)S(1)} %shard_map.68), channel_id=1, replica_groups={{0,256,384,640},{32,288,416,672},{64,320,448,704},{96,352,480,736},{896..., dimensions={0} | all-to-all | bytes 3145728 | tf_op jit(solution)/shard_map/all_to_all | solution.py:149
  46.1 0.2 shard_map.69
  46.3 17.1 %all_to_all.26.parts = bf16[8,2,96,128]{3,2,1,0:T(8,128)(2,1)S(1)} all-to-all(bf16[8,2,96,128]{3,2,1,0:T(8,128)(2,1)S(1)} %shard_map.69), channel_id=1, replica_groups={{0,32,64,96,896,928,960,992},{256,288,320,352,128,160,192,224},{384,416..., dimensions={0} | all-to-all | bytes 786432 | tf_op jit(solution)/shard_map/all_to_all | solution.py:149
  63.4 0.1 shard_map.70
  63.5 13.3 %all_to_all.27.part = bf16[8,2,96,128]{3,2,1,0:T(8,128)(2,1)S(1)} all-to-all(bf16[8,2,96,128]{3,2,1,0:T(8,128)(2,1)S(1)} %shard_map.70), channel_id=1, replica_groups={{0,32,64,96,896,928,960,992},{256,288,320,352,128,160,192,224},{384,416..., dimensions={0} | all-to-all | bytes 786432 | tf_op jit(solution)/shard_map/all_to_all | solution.py:149
  76.8 0.2 shard_map.71
  77.0 25.3 %all_to_all.28.mine = bf16[4,8,2,96,128]{4,3,2,1,0:T(8,128)(2,1)S(1)} all-to-all(bf16[4,8,2,96,128]{4,3,2,1,0:T(8,128)(2,1)S(1)} %shard_map.71), channel_id=1, replica_groups={{0,256,384,640},{32,288,416,672},{64,320,448,704},{96,352,480,736},{896..., dimensions={0} | all-to-all | bytes 3145728 | tf_op jit(solution)/shard_map/all_to_all | solution.py:149
  102.3 6.0 %collective-permute-start.2 = (bf16[4,8,2,96,128]{4,3,2,1,0:T(8,128)(2,1)S(1)}, bf16[4,8,2,96,128]{4,3,2,1,0:T(8,128)(2,1)S(1)}, u32[]{:S(2)}, u32[]{:S(2)}) collective-permute-start(bf16[4,8,2,96,128]{4,3,2,1,0:T(8,128)(2,1)S(1)} %all_to_all.28.mine), channel_id=1, source_target_pairs={{0,16},{16,0},{32,48},{48,32},{64,80},{80,64},{96,112},{112,96},{1... | collective-permute-start | bytes 4718600 | tf_op jit(solution)/shard_map/ppermute | solution.py:146
  108.3 0.6 shard_map.72
  108.9 1.9 %collective-permute-start.1 = (f32[384,128]{1,0:T(8,128)S(1)}, f32[384,128]{1,0:T(8,128)S(1)}, u32[]{:S(2)}, u32[]{:S(2)}) collective-permute-start(f32[384,128]{1,0:T(8,128)S(1)} %get-tuple-element.9), channel_id=1, source_target_pairs={{0,16},{16,0},{32,48},{48,32},{64,80},{80,64},{96,112},{112,96},{1... | collective-permute-start | bytes 589832 | tf_op jit(solution)/shard_map/ppermute | solution.py:146
  110.8 1.4 %collective-permute-done.1 = f32[384,128]{1,0:T(8,128)S(1)} collective-permute-done((f32[384,128]{1,0:T(8,128)S(1)}, f32[384,128]{1,0:T(8,128)S(1)}, u32[]{:S(2)}, u32[]{:S(2)}) %collective-permute-start.1) | collective-permute-done | bytes 196640 | tf_op jit(solution)/shard_map/ppermute | solution.py:146
  112.2 0.7 add.3
  112.9 8.9 %all-to-all-start.4 = ((f32[16,24,128]{2,1,0:T(8,128)}), f32[16,24,128]{2,1,0:T(8,128)S(1)}, u32[]{:S(2)}, u32[]{:S(2)}) async-start(f32[16,24,128]{2,1,0:T(8,128)} %bitcast.1), calls=%async_computation.4 | async-start | bytes 393216 | tf_op jit(solution)/shard_map/all_to_all | solution.py:167
  121.8 0.0 collective-permute-done.2.theirs
  121.8 2.3 %shard_map.73 = (f32[128,2048]{1,0:T(8,128)}, f32[2048,128]{1,0:T(8,128)}, f32[8,128]{1,0:T(8,128)S(1)}) custom-call(bf16[4,8,2,96,128]{4,3,2,1,0:T(8,128)(2,1)S(1)} %all_to_all.28.mine, bf16[4,8,2,96,128]{4,3,2,1,0:T(8,128)(2,1)S(1)} %collective-permute-done.2.theirs, bf16[384,128]{1,0:T(8,128)(2,1)S(1)} %copy-done.2, bf16[384,128]{1,0:T(8,128)(2,1)S(1)} %copy-done.3), custom_call_target="tpu_custom_call" | custom-call | tf_op jit(solution)/shard_map/pallas_call | solution.py:31
  124.1 7.6 %all-to-all-done.4.parts = f32[16,24,128]{2,1,0:T(8,128)S(1)} async-done(((f32[16,24,128]{2,1,0:T(8,128)}), f32[16,24,128]{2,1,0:T(8,128)S(1)}, u32[]{:S(2)}, u32[]{:S(2)}) %all-to-all-start.4) | async-done | bytes 196640 | tf_op jit(solution)/shard_map/all_to_all | solution.py:167
  131.7 0.6 shard_map.74
  (5 shorter events, 0.0 us)
Async XLA Ops:
  0.6 20.2 %copy-start = (bf16[128,2048]{1,0:T(8,128)(2,1)S(1)}, bf16[128,2048]{1,0:T(8,128)(2,1)}, u32[]{:S(2)}) copy-start(bf16[128,2048]{1,0:T(8,128)(2,1)} %w.1) | copy-start | bytes 1572868
  0.6 20.2 %copy-start.3 = (bf16[384,128]{1,0:T(8,128)(2,1)S(1)}, bf16[384,128]{1,0:T(8,128)(2,1)}, u32[]{:S(2)}) copy-start(bf16[384,128]{1,0:T(8,128)(2,1)} %y.5) | copy-start | bytes 294916
  0.7 20.2 %copy-start.2 = (bf16[384,128]{1,0:T(8,128)(2,1)S(1)}, bf16[384,128]{1,0:T(8,128)(2,1)}, u32[]{:S(2)}) copy-start(bf16[384,128]{1,0:T(8,128)(2,1)} %x.5) | copy-start | bytes 294916
  0.7 20.2 %copy-start.1 = (bf16[2048,128]{1,0:T(8,128)(2,1)S(1)}, bf16[2048,128]{1,0:T(8,128)(2,1)}, u32[]{:S(2)}) copy-start(bf16[2048,128]{1,0:T(8,128)(2,1)} %w_out.3) | copy-start | bytes 1572868
  2.8 18.1 %collective-permute-start = (bf16[2,1408,128]{2,1,0:T(8,128)(2,1)}, bf16[2,1408,128]{2,1,0:T(8,128)(2,1)S(1)}, u32[]{:S(2)}, u32[]{:S(2)}) collective-permute-start(bf16[2,1408,128]{2,1,0:T(8,128)(2,1)} %shard_map.67), channel_id=1, source_target_pairs={{0,16},{16,0},{32,48},{48,32},{64,80},{80,64},{96,112},{112,96},{1... | collective-permute-start | bytes 2162696 | tf_op jit(solution)/shard_map/ppermute | solution.py:146
  102.3 19.5 %collective-permute-start.2 = (bf16[4,8,2,96,128]{4,3,2,1,0:T(8,128)(2,1)S(1)}, bf16[4,8,2,96,128]{4,3,2,1,0:T(8,128)(2,1)S(1)}, u32[]{:S(2)}, u32[]{:S(2)}) collective-permute-start(bf16[4,8,2,96,128]{4,3,2,1,0:T(8,128)(2,1)S(1)} %all_to_all.28.mine), channel_id=1, source_target_pairs={{0,16},{16,0},{32,48},{48,32},{64,80},{80,64},{96,112},{112,96},{1... | collective-permute-start | bytes 4718600 | tf_op jit(solution)/shard_map/ppermute | solution.py:146
  108.9 3.3 %collective-permute-start.1 = (f32[384,128]{1,0:T(8,128)S(1)}, f32[384,128]{1,0:T(8,128)S(1)}, u32[]{:S(2)}, u32[]{:S(2)}) collective-permute-start(f32[384,128]{1,0:T(8,128)S(1)} %get-tuple-element.9), channel_id=1, source_target_pairs={{0,16},{16,0},{32,48},{48,32},{64,80},{80,64},{96,112},{112,96},{1... | collective-permute-start | bytes 589832 | tf_op jit(solution)/shard_map/ppermute | solution.py:146
  112.9 18.8 %all-to-all-start.4 = ((f32[16,24,128]{2,1,0:T(8,128)}), f32[16,24,128]{2,1,0:T(8,128)S(1)}, u32[]{:S(2)}, u32[]{:S(2)}) async-start(f32[16,24,128]{2,1,0:T(8,128)} %bitcast.1), calls=%async_computation.4 | async-start | bytes 393216 | tf_op jit(solution)/shard_map/all_to_all | solution.py:167

commit v10 on v8

--- a/solution.py
+++ b/solution.py
@@ -13,23 +13,24 @@
 Q = T // Z
 
 HALVES = ((0, 2, 3, 5), (7, 1, 4, 6))
+BACK = ((2, 4, 5, 7), (1, 3, 6, 0))
 at = lambda x, z, c: (x * Z + z) * C + c
 
 
-def groups(c):
-    fours = [[at(x, z, c) for x in half] for half in HALVES for z in range(Z)]
-    fours += [[at(x, z, 1 - c) for z in range(Z)] for x in range(X)]
-    eights = [[at(half[a], z, c) for half in HALVES for z in range(Z)] for a in range(4)]
-    eights += [[at(x, z, 1 - c) for x in range(X)] for z in range(Z)]
+def groups(halves):
+    fours = [[at(x, z, 0) for x in half] for half in halves for z in range(Z)]
+    fours += [[at(x, z, 1) for z in range(Z)] for x in range(X)]
+    eights = [[at(half[a], z, 0) for half in halves for z in range(Z)] for a in range(4)]
+    eights += [[at(x, z, 1) for x in range(X)] for z in range(Z)]
     return fours, eights
 
 
 SWAP = [(i, i ^ 1) for i in range(X * Z * C)]
 
 
-def place(first, x, z):
-    half = int(x in HALVES[1])
-    return jnp.where(first, HALVES[half].index(x), z), jnp.where(first, half * Z + z, x)
+def place(halves, core, x, z):
+    first, half = core == 0, int(x in halves[1])
+    return jnp.where(first, halves[half].index(x), z), jnp.where(first, half * Z + z, x)
 
 
 def call(body, outs, *operands, where=pltpu.VMEM, params=PARAMS, scratch=()):
@@ -80,7 +81,7 @@
         g = g + dot(theirs[1, :T], theirs[1, rows], ((1,), (1,)))
         h, g = h.astype(BF16), g.astype(BF16)
         for z in range(Z):
-            four, eight = place(core == 0, j, z)
+            four, eight = place(HALVES, core, j, z)
             out[four, eight, 0] = h[z * Q : (z + 1) * Q]
             out[four, eight, 1] = g[z * Q : (z + 1) * Q]
 
@@ -118,7 +119,7 @@
 
 
 def tokens(ref, core, x, which):
-    blocks = [ref[(*place(core == 1, x, z), which)] for z in range(Z)]
+    blocks = [ref[(*place(BACK, core, x, z), which)] for z in range(Z)]
     return jnp.concatenate(blocks, axis=0)
 
 
@@ -162,10 +163,10 @@
     )
     theirs = swap(theirs)
     sums = call(partial_sums, s(both, BF16), inputs, w_in, grad_out, w_out, theirs)
-    fours, eights = groups(0)
+    fours, eights = groups(HALVES)
     sums = call(add_fours, s(both[1:], BF16), exchange(sums, fours))
     mine = call(middle, s(both[1:], BF16), exchange(sums, eights))
-    fours, eights = groups(1)
+    fours, eights = groups(BACK)
     mine = exchange(call(copies, s(both, BF16), exchange(mine, eights)), fours)
     theirs = swap(mine)
     part = call(input_part, s((T, B), F32), mine, theirs, w_in)

time: 134 us -> 135 us (level); the launches traced: 134 us -> 133 us
  no operation moved by 1% of the time
where the time goes in v10:
time: 135 us; the launch traced here: 133 us
  blocking collectives  80.2 us (59%)
  starting transfers between devices  32.5 us (24%)
  waiting for transfers between devices  12.3 us (9%)
  Pallas kernels  7.08 us (5%)
    all_to_all x4, blocking collectives, exchange(): return lax.all_to_all(v, 'gx', 0, 0, axis_index_groups=groups, tiled=True)  80.2 us
    ppermute x2, starting transfers between devices, per_device(): swap = lambda v: lax.ppermute(v, 'gx', SWAP)  24.6 us
    all_to_all x1, starting transfers between devices, per_device(): part = lax.all_to_all(part.reshape(16, T // 16, B), 'gy', 0, 0, tiled=True)  7.84 us
    all_to_all x1, waiting for transfers between devices, per_device(): part = lax.all_to_all(part.reshape(16, T // 16, B), 'gy', 0, 0, tiled=True)  7.3 us
    pallas_call x8, Pallas kernels, call(): pl.pallas_call(body, out_shape=outs, in_specs=[read] * len(operands), out...  7.08 us
    ppermute x2, waiting for transfers between devices, per_device(): swap = lambda v: lax.ppermute(v, 'gx', SWAP)  5.02 us
  transfers between devices with their start and end apart: 3, of which 3 were waited for; matrix products, arithmetic and copies ran while one was open for 0% of the time, Pallas kernels for 2%

profile of v10, /device:TPU:1, one launch (start us, length us, event | category | flops | bytes accessed | tf_op | source)
XLA Modules:
  0.0 133.5 jit_solution(13888233904315565201)
XLA Ops:
  0.6 0.0 copy-start.2
  0.6 0.0 copy-start
  0.7 0.0 copy-start.3
  0.7 0.0 copy-start.1
  0.7 2.1 %shard_map.67 = bf16[2,1408,128]{2,1,0:T(8,128)(2,1)} custom-call(bf16[384,128]{1,0:T(8,128)(2,1)} %x.5, bf16[128,2048]{1,0:T(8,128)(2,1)} %w.1, bf16[384,128]{1,0:T(8,128)(2,1)} %y.5, bf16[2048,128]{1,0:T(8,128)(2,1)} %w_out.3), custom_call_target="tpu_custom_call" | custom-call | tf_op jit(solution)/shard_map/pallas_call | solution.py:38
  2.8 16.1 %collective-permute-start = (bf16[2,1408,128]{2,1,0:T(8,128)(2,1)}, bf16[2,1408,128]{2,1,0:T(8,128)(2,1)S(1)}, u32[]{:S(2)}, u32[]{:S(2)}) collective-permute-start(bf16[2,1408,128]{2,1,0:T(8,128)(2,1)} %shard_map.67), channel_id=1, source_target_pairs={{0,16},{16,0},{32,48},{48,32},{64,80},{80,64},{96,112},{112,96},{1... | collective-permute-start | bytes 2162696 | tf_op jit(solution)/shard_map/ppermute | solution.py:150
  18.9 2.0 %collective-permute-done.theirs = bf16[2,1408,128]{2,1,0:T(8,128)(2,1)S(1)} collective-permute-done((bf16[2,1408,128]{2,1,0:T(8,128)(2,1)}, bf16[2,1408,128]{2,1,0:T(8,128)(2,1)S(1)}, u32[]{:S(2)}, u32[]{:S(2)}) %collective-permute-start) | collective-permute-done | bytes 720928 | tf_op jit(solution)/shard_map/ppermute | solution.py:150
  20.9 0.0 copy-done.1
  20.9 1.0 shard_map.68
  21.9 24.2 %all_to_all.25.parts = bf16[4,8,2,96,128]{4,3,2,1,0:T(8,128)(2,1)S(1)} all-to-all(bf16[4,8,2,96,128]{4,3,2,1,0:T(8,128)(2,1)S(1)} %shard_map.68), channel_id=1, replica_groups={{0,256,384,640},{32,288,416,672},{64,320,448,704},{96,352,480,736},{896..., dimensions={0} | all-to-all | bytes 3145728 | tf_op jit(solution)/shard_map/all_to_all | solution.py:153
  46.1 0.2 shard_map.69
  46.3 17.1 %all_to_all.26.parts = bf16[8,2,96,128]{3,2,1,0:T(8,128)(2,1)S(1)} all-to-all(bf16[8,2,96,128]{3,2,1,0:T(8,128)(2,1)S(1)} %shard_map.69), channel_id=1, replica_groups={{0,32,64,96,896,928,960,992},{256,288,320,352,128,160,192,224},{384,416..., dimensions={0} | all-to-all | bytes 786432 | tf_op jit(solution)/shard_map/all_to_all | solution.py:153
  63.4 0.1 shard_map.70
  63.5 13.5 %all_to_all.27.part = bf16[8,2,96,128]{3,2,1,0:T(8,128)(2,1)S(1)} all-to-all(bf16[8,2,96,128]{3,2,1,0:T(8,128)(2,1)S(1)} %shard_map.70), channel_id=1, replica_groups={{256,288,320,352,128,160,192,224},{512,544,576,608,384,416,448,480},{64..., dimensions={0} | all-to-all | bytes 786432 | tf_op jit(solution)/shard_map/all_to_all | solution.py:153
  77.0 0.2 shard_map.71
  77.2 25.3 %all_to_all.28.mine = bf16[4,8,2,96,128]{4,3,2,1,0:T(8,128)(2,1)S(1)} all-to-all(bf16[4,8,2,96,128]{4,3,2,1,0:T(8,128)(2,1)S(1)} %shard_map.71), channel_id=1, replica_groups={{256,512,640,896},{288,544,672,928},{320,576,704,960},{352,608,736,992}..., dimensions={0} | all-to-all | bytes 3145728 | tf_op jit(solution)/shard_map/all_to_all | solution.py:153
  102.5 8.6 %collective-permute-start.1 = (bf16[4,8,2,96,128]{4,3,2,1,0:T(8,128)(2,1)S(1)}, bf16[4,8,2,96,128]{4,3,2,1,0:T(8,128)(2,1)S(1)}, u32[]{:S(2)}, u32[]{:S(2)}) collective-permute-start(bf16[4,8,2,96,128]{4,3,2,1,0:T(8,128)(2,1)S(1)} %all_to_all.28.mine), channel_id=1, source_target_pairs={{0,16},{16,0},{32,48},{48,32},{64,80},{80,64},{96,112},{112,96},{1... | collective-permute-start | bytes 4718600 | tf_op jit(solution)/shard_map/ppermute | solution.py:150
  111.1 3.0 %collective-permute-done.1.theirs = bf16[4,8,2,96,128]{4,3,2,1,0:T(8,128)(2,1)S(1)} collective-permute-done((bf16[4,8,2,96,128]{4,3,2,1,0:T(8,128)(2,1)S(1)}, bf16[4,8,2,96,128]{4,3,2,1,0:T(8,128)(2,1)S(1)}, u32[]{:S(2)}, u32[]{:S(2)}) %collective-permute-start.1) | collective-permute-done | bytes 1572896 | tf_op jit(solution)/shard_map/ppermute | solution.py:150
  114.1 0.6 shard_map.72
  114.7 0.7 copy-done.4
  115.4 7.8 %all-to-all-start.4 = ((f32[16,24,128]{2,1,0:T(8,128)}), f32[16,24,128]{2,1,0:T(8,128)S(1)}, u32[]{:S(2)}, u32[]{:S(2)}) async-start(f32[16,24,128]{2,1,0:T(8,128)} %bitcast.1), calls=%async_computation.4 | async-start | bytes 393216 | tf_op jit(solution)/shard_map/all_to_all | solution.py:173
  123.2 2.3 %shard_map.74 = (f32[128,2048]{1,0:T(8,128)}, f32[2048,128]{1,0:T(8,128)}) custom-call(bf16[4,8,2,96,128]{4,3,2,1,0:T(8,128)(2,1)S(1)} %all_to_all.28.mine, bf16[4,8,2,96,128]{4,3,2,1,0:T(8,128)(2,1)S(1)} %collective-permute-done.1.theirs, bf16[384,128]{1,0:T(8,128)(2,1)S(1)} %copy-done.2, bf16[384,128]{1,0:T(8,128)(2,1)S(1)} %copy-done.3), custom_call_target="tpu_custom_call" | custom-call | tf_op jit(solution)/shard_map/pallas_call | solution.py:38
  125.5 7.3 %all-to-all-done.4.parts = f32[16,24,128]{2,1,0:T(8,128)S(1)} async-done(((f32[16,24,128]{2,1,0:T(8,128)}), f32[16,24,128]{2,1,0:T(8,128)S(1)}, u32[]{:S(2)}, u32[]{:S(2)}) %all-to-all-start.4) | async-done | bytes 196640 | tf_op jit(solution)/shard_map/all_to_all | solution.py:173
  132.8 0.6 shard_map.73
  (4 shorter events, 0.0 us)
Async XLA Ops:
  0.6 20.2 %copy-start.2 = (bf16[384,128]{1,0:T(8,128)(2,1)S(1)}, bf16[384,128]{1,0:T(8,128)(2,1)}, u32[]{:S(2)}) copy-start(bf16[384,128]{1,0:T(8,128)(2,1)} %x.5) | copy-start | bytes 294916
  0.6 20.2 %copy-start = (bf16[128,2048]{1,0:T(8,128)(2,1)S(1)}, bf16[128,2048]{1,0:T(8,128)(2,1)}, u32[]{:S(2)}) copy-start(bf16[128,2048]{1,0:T(8,128)(2,1)} %w.1) | copy-start | bytes 1572868
  0.7 20.2 %copy-start.3 = (bf16[384,128]{1,0:T(8,128)(2,1)S(1)}, bf16[384,128]{1,0:T(8,128)(2,1)}, u32[]{:S(2)}) copy-start(bf16[384,128]{1,0:T(8,128)(2,1)} %y.5) | copy-start | bytes 294916
  0.7 20.2 %copy-start.1 = (bf16[2048,128]{1,0:T(8,128)(2,1)S(1)}, bf16[2048,128]{1,0:T(8,128)(2,1)}, u32[]{:S(2)}) copy-start(bf16[2048,128]{1,0:T(8,128)(2,1)} %w_out.3) | copy-start | bytes 1572868
  2.8 18.1 %collective-permute-start = (bf16[2,1408,128]{2,1,0:T(8,128)(2,1)}, bf16[2,1408,128]{2,1,0:T(8,128)(2,1)S(1)}, u32[]{:S(2)}, u32[]{:S(2)}) collective-permute-start(bf16[2,1408,128]{2,1,0:T(8,128)(2,1)} %shard_map.67), channel_id=1, source_target_pairs={{0,16},{16,0},{32,48},{48,32},{64,80},{80,64},{96,112},{112,96},{1... | collective-permute-start | bytes 2162696 | tf_op jit(solution)/shard_map/ppermute | solution.py:150
  102.5 11.6 %collective-permute-start.1 = (bf16[4,8,2,96,128]{4,3,2,1,0:T(8,128)(2,1)S(1)}, bf16[4,8,2,96,128]{4,3,2,1,0:T(8,128)(2,1)S(1)}, u32[]{:S(2)}, u32[]{:S(2)}) collective-permute-start(bf16[4,8,2,96,128]{4,3,2,1,0:T(8,128)(2,1)S(1)} %all_to_all.28.mine), channel_id=1, source_target_pairs={{0,16},{16,0},{32,48},{48,32},{64,80},{80,64},{96,112},{112,96},{1... | collective-permute-start | bytes 4718600 | tf_op jit(solution)/shard_map/ppermute | solution.py:150
  114.7 0.7 copy-start.4
  115.4 17.5 %all-to-all-start.4 = ((f32[16,24,128]{2,1,0:T(8,128)}), f32[16,24,128]{2,1,0:T(8,128)S(1)}, u32[]{:S(2)}, u32[]{:S(2)}) async-start(f32[16,24,128]{2,1,0:T(8,128)} %bitcast.1), calls=%async_computation.4 | async-start | bytes 393216 | tf_op jit(solution)/shard_map/all_to_all | solution.py:173

commit v11 on v10

--- a/solution.py
+++ b/solution.py
@@ -13,7 +13,7 @@
 Q = T // Z
 
 HALVES = ((0, 2, 3, 5), (7, 1, 4, 6))
-BACK = ((2, 4, 5, 7), (1, 3, 6, 0))
+BACK = ((0, 1, 2, 3), (7, 6, 5, 4))
 at = lambda x, z, c: (x * Z + z) * C + c
 
 

time: 135 us -> 138 us (1.022)
  the two profiles are of different devices: /device:TPU:1 before, /device:TPU:14 now
where the time goes in v11:
time: 138 us; the launch traced here: 137 us
  blocking collectives  98.1 us (71%)
  starting transfers between devices  16.1 us (12%)
  waiting for transfers between devices  14.5 us (11%)
  Pallas kernels  7.09 us (5%)
    all_to_all x4, blocking collectives, exchange(): return lax.all_to_all(v, 'gx', 0, 0, axis_index_groups=groups, tiled=True)  98.1 us
    all_to_all x1, starting transfers between devices, per_device(): part = lax.all_to_all(part.reshape(16, T // 16, B), 'gy', 0, 0, tiled=True)  12.2 us
    all_to_all x1, waiting for transfers between devices, per_device(): part = lax.all_to_all(part.reshape(16, T // 16, B), 'gy', 0, 0, tiled=True)  8.77 us
    pallas_call x8, Pallas kernels, call(): pl.pallas_call(body, out_shape=outs, in_specs=[read] * len(operands), out...  7.09 us
    ppermute x2, waiting for transfers between devices, per_device(): swap = lambda v: lax.ppermute(v, 'gx', SWAP)  5.74 us
    ppermute x2, starting transfers between devices, per_device(): swap = lambda v: lax.ppermute(v, 'gx', SWAP)  3.83 us
  transfers between devices with their start and end apart: 3, of which 3 were waited for; matrix products, arithmetic and copies ran while one was open for 0% of the time, Pallas kernels for 2%

profile of v11, /device:TPU:14, one launch (start us, length us, event | category | flops | bytes accessed | tf_op | source)
XLA Modules:
  0.0 137.2 jit_solution(6512444462090733760)
XLA Ops:
  0.6 0.0 copy-start.2
  0.6 0.0 copy-start
  0.7 2.1 %shard_map.67 = bf16[2,1408,128]{2,1,0:T(8,128)(2,1)} custom-call(bf16[384,128]{1,0:T(8,128)(2,1)} %x.5, bf16[128,2048]{1,0:T(8,128)(2,1)} %w.1, bf16[384,128]{1,0:T(8,128)(2,1)} %y.5, bf16[2048,128]{1,0:T(8,128)(2,1)} %w_out.3), custom_call_target="tpu_custom_call" | custom-call | tf_op jit(solution)/shard_map/pallas_call | solution.py:38
  2.8 1.9 %collective-permute-start = (bf16[2,1408,128]{2,1,0:T(8,128)(2,1)}, bf16[2,1408,128]{2,1,0:T(8,128)(2,1)S(1)}, u32[]{:S(2)}, u32[]{:S(2)}) collective-permute-start(bf16[2,1408,128]{2,1,0:T(8,128)(2,1)} %shard_map.67), channel_id=1, source_target_pairs={{0,16},{16,0},{32,48},{48,32},{64,80},{80,64},{96,112},{112,96},{1... | collective-permute-start | bytes 2162696 | tf_op jit(solution)/shard_map/ppermute | solution.py:150
  4.7 2.4 %collective-permute-done.theirs = bf16[2,1408,128]{2,1,0:T(8,128)(2,1)S(1)} collective-permute-done((bf16[2,1408,128]{2,1,0:T(8,128)(2,1)}, bf16[2,1408,128]{2,1,0:T(8,128)(2,1)S(1)}, u32[]{:S(2)}, u32[]{:S(2)}) %collective-permute-start) | collective-permute-done | bytes 720928 | tf_op jit(solution)/shard_map/ppermute | solution.py:150
  7.1 0.0 copy-done.2
  7.1 0.0 copy-done.3
  7.1 1.0 shard_map.68
  8.1 24.5 %all_to_all.25.parts = bf16[4,8,2,96,128]{4,3,2,1,0:T(8,128)(2,1)S(1)} all-to-all(bf16[4,8,2,96,128]{4,3,2,1,0:T(8,128)(2,1)S(1)} %shard_map.68), channel_id=1, replica_groups={{0,256,384,640},{32,288,416,672},{64,320,448,704},{96,352,480,736},{896..., dimensions={0} | all-to-all | bytes 3145728 | tf_op jit(solution)/shard_map/all_to_all | solution.py:153
  32.6 0.2 shard_map.69
  32.8 31.4 %all_to_all.26.parts = bf16[8,2,96,128]{3,2,1,0:T(8,128)(2,1)S(1)} all-to-all(bf16[8,2,96,128]{3,2,1,0:T(8,128)(2,1)S(1)} %shard_map.69), channel_id=1, replica_groups={{0,32,64,96,896,928,960,992},{256,288,320,352,128,160,192,224},{384,416..., dimensions={0} | all-to-all | bytes 786432 | tf_op jit(solution)/shard_map/all_to_all | solution.py:153
  64.1 0.1 shard_map.70
  64.2 15.7 %all_to_all.27.part = bf16[8,2,96,128]{3,2,1,0:T(8,128)(2,1)S(1)} all-to-all(bf16[8,2,96,128]{3,2,1,0:T(8,128)(2,1)S(1)} %shard_map.70), channel_id=1, replica_groups={{0,32,64,96,896,928,960,992},{128,160,192,224,768,800,832,864},{256,288..., dimensions={0} | all-to-all | bytes 786432 | tf_op jit(solution)/shard_map/all_to_all | solution.py:153
  79.9 0.2 shard_map.71
  80.1 26.6 %all_to_all.28.mine = bf16[4,8,2,96,128]{4,3,2,1,0:T(8,128)(2,1)S(1)} all-to-all(bf16[4,8,2,96,128]{4,3,2,1,0:T(8,128)(2,1)S(1)} %shard_map.71), channel_id=1, replica_groups={{0,128,256,384},{32,160,288,416},{64,192,320,448},{96,224,352,480},{896..., dimensions={0} | all-to-all | bytes 3145728 | tf_op jit(solution)/shard_map/all_to_all | solution.py:153
  106.7 1.9 %collective-permute-start.1 = (bf16[4,8,2,96,128]{4,3,2,1,0:T(8,128)(2,1)S(1)}, bf16[4,8,2,96,128]{4,3,2,1,0:T(8,128)(2,1)S(1)}, u32[]{:S(2)}, u32[]{:S(2)}) collective-permute-start(bf16[4,8,2,96,128]{4,3,2,1,0:T(8,128)(2,1)S(1)} %all_to_all.28.mine), channel_id=1, source_target_pairs={{0,16},{16,0},{32,48},{48,32},{64,80},{80,64},{96,112},{112,96},{1... | collective-permute-start | bytes 4718600 | tf_op jit(solution)/shard_map/ppermute | solution.py:150
  108.6 3.4 %collective-permute-done.1.theirs = bf16[4,8,2,96,128]{4,3,2,1,0:T(8,128)(2,1)S(1)} collective-permute-done((bf16[4,8,2,96,128]{4,3,2,1,0:T(8,128)(2,1)S(1)}, bf16[4,8,2,96,128]{4,3,2,1,0:T(8,128)(2,1)S(1)}, u32[]{:S(2)}, u32[]{:S(2)}) %collective-permute-start.1) | collective-permute-done | bytes 1572896 | tf_op jit(solution)/shard_map/ppermute | solution.py:150
  112.0 0.6 shard_map.72
  112.6 0.0 copy-start.4
  112.6 0.7 copy-done.4
  113.2 12.2 %all-to-all-start.4 = ((f32[16,24,128]{2,1,0:T(8,128)}), f32[16,24,128]{2,1,0:T(8,128)S(1)}, u32[]{:S(2)}, u32[]{:S(2)}) async-start(f32[16,24,128]{2,1,0:T(8,128)} %bitcast.1), calls=%async_computation.4 | async-start | bytes 393216 | tf_op jit(solution)/shard_map/all_to_all | solution.py:173
  125.5 2.3 %shard_map.74 = (f32[128,2048]{1,0:T(8,128)}, f32[2048,128]{1,0:T(8,128)}) custom-call(bf16[4,8,2,96,128]{4,3,2,1,0:T(8,128)(2,1)S(1)} %all_to_all.28.mine, bf16[4,8,2,96,128]{4,3,2,1,0:T(8,128)(2,1)S(1)} %collective-permute-done.1.theirs, bf16[384,128]{1,0:T(8,128)(2,1)S(1)} %copy-done.2, bf16[384,128]{1,0:T(8,128)(2,1)S(1)} %copy-done.3), custom_call_target="tpu_custom_call" | custom-call | tf_op jit(solution)/shard_map/pallas_call | solution.py:38
  127.8 8.8 %all-to-all-done.4.parts = f32[16,24,128]{2,1,0:T(8,128)S(1)} async-done(((f32[16,24,128]{2,1,0:T(8,128)}), f32[16,24,128]{2,1,0:T(8,128)S(1)}, u32[]{:S(2)}, u32[]{:S(2)}) %all-to-all-start.4) | async-done | bytes 196640 | tf_op jit(solution)/shard_map/all_to_all | solution.py:173
  136.6 0.6 shard_map.73
  (4 shorter events, 0.0 us)
Async XLA Ops:
  0.6 6.5 %copy-start.2 = (bf16[384,128]{1,0:T(8,128)(2,1)S(1)}, bf16[384,128]{1,0:T(8,128)(2,1)}, u32[]{:S(2)}) copy-start(bf16[384,128]{1,0:T(8,128)(2,1)} %x.5) | copy-start | bytes 294916
  0.6 6.4 %copy-start = (bf16[128,2048]{1,0:T(8,128)(2,1)S(1)}, bf16[128,2048]{1,0:T(8,128)(2,1)}, u32[]{:S(2)}) copy-start(bf16[128,2048]{1,0:T(8,128)(2,1)} %w.1) | copy-start | bytes 1572868
  0.7 6.4 %copy-start.3 = (bf16[384,128]{1,0:T(8,128)(2,1)S(1)}, bf16[384,128]{1,0:T(8,128)(2,1)}, u32[]{:S(2)}) copy-start(bf16[384,128]{1,0:T(8,128)(2,1)} %y.5) | copy-start | bytes 294916
  0.7 6.4 %copy-start.1 = (bf16[2048,128]{1,0:T(8,128)(2,1)S(1)}, bf16[2048,128]{1,0:T(8,128)(2,1)}, u32[]{:S(2)}) copy-start(bf16[2048,128]{1,0:T(8,128)(2,1)} %w_out.3) | copy-start | bytes 1572868
  2.8 4.3 %collective-permute-start = (bf16[2,1408,128]{2,1,0:T(8,128)(2,1)}, bf16[2,1408,128]{2,1,0:T(8,128)(2,1)S(1)}, u32[]{:S(2)}, u32[]{:S(2)}) collective-permute-start(bf16[2,1408,128]{2,1,0:T(8,128)(2,1)} %shard_map.67), channel_id=1, source_target_pairs={{0,16},{16,0},{32,48},{48,32},{64,80},{80,64},{96,112},{112,96},{1... | collective-permute-start | bytes 2162696 | tf_op jit(solution)/shard_map/ppermute | solution.py:150
  106.7 5.3 %collective-permute-start.1 = (bf16[4,8,2,96,128]{4,3,2,1,0:T(8,128)(2,1)S(1)}, bf16[4,8,2,96,128]{4,3,2,1,0:T(8,128)(2,1)S(1)}, u32[]{:S(2)}, u32[]{:S(2)}) collective-permute-start(bf16[4,8,2,96,128]{4,3,2,1,0:T(8,128)(2,1)S(1)} %all_to_all.28.mine), channel_id=1, source_target_pairs={{0,16},{16,0},{32,48},{48,32},{64,80},{80,64},{96,112},{112,96},{1... | collective-permute-start | bytes 4718600 | tf_op jit(solution)/shard_map/ppermute | solution.py:150
  112.6 0.7 copy-start.4
  113.2 23.4 %all-to-all-start.4 = ((f32[16,24,128]{2,1,0:T(8,128)}), f32[16,24,128]{2,1,0:T(8,128)S(1)}, u32[]{:S(2)}, u32[]{:S(2)}) async-start(f32[16,24,128]{2,1,0:T(8,128)} %bitcast.1), calls=%async_computation.4 | async-start | bytes 393216 | tf_op jit(solution)/shard_map/all_to_all | solution.py:173
